TPU v7x, 32 devices: a whole 2x2x4 slice. The times are simulated.
32 devices in a mesh: ctx: 4 (over z), tp: 8 (over y, x, core).
Axes of the slice: x: 2, y: 2, z: 4, core: 2. Of those that a mesh axis runs over, the one named last changes fastest.
Arguments:
- inputs: bfloat16 [1024, 8192], P(('ctx', 'tp')), may hold values from -6 to 6
- query_weight: bfloat16 [8192, 8192], P(None, 'tp'), may hold values from -0.0625 to 0.0625
- key_weight: bfloat16 [8192, 8192], P(None, 'tp'), may hold values from -0.0625 to 0.0625
- value_weight: bfloat16 [8192, 8192], P(None, 'tp'), may hold values from -0.0625 to 0.0625
- filter_taps: float32 [128, 8192], P(None, 'tp'), may hold values from -0.45 to 0.45
- out_grad: bfloat16 [1024, 8192], P('ctx', 'tp'), may hold values from -1.5 to 1.5
Outputs:
- mixed: bfloat16 [1024, 8192], P('ctx', 'tp')
- inputs_grad: bfloat16 [1024, 8192], P(('ctx', 'tp'))
- filter_grad: float32 [128, 8192], P(None, 'tp')
All inputs are finite; a program needn't handle non-finite values.
Results may differ from a plain program's by a relative error of at most 0.025.
Values may be sent and summed in bfloat16 or wider, within the bound.
No kernel may reach another device: no remote copies, remote signals or barrier semaphores. Data moves between devices by JAX's collectives and lax.ppermute only.
A program may use at most 128 MiB of HBM per device.

v0:
```python
import jax
import jax.numpy as jnp
from jax import lax
from jax.sharding import PartitionSpec as P


def from_behind(block, axis, distance):
    devices = range(lax.axis_size(axis))
    route = [(i - distance, i) for i in devices if i - distance in devices]
    return lax.ppermute(block, axis, route)


def forward_filter(padded, filter_taps, length):
    taps = filter_taps.shape[0]
    total = jnp.zeros((length, padded.shape[1]), jnp.float32)
    for offset in range(taps):
        start = taps - 1 - offset
        total = total + filter_taps[offset] * padded[start : start + length]
    return total


def backward_filter(padded, filter_taps, length):
    taps = filter_taps.shape[0]
    total = jnp.zeros((length, padded.shape[1]), jnp.float32)
    for offset in range(taps):
        total = total + filter_taps[offset] * padded[offset : offset + length]
    return total


def tap_products(grad_rows, padded, taps, length):
    rows_out = []
    for offset in range(taps):
        start = taps - 1 - offset
        rows_out.append(jnp.sum(grad_rows * padded[start : start + length], axis=0))
    return jnp.stack(rows_out)


def contract(left, right):
    return lax.dot_general(
        left, right, (((1,), (1,)), ((), ())), preferred_element_type=jnp.float32
    )


def on_device(inputs, query_weight, key_weight, value_weight, filter_taps, out_grad):
    group = query_weight.shape[1]
    taps = filter_taps.shape[0]
    margin = taps - 1
    own_rows = inputs.shape[0]
    piece = lax.all_gather(inputs, "tp", axis=0, tiled=True)
    query_part = jnp.dot(piece, query_weight, preferred_element_type=jnp.float32)
    keys_part = jnp.dot(piece, key_weight, preferred_element_type=jnp.float32)
    values_part = jnp.dot(piece, value_weight, preferred_element_type=jnp.float32)
    projected = jnp.concatenate([query_part, keys_part, values_part], axis=1).astype(jnp.bfloat16)
    length = projected.shape[0]
    query = projected[:, :group]
    keys = projected[:, group : 2 * group]
    values = projected[:, 2 * group :]
    product = (keys.astype(jnp.float32) * values.astype(jnp.float32)).astype(jnp.bfloat16)
    grad_f32 = out_grad.astype(jnp.float32)
    conv_in_grad = (grad_f32 * query.astype(jnp.float32)).astype(jnp.bfloat16)
    tail_part = from_behind(product[length - margin :], "ctx", 1)
    head_part = from_behind(conv_in_grad[:margin], "ctx", -1)
    padded_prod = jnp.concatenate([tail_part, product], axis=0).astype(jnp.float32)
    conv = forward_filter(padded_prod, filter_taps, length)
    mixed = (query.astype(jnp.float32) * conv).astype(jnp.bfloat16)
    query_grad = (grad_f32 * conv).astype(jnp.bfloat16)
    padded_grad = jnp.concatenate([conv_in_grad, head_part], axis=0).astype(jnp.float32)
    product_grad = backward_filter(padded_grad, filter_taps, length)
    keys_grad = (product_grad * values.astype(jnp.float32)).astype(jnp.bfloat16)
    values_grad = (product_grad * keys.astype(jnp.float32)).astype(jnp.bfloat16)
    local_taps = tap_products(conv_in_grad.astype(jnp.float32), padded_prod, taps, length)
    filter_grad = lax.psum(local_taps.astype(jnp.bfloat16), "ctx").astype(jnp.float32)
    query_rows = lax.slice_in_dim(query_grad, 0, lax.axis_size("tp") * own_rows, axis=0)
    keys_rows = lax.slice_in_dim(keys_grad, 0, lax.axis_size("tp") * own_rows, axis=0)
    values_rows = lax.slice_in_dim(values_grad, 0, lax.axis_size("tp") * own_rows, axis=0)
    total = contract(query_rows, query_weight)
    total = total + contract(keys_rows, key_weight)
    summed = lax.psum_scatter(
        (total + contract(values_rows, value_weight)).astype(jnp.bfloat16),
        "tp",
        scatter_dimension=0,
        tiled=True,
    )
    return (mixed, summed, filter_grad)


def solution(mesh):
    in_specs = (
        P(("ctx", "tp"), None),
        P(None, "tp"),
        P(None, "tp"),
        P(None, "tp"),
        P(None, "tp"),
        P("ctx", "tp"),
    )
    out_specs = (P("ctx", "tp"), P(("ctx", "tp"), None), P(None, "tp"))
    return jax.shard_map(
        on_device, mesh=mesh, in_specs=in_specs, out_specs=out_specs, check_vma=False
    )
```

profile of v0, /device:TPU:0, one launch (start us, length us, event | category | flops | bytes accessed | tf_op | source)
XLA Modules:
  0.0 274.8 jit_solution(8730651095999067808)
XLA Ops:
  7.9 1.4 fusion.271
  9.3 1.4 fusion.270
  13.3 1.4 fusion.267
  14.7 34.6 %all-gather.2.cloned.1.call-done = bf16[256,8192]{1,0:T(8,128)(2,1)} async-done(((bf16[32,8192]{1,0:T(8,128)(2,1)}), bf16[256,8192]{1,0:T(8,128)(2,1)}) %all-gather.2.cloned.1.call-update) | async-done | bytes 4194320 | tf_op jit(solution)/shard_map/all_gather | solution.py:49
  49.3 11.7 %convolution_convert_fusion.1 = bf16[256,1024]{1,0:T(8,128)(2,1)S(1)} fusion(bf16[256,8192]{1,0:T(8,128)(2,1)} %all-gather.2.cloned.1.call-done, bf16[8192,1024]{1,0:T(8,128)(2,1)} %param.8), kind=kOutput, calls=%fused_computation.138 | convolution fusion | flops 4295229440 | bytes 21495808 | tf_op jit(solution)/shard_map/dot_general | solution.py:51
  61.0 9.3 %fusion.3 = (bf16[256,1024]{1,0:T(8,128)(2,1)S(1)}, bf16[256,1024]{1,0:T(8,128)(2,1)}) fusion(bf16[256,1024]{1,0:T(8,128)(2,1)S(1)} %convolution_convert_fusion.1, bf16[256,8192]{1,0:T(8,128)(2,1)S(1)} %copy-done.4, bf16[8192,1024]{1,0:T(8,128)(2,1)} %param.9), kind=kOutput, calls=%fused_computation.142 | convolution fusion | flops 4296278016 | bytes 22544384 | tf_op jit(solution)/shard_map/dot_general | solution.py:52
  70.5 3.6 %collective-permute-start = (bf16[127,1024]{1,0:T(8,128)(2,1)S(1)}, bf16[127,1024]{1,0:T(8,128)(2,1)S(1)}, u32[]{:S(2)}, u32[]{:S(2)}) collective-permute-start(bf16[127,1024]{1,0:T(8,128)(2,1)S(1)} %slice.1812), channel_id=1, source_target_pairs={{0,8},{8,16},{16,24},{1,9},{9,17},{17,25},{2,10},{10,18},{18,26},{... | collective-permute-start | bytes 780296 | tf_op jit(solution)/shard_map/ppermute | solution.py:10
  75.2 1.3 fusion.272
  76.6 3.2 %collective-permute-done = bf16[127,1024]{1,0:T(8,128)(2,1)S(1)} collective-permute-done((bf16[127,1024]{1,0:T(8,128)(2,1)S(1)}, bf16[127,1024]{1,0:T(8,128)(2,1)S(1)}, u32[]{:S(2)}, u32[]{:S(2)}) %collective-permute-start) | collective-permute-done | bytes 260128 | tf_op jit(solution)/shard_map/ppermute | solution.py:10
  80.0 34.0 %fusion.1 = (bf16[256,1024]{1,0:T(8,128)(2,1)}, f32[256,1024]{1,0:T(8,128)S(1)}, bf16[256,1024]{1,0:T(8,128)(2,1)S(1)}) fusion(f32[383,1024]{1,0:T(8,128)S(1)} %maximum_convert_fusion, f32[1024]{0:T(1024)S(1)} %bitcast.351, f32[1024]{0:T(1024)S(1)} %bitcast.353, f32[1024]{0:T(1024)S(1)} %bitcast.291, f32[1024]{0:T(1024)S(1)} %bitcast.293, ...), kind=kOutput, calls=%fused_computation.140 | convolution fusion | flops 4362862592 | bytes 157810688 | tf_op jit(solution)/shard_map/dot_general | solution.py:50
  114.0 2.5 fusion.128
  116.8 2.5 fusion.129
  119.4 2.5 fusion.130
  121.9 2.5 fusion.131
  124.5 2.5 fusion.132
  127.0 2.8 %fusion.133 = (bf16[1024]{0:T(1024)(128)(2,1)S(1)}, bf16[1024]{0:T(1024)(128)(2,1)S(1)}, bf16[1024]{0:T(1024)(128)(2,1)S(1)}, bf16[1024]{0:T(1024)(128)(2,1)S(1)...) fusion(bf16[256,1024]{1,0:T(8,128)(2,1)S(1)} %get-tuple-element, ...), kind=kLoop, calls=%fused_computation.272 | loop fusion | flops 9680896 | bytes 19435520 | tf_op jit(solution)/shard_map/reduce_sum | solution.py:34
  129.7 2.5 fusion.134
  133.9 10.6 %stack.644 = bf16[128,1024]{1,0:T(8,128)(2,1)} concatenate(bf16[1,1024]{1,0:T(2,128)(2,1)S(1)} %stack.516, bf16[1,1024]{1,0:T(2,128)(2,1)S(1)} %stack.517, bf16[1,1024]{1,0:T(2,128)(2,1)S(1)} %stack.518, bf16[1,1024]{1,0:T(2,128)(2,1)S(1)} %stack.519, bf16[1,1024]{1,0:T(2,128)(2,1)S(1)} %stack.520, bf16[1,1024]{1,0:T(2,128)(2,1)S(1)} %stack.521, bf16[1,1024]{1,0:T(2,128)(2,1)S(1)} %stack.522, ...), dimensions={0} | concatenate | bytes 524288 | tf_op jit(solution)/shard_map/stack | solution.py:35
  145.8 19.1 %fusion.262 = f32[256,8192]{1,0:T(8,128)} fusion(bf16[8192,1024]{1,0:T(8,128)(2,1)} %param.7, f32[256,1024]{1,0:T(8,128)S(1)} %get-tuple-element.133, bf16[256,1024]{1,0:T(8,128)(2,1)S(1)} %copy-done), kind=kOutput, calls=%fused_computation.533 | convolution fusion | flops 4295753728 | bytes 26738688 | tf_op jit(solution)/shard_map/dot_general | solution.py:39
  165.2 24.0 %fusion.135 = f32[256,1024]{1,0:T(8,128)S(1)} fusion(f32[383,1024]{1,0:T(8,128)S(1)} %maximum_convert_fusion.1, f32[1024]{0:T(1024)S(1)} %bitcast.352, f32[1024]{0:T(1024)S(1)} %bitcast.354, f32[1024]{0:T(1024)S(1)} %bitcast.292, f32[1024]{0:T(1024)S(1)} %bitcast.294, f32[1024]{0:T(1024)S(1)} %bitcast.296, f32[1024]{0:T(1024)S(1)} %bitcast.298, ...), kind=kLoop, calls=%fused_computation.275 | loop fusion | flops 66846720 | bytes 135790592 | tf_op jit(solution)/shard_map/add | solution.py:26
  189.2 13.0 %convolution_add_fusion.1 = f32[256,8192]{1,0:T(8,128)} fusion(f32[256,8192]{1,0:T(8,128)} %fusion.262, bf16[8192,1024]{1,0:T(8,128)(2,1)} %param.8, f32[256,1024]{1,0:T(8,128)S(1)} %fusion.135, bf16[256,1024]{1,0:T(8,128)(2,1)S(1)} %copy-done.3), kind=kOutput, calls=%fused_computation.129 | convolution fusion | flops 4297850880 | bytes 35127296 | tf_op jit(solution)/shard_map/dot_general | solution.py:39
  202.2 12.4 %fusion = bf16[256,8192]{1,0:T(8,128)(2,1)} fusion(f32[256,8192]{1,0:T(8,128)} %convolution_add_fusion.1, bf16[8192,1024]{1,0:T(8,128)(2,1)} %param.9, f32[256,1024]{1,0:T(8,128)S(1)} %fusion.135, bf16[256,1024]{1,0:T(8,128)(2,1)S(1)} %copy-done.2), kind=kOutput, calls=%fused_computation.130 | convolution fusion | flops 4299948032 | bytes 30932992 | tf_op jit(solution)/shard_map/dot_general | solution.py:39
  214.7 1.8 convert_element_type.64
  216.4 51.8 %reduce-scatter.2.cloned.1.call-done = bf16[32,8192]{1,0:T(8,128)(2,1)} async-done(((bf16[256,8192]{1,0:T(8,128)(2,1)}), bf16[32,8192]{1,0:T(8,128)(2,1)}) %reduce-scatter.2.cloned.1.call-update) | async-done | bytes 524304 | tf_op jit(solution)/shard_map/reduce_scatter | solution.py:78
  (155 shorter events, 7.4 us)
Async XLA Ops:
  7.2 42.2 %all-gather.2.cloned.1.call-start = ((), (), s32[]{:S(2)}) async-start(), calls=%async_computation.1 | async-start | bytes 4718592 | tf_op jit(solution)/shard_map/all_gather | solution.py:49
  7.9 206.7 %all-reduce.2.cloned.1.call-start = ((), (), s32[]{:S(2)}) async-start(), calls=%async_computation.3 | async-start | bytes 524288 | tf_op jit(solution)/shard_map/psum | solution.py:72
  49.3 11.7 %copy-start.4 = (bf16[256,8192]{1,0:T(8,128)(2,1)S(1)}, bf16[256,8192]{1,0:T(8,128)(2,1)}, u32[]{:S(2)}) copy-start(bf16[256,8192]{1,0:T(8,128)(2,1)} %all-gather.2.cloned.1.call-done) | copy-start | bytes 12582916
  61.0 9.4 %copy-start.1 = (bf16[256,1024]{1,0:T(8,128)(2,1)}, bf16[256,1024]{1,0:T(8,128)(2,1)S(1)}, u32[]{:S(2)}) copy-start(bf16[256,1024]{1,0:T(8,128)(2,1)S(1)} %convolution_convert_fusion.1) | copy-start | bytes 1572868
  70.5 9.4 %collective-permute-start = (bf16[127,1024]{1,0:T(8,128)(2,1)S(1)}, bf16[127,1024]{1,0:T(8,128)(2,1)S(1)}, u32[]{:S(2)}, u32[]{:S(2)}) collective-permute-start(bf16[127,1024]{1,0:T(8,128)(2,1)S(1)} %slice.1812), channel_id=1, source_target_pairs={{0,8},{8,16},{16,24},{1,9},{9,17},{17,25},{2,10},{10,18},{18,26},{... | collective-permute-start | bytes 780296 | tf_op jit(solution)/shard_map/ppermute | solution.py:10
  80.0 34.0 %copy-start = (bf16[256,1024]{1,0:T(8,128)(2,1)S(1)}, bf16[256,1024]{1,0:T(8,128)(2,1)}, u32[]{:S(2)}) copy-start(bf16[256,1024]{1,0:T(8,128)(2,1)} %param.11) | copy-start | bytes 1572868
  144.5 123.8 %reduce-scatter.2.cloned.1.call-start = ((), (), s32[]{:S(2)}) async-start(), calls=%async_computation.2 | async-start | bytes 4718592 | tf_op jit(solution)/shard_map/reduce_scatter | solution.py:78
  144.5 20.4 %collective-permute-start.1 = (bf16[127,1024]{1,0:T(8,128)(2,1)S(1)}, bf16[127,1024]{1,0:T(8,128)(2,1)S(1)}, u32[]{:S(2)}, u32[]{:S(2)}) collective-permute-start(bf16[127,1024]{1,0:T(8,128)(2,1)S(1)} %slice.1941), channel_id=1, source_target_pairs={{8,0},{16,8},{24,16},{9,1},{17,9},{25,17},{10,2},{18,10},{26,18},{... | collective-permute-start | bytes 780296 | tf_op jit(solution)/shard_map/ppermute | solution.py:10
  165.1 24.0 %copy-start.3 = (bf16[256,1024]{1,0:T(8,128)(2,1)S(1)}, bf16[256,1024]{1,0:T(8,128)(2,1)}, u32[]{:S(2)}) copy-start(bf16[256,1024]{1,0:T(8,128)(2,1)} %get-tuple-element.263) | copy-start | bytes 1572868
  189.2 13.0 %copy-start.2 = (bf16[256,1024]{1,0:T(8,128)(2,1)S(1)}, bf16[256,1024]{1,0:T(8,128)(2,1)}, u32[]{:S(2)}) copy-start(bf16[256,1024]{1,0:T(8,128)(2,1)} %copy-done.1) | copy-start | bytes 1572868
Sparse Core Ops, SparseCore 0:
  9.9 39.4 all-gather.1
  144.6 36.9 all-reduce.1
  214.7 53.5 reduce-scatter.1
where the time goes:
time: 276 us; the launch traced here: 275 us
  matrix products  99.5 us (36%)
  waiting for transfers between devices  90.5 us (33%)
  other arithmetic  44.3 us (16%)
  local copies, waits for them, and re-layouts  20.6 us (7%)
  between operations  14.9 us (5%)
  starting transfers between devices  4.99 us (2%)
    reduce_scatter x1, waiting for transfers between devices, on_device(): lax.psum_scatter((total + contract(values_rows, value_weight)).astype(jnp...  51.8 us
    dot_general x3, matrix products, contract(): lax.dot_general(left, right, (((1,), (1,)), ((), ())), preferred_element_...  44.5 us
    all_gather x1, waiting for transfers between devices, on_device(): piece = lax.all_gather(inputs, 'tp', axis=0, tiled=True)  34.6 us
    dot_general x1, matrix products, on_device(): jnp.dot(piece, query_weight, preferred_element_type=jnp.float32)  34 us
    add x1, other arithmetic, backward_filter(): total = total + filter_taps[offset] * padded[offset:offset + length]  24 us
    reduce_sum x8, other arithmetic, tap_products(): rows_out.append(jnp.sum(grad_rows * padded[start:start + length], axis=0))  18.2 us
    dot_general x1, matrix products, on_device(): keys_part = jnp.dot(piece, key_weight, preferred_element_type=jnp.float32)  11.7 us
    another operation x129, local copies, waits for them, and re-layouts, tap_products(): return jnp.stack(rows_out)  11.2 us
  transfers between devices with their start and end apart: 5, of which 3 were waited for; matrix products, arithmetic and copies ran while one was open for 29% of the time, Pallas kernels for 0%

commit v1 on v0

v1 whole, which is shorter than its diff:
```python
import jax
import jax.numpy as jnp
import numpy as np
from jax import lax
from jax.experimental import pallas as pl
from jax.experimental.pallas import tpu as pltpu
from jax.sharding import PartitionSpec as P

F32 = jnp.float32
BF16 = jnp.bfloat16
VMEM_BYTES = 56 * 2**20
FWD_CHUNKS = 2
BWD_CHUNKS = 2
EXACT = True


def from_behind(block, axis, distance):
    devices = range(lax.axis_size(axis))
    route = [(i - distance, i) for i in devices if i - distance in devices]
    return lax.ppermute(block, axis, route)


def swap(block, way):
    offsets = {0: (1, 1), 1: (2, 4), 2: (4, 2)}[way]
    return lax.ppermute(block, "tp", [(i, i ^ offsets[i % 2]) for i in range(8)])


def row_order(tp, paired):
    if not paired:
        return jnp.arange(tp, dtype=jnp.int32)
    me = lax.axis_index("tp").astype(jnp.int32)
    odd = me % 2
    first = 2 + 2 * odd
    second = 6 - first
    own = [me, me ^ first, me ^ second, me ^ 6]
    other = me ^ 1
    return jnp.stack(own + [other, other ^ second, other ^ first, other ^ 6])


def gather_rows(block, paired):
    if not paired:
        return [lax.all_gather(block, "tp", axis=0, tiled=True)]
    near = jnp.concatenate([block, swap(block, 1)], axis=0)
    far = swap(near, 2)
    return [near, far, swap(near, 0), swap(far, 0)]


def scatter_rows(parts, own_rows, paired):
    if not paired:
        return lax.psum_scatter(parts[0], "tp", scatter_dimension=0, tiled=True)
    keep, give = parts
    total = (keep.astype(F32) + swap(give, 0).astype(F32)).astype(BF16)
    mine, first = total[:own_rows], total[own_rows : 2 * own_rows]
    far = swap(total[2 * own_rows :], 2)
    first = (first.astype(F32) + far[own_rows:].astype(F32)).astype(BF16)
    return (mine.astype(F32) + far[:own_rows].astype(F32) + swap(first, 1).astype(F32)).astype(BF16)


def step_rows(depth):
    step = 1024
    while depth % step:
        step //= 2
    return step


def forward_chunk(pieces, weights, start, depth, acc, last, order, out_grad, taps):
    rows = sum(p.shape[0] for p in pieces)
    group = weights[0].shape[1]
    step = step_rows(depth)
    steps = depth // step
    blocks = order.shape[0]
    own = rows // blocks
    n_x = len(pieces)
    has_acc = acc is not None

    def kernel(*refs):
        order_ref, refs = refs[0], refs[1:]
        x_refs, w_refs, refs = refs[:n_x], refs[n_x : n_x + 3], refs[n_x + 3 :]
        if has_acc:
            acc_in, refs = refs[0], refs[1:]
        if last:
            grad_ref, refs = refs[0], refs[1:]
            q_ref, k_ref, v_ref, prod_ref, cig_ref, tail_ref, head_ref = refs[:7]
            total, x_buf, w_buf, x_sem, w_sem = refs[7:]
        else:
            total, x_buf, w_buf, x_sem, w_sem = refs

        def weight_copy(k, m):
            return pltpu.make_async_copy(
                w_refs[m].at[pl.ds(start + k * step, step), :], w_buf.at[k, m], w_sem.at[k, m]
            )

        at, x_copies = 0, []
        for i, piece in enumerate(x_refs):
            x_copies.append(
                pltpu.make_async_copy(piece, x_buf.at[pl.ds(at, piece.shape[0]), :], x_sem.at[i])
            )
            at += piece.shape[0]
        for copy in x_copies:
            copy.start()
        for k in range(steps):
            for m in range(3):
                weight_copy(k, m).start()
        if has_acc:
            total[...] = acc_in[...]
        else:
            total[...] = jnp.zeros_like(total)
        for copy in x_copies:
            copy.wait()

        def body(k, carry):
            x = x_buf[:, pl.ds(pl.multiple_of(k * step, step), step)]
            for m in range(3):
                weight_copy(k, m).wait()
                total[:, m * group : (m + 1) * group] += jnp.dot(x, w_buf[k, m], preferred_element_type=F32)
            return carry

        lax.fori_loop(0, steps, body, 0)
        if last:
            for b in range(blocks):
                here = pl.ds(pl.multiple_of(order_ref[b] * own, own), own)
                part = [total[b * own : (b + 1) * own, m * group : (m + 1) * group].astype(BF16) for m in range(3)]
                q_ref[here, :], k_ref[here, :], v_ref[here, :] = part
                query, keys, values = [p.astype(F32) for p in part]
                prod_ref[here, :] = (keys * values).astype(BF16)
                cig_ref[here, :] = (grad_ref[here, :].astype(F32) * query).astype(BF16)
            tail_ref[...] = prod_ref[rows - taps :, :]
            head_ref[...] = cig_ref[:taps, :]

    vmem, anywhere = pl.BlockSpec(memory_space=pltpu.VMEM), pl.BlockSpec(memory_space=pl.ANY)
    in_specs = [pl.BlockSpec(memory_space=pltpu.SMEM)] + [anywhere] * (n_x + 3)
    args = [order, *pieces, *weights]
    if has_acc:
        in_specs.append(vmem)
        args.append(acc)
    scratch = [
        pltpu.VMEM((rows, depth), BF16),
        pltpu.VMEM((steps, 3, step, group), BF16),
        pltpu.SemaphoreType.DMA((n_x,)),
        pltpu.SemaphoreType.DMA((steps, 3)),
    ]
    full = jax.ShapeDtypeStruct((rows, group), BF16)
    edge = jax.ShapeDtypeStruct((taps, group), BF16)
    if last:
        in_specs.append(vmem)
        args.append(out_grad)
        out_shape = [full] * 5 + [edge] * 2
        scratch = [pltpu.VMEM((rows, 3 * group), F32)] + scratch
    else:
        out_shape = [jax.ShapeDtypeStruct((rows, 3 * group), F32)]
    return pl.pallas_call(
        kernel,
        in_specs=in_specs,
        out_specs=[vmem] * len(out_shape),
        out_shape=out_shape,
        scratch_shapes=scratch,
        compiler_params=pltpu.CompilerParams(vmem_limit_bytes=VMEM_BYTES),
        cost_estimate=pl.CostEstimate(
            flops=6 * rows * depth * group, bytes_accessed=6 * depth * group, transcendentals=0
        ),
        name="project",
    )(*args)


def halves(matrix):
    high = matrix.astype(jnp.bfloat16)
    low = (matrix - high.astype(np.float64)).astype(jnp.bfloat16)
    return high, low


def transforms(length, taps):
    size = length + taps
    angle = 2 * np.pi / size * np.outer(np.arange(size // 2) + 0.5, np.arange(size))
    there = np.concatenate([np.cos(angle), -np.sin(angle)], axis=0)
    back = there.T * (2.0 / size)
    lags = back[np.arange(taps, 0, -1)]
    rows = np.concatenate([back[taps:], back[:length], lags], axis=0)
    return [*halves(there), *halves(rows)]


def middle(query, keys, values, product, conv_in_grad, before, after, filter_taps, out_grad, order):
    length, group = query.shape
    taps = filter_taps.shape[0]
    half = (length + taps) // 2
    width = min(256, group)
    blocks = order.shape[0]
    own = length // blocks
    mats = [jnp.asarray(m) for m in transforms(length, taps)]

    def kernel(order_ref, th_ref, tl_ref, bh_ref, bl_ref, q_ref, k_ref, v_ref, p_ref, c_ref, before_ref, after_ref,
               taps_ref, grad_ref, mixed_ref, qg_ref, kg_ref, vg_ref, fg_ref, sq, sk, sv):
        def there(x, start):
            stop = start + x.shape[0]
            y = jnp.dot(th_ref[:, start:stop], x, preferred_element_type=F32)
            if EXACT:
                y = y + jnp.dot(tl_ref[:, start:stop], x, preferred_element_type=F32)
            return y

        def back(start, stop, re, im):
            y = jnp.concatenate([re, im], axis=0)
            high = y.astype(BF16)
            out = jnp.dot(bh_ref[start:stop, :], high, preferred_element_type=F32)
            if EXACT:
                low = (y - high.astype(F32)).astype(BF16)
                out = out + jnp.dot(bh_ref[start:stop, :], low, preferred_element_type=F32)
                out = out + jnp.dot(bl_ref[start:stop, :], high, preferred_element_type=F32)
            return out

        f = taps_ref[...]
        f_high = f.astype(BF16)
        h = there(f_high, 0)
        if EXACT:
            f_low = (f - f_high.astype(F32)).astype(BF16)
            h = h + jnp.dot(th_ref[:, :taps], f_low, preferred_element_type=F32)
        hr, hi = h[:half], h[half:]
        p = there(p_ref[...], taps) + there(before_ref[...], 0)
        pr, pi = p[:half], p[half:]
        c = there(c_ref[...], 0)
        cr, ci = c[:half], c[half:]
        g = c + there(after_ref[...], length)
        gr, gi = g[:half], g[half:]
        conv = back(0, length, pr * hr - pi * hi, pr * hi + pi * hr)
        product_grad = back(length, 2 * length, hr * gr + hi * gi, hr * gi - hi * gr)
        fg_ref[...] = back(2 * length, 2 * length + taps, cr * pr + ci * pi, cr * pi - ci * pr).astype(BF16)
        mixed_ref[...] = (q_ref[...].astype(F32) * conv).astype(BF16)
        sq[...] = (grad_ref[...].astype(F32) * conv).astype(BF16)
        sk[...] = (product_grad * v_ref[...].astype(F32)).astype(BF16)
        sv[...] = (product_grad * k_ref[...].astype(F32)).astype(BF16)
        for b in range(blocks):
            here = pl.ds(pl.multiple_of(order_ref[b] * own, own), own)
            to = slice(b * own, (b + 1) * own)
            qg_ref[to, :] = sq[here, :]
            kg_ref[to, :] = sk[here, :]
            vg_ref[to, :] = sv[here, :]

    def whole(a):
        return pl.BlockSpec(a.shape, lambda i: (0, 0))

    def cols(a):
        return pl.BlockSpec((a.shape[0], width), lambda i: (0, i))

    arrays = [query, keys, values, product, conv_in_grad, before, after, filter_taps, out_grad]
    full = jax.ShapeDtypeStruct((length, group), BF16)
    outs = [full] * 4 + [jax.ShapeDtypeStruct((taps, group), BF16)]
    return pl.pallas_call(
        kernel,
        grid=(group // width,),
        in_specs=[pl.BlockSpec(memory_space=pltpu.SMEM)] + [whole(m) for m in mats] + [cols(a) for a in arrays],
        out_specs=[cols(a) for a in outs],
        out_shape=outs,
        scratch_shapes=[pltpu.VMEM((length, width), BF16)] * 3,
        compiler_params=pltpu.CompilerParams(vmem_limit_bytes=VMEM_BYTES),
        cost_estimate=pl.CostEstimate(flops=3 * 10**9, bytes_accessed=8 * 10**6, transcendentals=0),
        name="filter",
    )(order, *mats, *arrays)


def backward_chunk(grads, weights, start, depth, parts):
    rows, group = grads[0].shape
    step = step_rows(depth)
    steps = depth // step
    share = rows // parts

    def kernel(*refs):
        g_refs, w_refs, out_refs = refs[:3], refs[3:6], refs[6 : 6 + parts]
        w_buf, w_sem = refs[6 + parts :]

        def weight_copy(k, m):
            return pltpu.make_async_copy(
                w_refs[m].at[pl.ds(start + k * step, step), :], w_buf.at[k, m], w_sem.at[k, m]
            )

        for k in range(steps):
            for m in range(3):
                weight_copy(k, m).start()

        def body(k, carry):
            total = None
            for m in range(3):
                weight_copy(k, m).wait()
                term = lax.dot_general(
                    g_refs[m][...], w_buf[k, m], (((1,), (1,)), ((), ())), preferred_element_type=F32
                )
                total = term if total is None else total + term
            at = pl.ds(pl.multiple_of(k * step, step), step)
            for i in range(parts):
                out_refs[i][:, at] = total[i * share : (i + 1) * share].astype(BF16)
            return carry

        lax.fori_loop(0, steps, body, 0)

    vmem, anywhere = pl.BlockSpec(memory_space=pltpu.VMEM), pl.BlockSpec(memory_space=pl.ANY)
    return pl.pallas_call(
        kernel,
        in_specs=[vmem] * 3 + [anywhere] * 3,
        out_specs=[vmem] * parts,
        out_shape=[jax.ShapeDtypeStruct((share, depth), BF16)] * parts,
        scratch_shapes=[
            pltpu.VMEM((steps, 3, step, group), BF16),
            pltpu.SemaphoreType.DMA((steps, 3)),
        ],
        compiler_params=pltpu.CompilerParams(vmem_limit_bytes=VMEM_BYTES),
        cost_estimate=pl.CostEstimate(
            flops=6 * rows * depth * group, bytes_accessed=6 * depth * group, transcendentals=0
        ),
        name="project_back",
    )(*grads, *weights)


def on_device(inputs, query_weight, key_weight, value_weight, filter_taps, out_grad):
    weights = (query_weight, key_weight, value_weight)
    tp = lax.axis_size("tp")
    paired = tp == 8
    own_rows, width = inputs.shape
    taps = filter_taps.shape[0]
    order = row_order(tp, paired)
    depth = width // FWD_CHUNKS
    acc = None
    for i in range(FWD_CHUNKS):
        pieces = gather_rows(inputs[:, i * depth : (i + 1) * depth], paired)
        last = i == FWD_CHUNKS - 1
        out = forward_chunk(pieces, weights, i * depth, depth, acc, last, order, out_grad, taps)
        acc = out[0]
    query, keys, values, product, conv_in_grad, tail, head = out
    before = from_behind(tail, "ctx", 1)
    after = from_behind(head, "ctx", -1)
    mixed, query_grad, keys_grad, values_grad, local_taps = middle(
        query, keys, values, product, conv_in_grad, before, after, filter_taps, out_grad, order
    )
    filter_grad = lax.psum(local_taps, "ctx").astype(F32)
    depth = width // BWD_CHUNKS
    summed = []
    for i in range(BWD_CHUNKS):
        parts = backward_chunk(
            (query_grad, keys_grad, values_grad), weights, i * depth, depth, 2 if paired else 1
        )
        summed.append(scatter_rows(parts, own_rows, paired))
    return mixed, jnp.concatenate(summed, axis=1), filter_grad


def solution(mesh):
    in_specs = (
        P(("ctx", "tp"), None),
        P(None, "tp"),
        P(None, "tp"),
        P(None, "tp"),
        P(None, "tp"),
        P("ctx", "tp"),
    )
    out_specs = (P("ctx", "tp"), P(("ctx", "tp"), None), P(None, "tp"))
    return jax.shard_map(
        on_device, mesh=mesh, in_specs=in_specs, out_specs=out_specs, check_vma=False
    )
```

time: 276 us -> 184 us (0.67)
  matrix products: 99.5 us -> 0 us
  Pallas kernels: 0 us -> 75 us
  other arithmetic: 44.3 us -> 3.51 us
  waiting for transfers between devices: 90.5 us -> 65.2 us
  local copies, waits for them, and re-layouts: 20.6 us -> 5.8 us
  starting transfers between devices: 4.99 us -> 19.5 us
    dot_general x6 -> x0, matrix products: 99.5 us -> none  [the longest x3 44.5 us: contract(): lax.dot_general(left, right, (((1,), (1,)), ((), ())), preferred_element_...]
    pallas_call x0 -> x5, Pallas kernels: none -> 75 us  [the longest x2 39.9 us: forward_chunk(): pl.pallas_call(kernel, in_specs=in_specs, out_specs=[vmem] * len(out_shap...]
    reduce_scatter x1 -> x0, waiting for transfers between devices: 51.8 us -> none  [on_device(): lax.psum_scatter((total + contract(values_rows, value_weight)).astype(jnp...]
    all_gather x1 -> x0, waiting for transfers between devices: 34.6 us -> none  [on_device(): piece = lax.all_gather(inputs, 'tp', axis=0, tiled=True)]
    ppermute x0 -> x14, waiting for transfers between devices: none -> 34 us  [swap(): lax.ppermute(block, 'tp', [(i, i ^ offsets[i % 2]) for i in range(8)])]
    add x1 -> x0, other arithmetic: 24 us -> none  [backward_filter(): total = total + filter_taps[offset] * padded[offset:offset + length]]
    psum x1, waiting for transfers between devices: 0.02 us -> 22 us  [on_device(): filter_grad = lax.psum(local_taps, 'ctx').astype(F32)]
    reduce_sum x8 -> x0, other arithmetic: 18.2 us -> none  [tap_products(): rows_out.append(jnp.sum(grad_rows * padded[start:start + length], axis=0))]
  transfers between devices with their start and end apart: 5 -> 17, of which waited for: 3 -> 10; matrix products, arithmetic and copies ran while one was open for 29% -> 2% of each run, Pallas kernels for 0% -> 18%
where the time goes in v1:
time: 184 us; the launch traced here: 183 us
  Pallas kernels  75 us (41%)
  waiting for transfers between devices  65.2 us (35%)
  starting transfers between devices  19.5 us (11%)
  between operations  14.3 us (8%)
  local copies, waits for them, and re-layouts  5.8 us (3%)
  other arithmetic  3.51 us (2%)
    pallas_call x2, Pallas kernels, forward_chunk(): pl.pallas_call(kernel, in_specs=in_specs, out_specs=[vmem] * len(out_shap...  39.9 us
    ppermute x14, waiting for transfers between devices, swap(): lax.ppermute(block, 'tp', [(i, i ^ offsets[i % 2]) for i in range(8)])  34 us
    pallas_call x2, Pallas kernels, backward_chunk(): pl.pallas_call(kernel, in_specs=[vmem] * 3 + [anywhere] * 3, out_specs=[v...  26.4 us
    psum x1, waiting for transfers between devices, on_device(): filter_grad = lax.psum(local_taps, 'ctx').astype(F32)  22 us
    ppermute x14, starting transfers between devices, swap(): lax.ppermute(block, 'tp', [(i, i ^ offsets[i % 2]) for i in range(8)])  14.2 us
    ppermute x2, waiting for transfers between devices, from_behind(): return lax.ppermute(block, axis, route)  9.21 us
    pallas_call x1, Pallas kernels, middle(): pl.pallas_call(kernel, grid=(group // width,), in_specs=[pl.BlockSpec(mem...  8.71 us
    ppermute x2, starting transfers between devices, from_behind(): return lax.ppermute(block, axis, route)  5.29 us
  transfers between devices with their start and end apart: 17, of which 10 were waited for; matrix products, arithmetic and copies ran while one was open for 2% of the time, Pallas kernels for 18%

profile of v1, /device:TPU:0, one launch (start us, length us, event | category | flops | bytes accessed | tf_op | source)
XLA Modules:
  0.0 183.3 jit_solution(10748267462407532311)
XLA Ops:
  8.3 3.0 %collective-permute-start.4 = (bf16[32,4096]{1,0:T(8,128)(2,1)S(1)}, bf16[32,4096]{1,0:T(8,128)(2,1)S(1)}, u32[]{:S(2)}, u32[]{:S(2)}) collective-permute-start(bf16[32,4096]{1,0:T(8,128)(2,1)S(1)} %get-tuple-element.35), channel_id=1, source_target_pairs={{0,2},{1,5},{2,0},{3,7},{4,6},{5,1},{6,4},{7,3},{8,10},{9,13},{10,... | collective-permute-start | bytes 786440 | tf_op jit(solution)/shard_map/ppermute | solution.py:25
  11.4 4.3 %collective-permute-done.4 = bf16[32,4096]{1,0:T(8,128)(2,1)S(1)} collective-permute-done((bf16[32,4096]{1,0:T(8,128)(2,1)S(1)}, bf16[32,4096]{1,0:T(8,128)(2,1)S(1)}, u32[]{:S(2)}, u32[]{:S(2)}) %collective-permute-start.4) | collective-permute-done | bytes 262176 | tf_op jit(solution)/shard_map/ppermute | solution.py:25
  15.7 2.1 %collective-permute-start.5 = (bf16[64,4096]{1,0:T(8,128)(2,1)S(1)}, bf16[64,4096]{1,0:T(8,128)(2,1)S(1)}, u32[]{:S(2)}, u32[]{:S(2)}) collective-permute-start(bf16[64,4096]{1,0:T(8,128)(2,1)S(1)} %pad_maximum_fusion.1.refs_1_), channel_id=1, source_target_pairs={{0,4},{1,3},{2,6},{3,1},{4,0},{5,7},{6,2},{7,5},{8,12},{9,11},{10,... | collective-permute-start | bytes 1572872 | tf_op jit(solution)/shard_map/ppermute | solution.py:25
  17.8 1.4 collective-permute-done
  19.2 2.4 %collective-permute-start.1 = (bf16[64,4096]{1,0:T(8,128)(2,1)S(1)}, bf16[64,4096]{1,0:T(8,128)(2,1)S(1)}, u32[]{:S(2)}, u32[]{:S(2)}) collective-permute-start(bf16[64,4096]{1,0:T(8,128)(2,1)S(1)} %pad_maximum_fusion.refs_1_), channel_id=1, source_target_pairs={{0,4},{1,3},{2,6},{3,1},{4,0},{5,7},{6,2},{7,5},{8,12},{9,11},{10,... | collective-permute-start | bytes 1572872 | tf_op jit(solution)/shard_map/ppermute | solution.py:25
  21.7 3.3 %collective-permute-done.5.refs_2_ = bf16[64,4096]{1,0:T(8,128)(2,1)S(1)} collective-permute-done((bf16[64,4096]{1,0:T(8,128)(2,1)S(1)}, bf16[64,4096]{1,0:T(8,128)(2,1)S(1)}, u32[]{:S(2)}, u32[]{:S(2)}) %collective-permute-start.5) | collective-permute-done | bytes 524320 | tf_op jit(solution)/shard_map/ppermute | solution.py:25
  26.1 4.5 %collective-permute-done.1.refs_2_ = bf16[64,4096]{1,0:T(8,128)(2,1)S(1)} collective-permute-done((bf16[64,4096]{1,0:T(8,128)(2,1)S(1)}, bf16[64,4096]{1,0:T(8,128)(2,1)S(1)}, u32[]{:S(2)}, u32[]{:S(2)}) %collective-permute-start.1) | collective-permute-done | bytes 524320 | tf_op jit(solution)/shard_map/ppermute | solution.py:25
  32.2 19.2 %project.2.refs_8_ = f32[256,3072]{1,0:T(8,128)} custom-call(s32[8]{0:T(128)} %stack.35.refs_0_.order_ref, bf16[64,4096]{1,0:T(8,128)(2,1)} %copy-done.1, bf16[64,4096]{1,0:T(8,128)(2,1)} %copy-done.5, bf16[64,4096]{1,0:T(8,128)(2,1)} %copy-done.6, bf16[64,4096]{1,0:T(8,128)(2,1)} %copy-done.7, bf16[8192,1024]{1,0:T(8,128)(2,1)} %refs_3_.3, ...), custom_call_target="tpu_custom_call" | custom-call | flops 6442450944 | bytes 25165824 | tf_op jit(solution)/shard_map/project/pallas_call | solution.py:151
  53.1 20.7 %project.3 = (bf16[256,1024]{1,0:T(8,128)(2,1)}, bf16[256,1024]{1,0:T(8,128)(2,1)}, bf16[256,1024]{1,0:T(8,128)(2,1)}, bf16[256,1024]{1,0:T(8,128)(2,1)}, bf16[2...) custom-call(s32[8]{0:T(128)} %stack.35.refs_0_.order_ref, bf16[64,4096]{1,0:T(8,128)(2,1)} %copy-done, ...), custom_call_target="tpu_custom_call" | custom-call | flops 6442450944 | bytes 25165824 | tf_op jit(solution)/shard_map/project/pallas_call | solution.py:151
  73.8 4.0 %collective-permute-start.8 = (bf16[128,1024]{1,0:T(8,128)(2,1)}, bf16[128,1024]{1,0:T(8,128)(2,1)S(1)}, u32[]{:S(2)}, u32[]{:S(2)}) collective-permute-start(bf16[128,1024]{1,0:T(8,128)(2,1)} %get-tuple-element.24), channel_id=1, source_target_pairs={{0,8},{8,16},{16,24},{1,9},{9,17},{17,25},{2,10},{10,18},{18,26},{... | collective-permute-start | bytes 786440 | tf_op jit(solution)/shard_map/ppermute | solution.py:20
  77.8 1.3 collective-permute-start.9
  79.1 5.2 %collective-permute-done.8.before_ref = bf16[128,1024]{1,0:T(8,128)(2,1)S(1)} collective-permute-done((bf16[128,1024]{1,0:T(8,128)(2,1)}, bf16[128,1024]{1,0:T(8,128)(2,1)S(1)}, u32[]{:S(2)}, u32[]{:S(2)}) %collective-permute-start.8) | collective-permute-done | bytes 262176 | tf_op jit(solution)/shard_map/ppermute | solution.py:20
  84.3 4.0 %collective-permute-done.9.after_ref = bf16[128,1024]{1,0:T(8,128)(2,1)S(1)} collective-permute-done((bf16[128,1024]{1,0:T(8,128)(2,1)}, bf16[128,1024]{1,0:T(8,128)(2,1)S(1)}, u32[]{:S(2)}, u32[]{:S(2)}) %collective-permute-start.9) | collective-permute-done | bytes 262176 | tf_op jit(solution)/shard_map/ppermute | solution.py:20
  89.0 8.7 %filter.1 = (bf16[256,1024]{1,0:T(8,128)(2,1)}, bf16[256,1024]{1,0:T(8,128)(2,1)}, bf16[256,1024]{1,0:T(8,128)(2,1)}, bf16[256,1024]{1,0:T(8,128)(2,1)}, bf16[128,1024]{1,0:T(8,128)(2,1)}) custom-call(s32[8]{0:T(128)} %stack.35.refs_0_.order_ref, bf16[384,384]{1,0:T(8,128)(2,1)} %constant.28.clone.th_ref, bf16[384,384]{1,0:T(8,128)(2,1)} %constant.29.clone.tl_ref, ...), custom_call_target="tpu_custom_call" | custom-call | flops 3000000000 | bytes 8000000 | tf_op jit(solution)/shard_map/filter/pallas_call | solution.py:245
  97.7 13.2 %project_back.2 = (bf16[128,4096]{1,0:T(8,128)(2,1)}, bf16[128,4096]{1,0:T(8,128)(2,1)}) custom-call(bf16[256,1024]{1,0:T(8,128)(2,1)} %get-tuple-element.27.refs_0_, bf16[256,1024]{1,0:T(8,128)(2,1)} %get-tuple-element.28.refs_1_, bf16[256,1024]{1,0:T(8,128)(2,1)} %get-tuple-element.29.refs_2_, bf16[8192,1024]{1,0:T(8,128)(2,1)} %refs_3_.3, ...), custom_call_target="tpu_custom_call" | custom-call | flops 6442450944 | bytes 25165824 | tf_op jit(solution)/shard_map/project_back/pallas_call | solution.py:293
  111.0 13.2 %project_back.3 = (bf16[128,4096]{1,0:T(8,128)(2,1)}, bf16[128,4096]{1,0:T(8,128)(2,1)}) custom-call(bf16[256,1024]{1,0:T(8,128)(2,1)} %get-tuple-element.27.refs_0_, bf16[256,1024]{1,0:T(8,128)(2,1)} %get-tuple-element.28.refs_1_, bf16[256,1024]{1,0:T(8,128)(2,1)} %get-tuple-element.29.refs_2_, bf16[8192,1024]{1,0:T(8,128)(2,1)} %refs_3_.3, ...), custom_call_target="tpu_custom_call" | custom-call | flops 6442450944 | bytes 25165824 | tf_op jit(solution)/shard_map/project_back/pallas_call | solution.py:293
  124.8 22.0 %all-reduce.2.cloned.1.call-done = bf16[128,1024]{1,0:T(8,128)(2,1)} async-done(((bf16[128,1024]{1,0:T(8,128)(2,1)}), bf16[128,1024]{1,0:T(8,128)(2,1)}) %all-reduce.2.cloned.1.call-update) | async-done | bytes 262160 | tf_op jit(solution)/shard_map/psum | solution.py:330
  146.8 1.8 convert_element_type.83
  148.9 1.5 collective-permute-start.11
  151.7 6.5 %collective-permute-done.11 = bf16[64,4096]{1,0:T(8,128)(2,1)S(1)} collective-permute-done((bf16[64,4096]{1,0:T(8,128)(2,1)S(1)}, bf16[64,4096]{1,0:T(8,128)(2,1)S(1)}, u32[]{:S(2)}, u32[]{:S(2)}) %collective-permute-start.11) | collective-permute-done | bytes 524320 | tf_op jit(solution)/shard_map/ppermute | solution.py:25
  158.2 1.5 collective-permute-start.12
  159.8 9.2 %collective-permute-done.14 = bf16[64,4096]{1,0:T(8,128)(2,1)S(1)} collective-permute-done((bf16[64,4096]{1,0:T(8,128)(2,1)S(1)}, bf16[64,4096]{1,0:T(8,128)(2,1)S(1)}, u32[]{:S(2)}, u32[]{:S(2)}) %collective-permute-start.14) | collective-permute-done | bytes 524320 | tf_op jit(solution)/shard_map/ppermute | solution.py:25
  169.1 1.5 collective-permute-start.15
  170.7 4.8 %collective-permute-done.15 = bf16[32,4096]{1,0:T(8,128)(2,1)S(1)} collective-permute-done((bf16[32,4096]{1,0:T(8,128)(2,1)S(1)}, bf16[32,4096]{1,0:T(8,128)(2,1)S(1)}, u32[]{:S(2)}, u32[]{:S(2)}) %collective-permute-start.15) | collective-permute-done | bytes 262176 | tf_op jit(solution)/shard_map/ppermute | solution.py:25
  (54 shorter events, 9.6 us)
Async XLA Ops:
  7.2 139.7 %all-reduce.2.cloned.1.call-start = ((), (), s32[]{:S(2)}) async-start(), calls=%async_computation | async-start | bytes 524288 | tf_op jit(solution)/shard_map/psum | solution.py:330
  8.3 7.4 %collective-permute-start.4 = (bf16[32,4096]{1,0:T(8,128)(2,1)S(1)}, bf16[32,4096]{1,0:T(8,128)(2,1)S(1)}, u32[]{:S(2)}, u32[]{:S(2)}) collective-permute-start(bf16[32,4096]{1,0:T(8,128)(2,1)S(1)} %get-tuple-element.35), channel_id=1, source_target_pairs={{0,2},{1,5},{2,0},{3,7},{4,6},{5,1},{6,4},{7,3},{8,10},{9,13},{10,... | collective-permute-start | bytes 786440 | tf_op jit(solution)/shard_map/ppermute | solution.py:25
  11.3 7.9 %collective-permute-start = (bf16[32,4096]{1,0:T(8,128)(2,1)S(1)}, bf16[32,4096]{1,0:T(8,128)(2,1)S(1)}, u32[]{:S(2)}, u32[]{:S(2)}) collective-permute-start(bf16[32,4096]{1,0:T(8,128)(2,1)S(1)} %get-tuple-element.36), channel_id=1, source_target_pairs={{0,2},{1,5},{2,0},{3,7},{4,6},{5,1},{6,4},{7,3},{8,10},{9,13},{10,... | collective-permute-start | bytes 786440 | tf_op jit(solution)/shard_map/ppermute | solution.py:25
  15.7 14.9 %copy-start.1 = (bf16[64,4096]{1,0:T(8,128)(2,1)}, bf16[64,4096]{1,0:T(8,128)(2,1)S(1)}, u32[]{:S(2)}) copy-start(bf16[64,4096]{1,0:T(8,128)(2,1)S(1)} %pad_maximum_fusion.1.refs_1_) | copy-start | bytes 1572868
  15.7 9.3 %collective-permute-start.5 = (bf16[64,4096]{1,0:T(8,128)(2,1)S(1)}, bf16[64,4096]{1,0:T(8,128)(2,1)S(1)}, u32[]{:S(2)}, u32[]{:S(2)}) collective-permute-start(bf16[64,4096]{1,0:T(8,128)(2,1)S(1)} %pad_maximum_fusion.1.refs_1_), channel_id=1, source_target_pairs={{0,4},{1,3},{2,6},{3,1},{4,0},{5,7},{6,2},{7,5},{8,12},{9,11},{10,... | collective-permute-start | bytes 1572872 | tf_op jit(solution)/shard_map/ppermute | solution.py:25
  19.2 32.2 %copy-start = (bf16[64,4096]{1,0:T(8,128)(2,1)}, bf16[64,4096]{1,0:T(8,128)(2,1)S(1)}, u32[]{:S(2)}) copy-start(bf16[64,4096]{1,0:T(8,128)(2,1)S(1)} %pad_maximum_fusion.refs_1_) | copy-start | bytes 1572868
  19.2 11.3 %collective-permute-start.1 = (bf16[64,4096]{1,0:T(8,128)(2,1)S(1)}, bf16[64,4096]{1,0:T(8,128)(2,1)S(1)}, u32[]{:S(2)}, u32[]{:S(2)}) collective-permute-start(bf16[64,4096]{1,0:T(8,128)(2,1)S(1)} %pad_maximum_fusion.refs_1_), channel_id=1, source_target_pairs={{0,4},{1,3},{2,6},{3,1},{4,0},{5,7},{6,2},{7,5},{8,12},{9,11},{10,... | collective-permute-start | bytes 1572872 | tf_op jit(solution)/shard_map/ppermute | solution.py:25
  21.7 8.9 %collective-permute-start.6 = (bf16[64,4096]{1,0:T(8,128)(2,1)S(1)}, bf16[64,4096]{1,0:T(8,128)(2,1)S(1)}, u32[]{:S(2)}, u32[]{:S(2)}) collective-permute-start(bf16[64,4096]{1,0:T(8,128)(2,1)S(1)} %pad_maximum_fusion.1.refs_1_), channel_id=1, source_target_pairs={{0,1},{1,0},{2,3},{3,2},{4,5},{5,4},{6,7},{7,6},{8,9},{9,8},{10,11... | collective-permute-start | bytes 1572872 | tf_op jit(solution)/shard_map/ppermute | solution.py:25
  25.0 5.7 %copy-start.5 = (bf16[64,4096]{1,0:T(8,128)(2,1)}, bf16[64,4096]{1,0:T(8,128)(2,1)S(1)}, u32[]{:S(2)}) copy-start(bf16[64,4096]{1,0:T(8,128)(2,1)S(1)} %collective-permute-done.5.refs_2_) | copy-start | bytes 1572868
  25.0 5.6 %collective-permute-start.7 = (bf16[64,4096]{1,0:T(8,128)(2,1)S(1)}, bf16[64,4096]{1,0:T(8,128)(2,1)S(1)}, u32[]{:S(2)}, u32[]{:S(2)}) collective-permute-start(bf16[64,4096]{1,0:T(8,128)(2,1)S(1)} %collective-permute-done.5.refs_2_), channel_id=1, source_target_pairs={{0,1},{1,0},{2,3},{3,2},{4,5},{5,4},{6,7},{7,6},{8,9},{9,8},{10,11... | collective-permute-start | bytes 1572872 | tf_op jit(solution)/shard_map/ppermute | solution.py:25
  25.7 25.8 %collective-permute-start.2 = (bf16[64,4096]{1,0:T(8,128)(2,1)S(1)}, bf16[64,4096]{1,0:T(8,128)(2,1)S(1)}, u32[]{:S(2)}, u32[]{:S(2)}) collective-permute-start(bf16[64,4096]{1,0:T(8,128)(2,1)S(1)} %pad_maximum_fusion.refs_1_), channel_id=1, source_target_pairs={{0,1},{1,0},{2,3},{3,2},{4,5},{5,4},{6,7},{7,6},{8,9},{9,8},{10,11... | collective-permute-start | bytes 1572872 | tf_op jit(solution)/shard_map/ppermute | solution.py:25
  30.6 20.9 %copy-start.4 = (bf16[64,4096]{1,0:T(8,128)(2,1)}, bf16[64,4096]{1,0:T(8,128)(2,1)S(1)}, u32[]{:S(2)}) copy-start(bf16[64,4096]{1,0:T(8,128)(2,1)S(1)} %collective-permute-done.1.refs_2_) | copy-start | bytes 1572868
  30.6 20.9 %collective-permute-start.3 = (bf16[64,4096]{1,0:T(8,128)(2,1)S(1)}, bf16[64,4096]{1,0:T(8,128)(2,1)S(1)}, u32[]{:S(2)}, u32[]{:S(2)}) collective-permute-start(bf16[64,4096]{1,0:T(8,128)(2,1)S(1)} %collective-permute-done.1.refs_2_), channel_id=1, source_target_pairs={{0,1},{1,0},{2,3},{3,2},{4,5},{5,4},{6,7},{7,6},{8,9},{9,8},{10,11... | collective-permute-start | bytes 1572872 | tf_op jit(solution)/shard_map/ppermute | solution.py:25
  73.8 10.5 %collective-permute-start.8 = (bf16[128,1024]{1,0:T(8,128)(2,1)}, bf16[128,1024]{1,0:T(8,128)(2,1)S(1)}, u32[]{:S(2)}, u32[]{:S(2)}) collective-permute-start(bf16[128,1024]{1,0:T(8,128)(2,1)} %get-tuple-element.24), channel_id=1, source_target_pairs={{0,8},{8,16},{16,24},{1,9},{9,17},{17,25},{2,10},{10,18},{18,26},{... | collective-permute-start | bytes 786440 | tf_op jit(solution)/shard_map/ppermute | solution.py:20
  77.8 10.5 %collective-permute-start.9 = (bf16[128,1024]{1,0:T(8,128)(2,1)}, bf16[128,1024]{1,0:T(8,128)(2,1)S(1)}, u32[]{:S(2)}, u32[]{:S(2)}) collective-permute-start(bf16[128,1024]{1,0:T(8,128)(2,1)} %get-tuple-element.25), channel_id=1, source_target_pairs={{8,0},{16,8},{24,16},{9,1},{17,9},{25,17},{10,2},{18,10},{26,18},{... | collective-permute-start | bytes 786440 | tf_op jit(solution)/shard_map/ppermute | solution.py:20
  84.3 4.0 %copy-start.10 = (bf16[128,1024]{1,0:T(8,128)(2,1)}, bf16[128,1024]{1,0:T(8,128)(2,1)S(1)}, u32[]{:S(2)}) copy-start(bf16[128,1024]{1,0:T(8,128)(2,1)S(1)} %collective-permute-done.8.before_ref) | copy-start | bytes 786436
  110.9 37.7 %collective-permute-start.10 = (bf16[128,4096]{1,0:T(8,128)(2,1)}, bf16[128,4096]{1,0:T(8,128)(2,1)S(1)}, u32[]{:S(2)}, u32[]{:S(2)}) collective-permute-start(bf16[128,4096]{1,0:T(8,128)(2,1)} %get-tuple-element.31), channel_id=1, source_target_pairs={{0,1},{1,0},{2,3},{3,2},{4,5},{5,4},{6,7},{7,6},{8,9},{9,8},{10,11... | collective-permute-start | bytes 3145736 | tf_op jit(solution)/shard_map/ppermute | solution.py:25
  111.0 37.6 %copy-start.2 = (bf16[128,4096]{1,0:T(8,128)(2,1)S(1)}, bf16[128,4096]{1,0:T(8,128)(2,1)}, u32[]{:S(2)}) copy-start(bf16[128,4096]{1,0:T(8,128)(2,1)} %get-tuple-element.30) | copy-start | bytes 3145732
  124.2 26.3 %collective-permute-start.13 = (bf16[128,4096]{1,0:T(8,128)(2,1)}, bf16[128,4096]{1,0:T(8,128)(2,1)S(1)}, u32[]{:S(2)}, u32[]{:S(2)}) collective-permute-start(bf16[128,4096]{1,0:T(8,128)(2,1)} %get-tuple-element.33), channel_id=1, source_target_pairs={{0,1},{1,0},{2,3},{3,2},{4,5},{5,4},{6,7},{7,6},{8,9},{9,8},{10,11... | collective-permute-start | bytes 3145736 | tf_op jit(solution)/shard_map/ppermute | solution.py:25
  148.6 1.8 %copy-start.3 = (bf16[128,4096]{1,0:T(8,128)(2,1)S(1)}, bf16[128,4096]{1,0:T(8,128)(2,1)}, u32[]{:S(2)}) copy-start(bf16[128,4096]{1,0:T(8,128)(2,1)} %get-tuple-element.32) | copy-start | bytes 3145732
  148.9 9.2 %collective-permute-start.11 = (bf16[64,4096]{1,0:T(8,128)(2,1)S(1)}, bf16[64,4096]{1,0:T(8,128)(2,1)S(1)}, u32[]{:S(2)}, u32[]{:S(2)}) collective-permute-start(bf16[64,4096]{1,0:T(8,128)(2,1)S(1)} %slice.49), channel_id=1, source_target_pairs={{0,4},{1,3},{2,6},{3,1},{4,0},{5,7},{6,2},{7,5},{8,12},{9,11},{10,... | collective-permute-start | bytes 1572872 | tf_op jit(solution)/shard_map/ppermute | solution.py:25
  150.8 18.2 %collective-permute-start.14 = (bf16[64,4096]{1,0:T(8,128)(2,1)S(1)}, bf16[64,4096]{1,0:T(8,128)(2,1)S(1)}, u32[]{:S(2)}, u32[]{:S(2)}) collective-permute-start(bf16[64,4096]{1,0:T(8,128)(2,1)S(1)} %slice.54), channel_id=1, source_target_pairs={{0,4},{1,3},{2,6},{3,1},{4,0},{5,7},{6,2},{7,5},{8,12},{9,11},{10,... | collective-permute-start | bytes 1572872 | tf_op jit(solution)/shard_map/ppermute | solution.py:25
  158.2 12.4 %collective-permute-start.12 = (bf16[32,4096]{1,0:T(8,128)(2,1)S(1)}, bf16[32,4096]{1,0:T(8,128)(2,1)S(1)}, u32[]{:S(2)}, u32[]{:S(2)}) collective-permute-start(bf16[32,4096]{1,0:T(8,128)(2,1)S(1)} %add_convert_fusion.5), channel_id=1, source_target_pairs={{0,2},{1,5},{2,0},{3,7},{4,6},{5,1},{6,4},{7,3},{8,10},{9,13},{10,... | collective-permute-start | bytes 786440 | tf_op jit(solution)/shard_map/ppermute | solution.py:25
  169.1 6.4 %collective-permute-start.15 = (bf16[32,4096]{1,0:T(8,128)(2,1)S(1)}, bf16[32,4096]{1,0:T(8,128)(2,1)S(1)}, u32[]{:S(2)}, u32[]{:S(2)}) collective-permute-start(bf16[32,4096]{1,0:T(8,128)(2,1)S(1)} %add_convert_fusion.3), channel_id=1, source_target_pairs={{0,2},{1,5},{2,0},{3,7},{4,6},{5,1},{6,4},{7,3},{8,10},{9,13},{10,... | collective-permute-start | bytes 786440 | tf_op jit(solution)/shard_map/ppermute | solution.py:25
  (5 other events, 3.9 us)
Sparse Core Ops, SparseCore 0:
  111.1 35.6 all-reduce.1

commit v2 on v1

--- a/solution.py
+++ b/solution.py
@@ -8,7 +8,10 @@
 
 F32 = jnp.float32
 BF16 = jnp.bfloat16
-VMEM_BYTES = 56 * 2**20
+FWD_VMEM = 46 * 2**20
+BWD_VMEM = 46 * 2**20
+MID_VMEM = 28 * 2**20
+SLOTS = 3
 FWD_CHUNKS = 2
 BWD_CHUNKS = 2
 EXACT = True
@@ -27,14 +30,31 @@
 
 def row_order(tp, paired):
     if not paired:
-        return jnp.arange(tp, dtype=jnp.int32)
-    me = lax.axis_index("tp").astype(jnp.int32)
-    odd = me % 2
-    first = 2 + 2 * odd
+        return list(range(tp))
+    me = lax.axis_index("tp")
+    first = 2 + 2 * (me % 2)
     second = 6 - first
     own = [me, me ^ first, me ^ second, me ^ 6]
     other = me ^ 1
-    return jnp.stack(own + [other, other ^ second, other ^ first, other ^ 6])
+    return own + [other, other ^ second, other ^ first, other ^ 6]
+
+
+def block_rows(index, own):
+    start = index * own
+    return pl.ds(start if isinstance(start, int) else pl.multiple_of(start, own), own)
+
+
+def sum_over(block, axis):
+    size = lax.axis_size(axis)
+    if size & (size - 1):
+        return lax.psum(block, axis).astype(F32)
+    total, distance = block.astype(F32), 1
+    while distance < size:
+        route = [(i, i ^ distance) for i in range(size)]
+        mine = total.astype(BF16)
+        total = mine.astype(F32) + lax.ppermute(mine, axis, route).astype(F32)
+        distance *= 2
+    return total
 
 
 def gather_rows(block, paired):
@@ -57,68 +77,74 @@
 
 
 def step_rows(depth):
-    step = 1024
+    step = 512
     while depth % step:
         step //= 2
     return step
 
 
-def forward_chunk(pieces, weights, start, depth, acc, last, order, out_grad, taps):
+def stream_weights(w_refs, w_buf, w_sem, start, step, steps, compute):
+    def copy(k, m):
+        slot = lax.rem(k, SLOTS)
+        rows = pl.ds(start + k * step, step)
+        return pltpu.make_async_copy(w_refs[m].at[rows, :], w_buf.at[slot, m], w_sem.at[slot, m])
+
+    for k in range(min(SLOTS - 1, steps)):
+        for m in range(3):
+            copy(k, m).start()
+
+    def body(k, carry):
+        @pl.when(k + SLOTS - 1 < steps)
+        def _():
+            for m in range(3):
+                copy(k + SLOTS - 1, m).start()
+
+        for m in range(3):
+            copy(k, m).wait()
+        compute(k, lax.rem(k, SLOTS))
+        return carry
+
+    return lambda: lax.fori_loop(0, steps, body, 0)
+
+
+def weight_scratch(step, group):
+    return [pltpu.VMEM((SLOTS, 3, step, group), BF16), pltpu.SemaphoreType.DMA((SLOTS, 3))]
+
+
+def forward_chunk(pieces, weights, start, depth, acc, last, tp, paired, out_grad, taps):
     rows = sum(p.shape[0] for p in pieces)
     group = weights[0].shape[1]
     step = step_rows(depth)
-    steps = depth // step
-    blocks = order.shape[0]
-    own = rows // blocks
+    own = rows // tp
     n_x = len(pieces)
     has_acc = acc is not None
 
     def kernel(*refs):
-        order_ref, refs = refs[0], refs[1:]
         x_refs, w_refs, refs = refs[:n_x], refs[n_x : n_x + 3], refs[n_x + 3 :]
         if has_acc:
             acc_in, refs = refs[0], refs[1:]
         if last:
             grad_ref, refs = refs[0], refs[1:]
             q_ref, k_ref, v_ref, prod_ref, cig_ref, tail_ref, head_ref = refs[:7]
-            total, x_buf, w_buf, x_sem, w_sem = refs[7:]
+            total, x_buf, w_buf, w_sem = refs[7:]
         else:
-            total, x_buf, w_buf, x_sem, w_sem = refs
-
-        def weight_copy(k, m):
-            return pltpu.make_async_copy(
-                w_refs[m].at[pl.ds(start + k * step, step), :], w_buf.at[k, m], w_sem.at[k, m]
-            )
-
-        at, x_copies = 0, []
-        for i, piece in enumerate(x_refs):
-            x_copies.append(
-                pltpu.make_async_copy(piece, x_buf.at[pl.ds(at, piece.shape[0]), :], x_sem.at[i])
-            )
-            at += piece.shape[0]
-        for copy in x_copies:
-            copy.start()
-        for k in range(steps):
-            for m in range(3):
-                weight_copy(k, m).start()
-        if has_acc:
-            total[...] = acc_in[...]
-        else:
-            total[...] = jnp.zeros_like(total)
-        for copy in x_copies:
-            copy.wait()
-
-        def body(k, carry):
+            total, x_buf, w_buf, w_sem = refs
+
+        def compute(k, slot):
             x = x_buf[:, pl.ds(pl.multiple_of(k * step, step), step)]
             for m in range(3):
-                weight_copy(k, m).wait()
-                total[:, m * group : (m + 1) * group] += jnp.dot(x, w_buf[k, m], preferred_element_type=F32)
-            return carry
-
-        lax.fori_loop(0, steps, body, 0)
+                total[:, m * group : (m + 1) * group] += jnp.dot(x, w_buf[slot, m], preferred_element_type=F32)
+
+        run = stream_weights(w_refs, w_buf, w_sem, start, step, depth // step, compute)
+        at = 0
+        for piece in x_refs:
+            x_buf[at : at + piece.shape[0], :] = piece[...]
+            at += piece.shape[0]
+        total[...] = acc_in[...] if has_acc else jnp.zeros_like(total)
+        run()
         if last:
-            for b in range(blocks):
-                here = pl.ds(pl.multiple_of(order_ref[b] * own, own), own)
+            for b, index in enumerate(row_order(tp, paired)):
+                here = block_rows(index, own)
                 part = [total[b * own : (b + 1) * own, m * group : (m + 1) * group].astype(BF16) for m in range(3)]
                 q_ref[here, :], k_ref[here, :], v_ref[here, :] = part
                 query, keys, values = [p.astype(F32) for p in part]
@@ -128,17 +154,12 @@
             head_ref[...] = cig_ref[:taps, :]
 
     vmem, anywhere = pl.BlockSpec(memory_space=pltpu.VMEM), pl.BlockSpec(memory_space=pl.ANY)
-    in_specs = [pl.BlockSpec(memory_space=pltpu.SMEM)] + [anywhere] * (n_x + 3)
-    args = [order, *pieces, *weights]
+    in_specs = [vmem] * n_x + [anywhere] * 3
+    args = [*pieces, *weights]
     if has_acc:
         in_specs.append(vmem)
         args.append(acc)
-    scratch = [
-        pltpu.VMEM((rows, depth), BF16),
-        pltpu.VMEM((steps, 3, step, group), BF16),
-        pltpu.SemaphoreType.DMA((n_x,)),
-        pltpu.SemaphoreType.DMA((steps, 3)),
-    ]
+    scratch = [pltpu.VMEM((rows, depth), BF16), *weight_scratch(step, group)]
     full = jax.ShapeDtypeStruct((rows, group), BF16)
     edge = jax.ShapeDtypeStruct((taps, group), BF16)
     if last:
@@ -154,7 +175,7 @@
         out_specs=[vmem] * len(out_shape),
         out_shape=out_shape,
         scratch_shapes=scratch,
-        compiler_params=pltpu.CompilerParams(vmem_limit_bytes=VMEM_BYTES),
+        compiler_params=pltpu.CompilerParams(vmem_limit_bytes=FWD_VMEM),
         cost_estimate=pl.CostEstimate(
             flops=6 * rows * depth * group, bytes_accessed=6 * depth * group, transcendentals=0
         ),
@@ -178,16 +199,15 @@
     return [*halves(there), *halves(rows)]
 
 
-def middle(query, keys, values, product, conv_in_grad, before, after, filter_taps, out_grad, order):
+def middle(query, keys, values, product, conv_in_grad, before, after, filter_taps, out_grad, tp, paired):
     length, group = query.shape
     taps = filter_taps.shape[0]
     half = (length + taps) // 2
     width = min(256, group)
-    blocks = order.shape[0]
-    own = length // blocks
+    own = length // tp
     mats = [jnp.asarray(m) for m in transforms(length, taps)]
 
-    def kernel(order_ref, th_ref, tl_ref, bh_ref, bl_ref, q_ref, k_ref, v_ref, p_ref, c_ref, before_ref, after_ref,
+    def kernel(th_ref, tl_ref, bh_ref, bl_ref, q_ref, k_ref, v_ref, p_ref, c_ref, before_ref, after_ref,
                taps_ref, grad_ref, mixed_ref, qg_ref, kg_ref, vg_ref, fg_ref, sq, sk, sv):
         def there(x, start):
             stop = start + x.shape[0]
@@ -226,8 +246,8 @@
         sq[...] = (grad_ref[...].astype(F32) * conv).astype(BF16)
         sk[...] = (product_grad * v_ref[...].astype(F32)).astype(BF16)
         sv[...] = (product_grad * k_ref[...].astype(F32)).astype(BF16)
-        for b in range(blocks):
-            here = pl.ds(pl.multiple_of(order_ref[b] * own, own), own)
+        for b, index in enumerate(row_order(tp, paired)):
+            here = block_rows(index, own)
             to = slice(b * own, (b + 1) * own)
             qg_ref[to, :] = sq[here, :]
             kg_ref[to, :] = sk[here, :]
@@ -245,49 +265,37 @@
     return pl.pallas_call(
         kernel,
         grid=(group // width,),
-        in_specs=[pl.BlockSpec(memory_space=pltpu.SMEM)] + [whole(m) for m in mats] + [cols(a) for a in arrays],
+        in_specs=[whole(m) for m in mats] + [cols(a) for a in arrays],
         out_specs=[cols(a) for a in outs],
         out_shape=outs,
         scratch_shapes=[pltpu.VMEM((length, width), BF16)] * 3,
-        compiler_params=pltpu.CompilerParams(vmem_limit_bytes=VMEM_BYTES),
+        compiler_params=pltpu.CompilerParams(vmem_limit_bytes=MID_VMEM),
         cost_estimate=pl.CostEstimate(flops=3 * 10**9, bytes_accessed=8 * 10**6, transcendentals=0),
         name="filter",
-    )(order, *mats, *arrays)
+    )(*mats, *arrays)
 
 
 def backward_chunk(grads, weights, start, depth, parts):
     rows, group = grads[0].shape
     step = step_rows(depth)
-    steps = depth // step
     share = rows // parts
 
     def kernel(*refs):
         g_refs, w_refs, out_refs = refs[:3], refs[3:6], refs[6 : 6 + parts]
         w_buf, w_sem = refs[6 + parts :]
 
-        def weight_copy(k, m):
-            return pltpu.make_async_copy(
-                w_refs[m].at[pl.ds(start + k * step, step), :], w_buf.at[k, m], w_sem.at[k, m]
-            )
-
-        for k in range(steps):
-            for m in range(3):
-                weight_copy(k, m).start()
-
-        def body(k, carry):
+        def compute(k, slot):
             total = None
             for m in range(3):
-                weight_copy(k, m).wait()
                 term = lax.dot_general(
-                    g_refs[m][...], w_buf[k, m], (((1,), (1,)), ((), ())), preferred_element_type=F32
+                    g_refs[m][...], w_buf[slot, m], (((1,), (1,)), ((), ())), preferred_element_type=F32
                 )
                 total = term if total is None else total + term
             at = pl.ds(pl.multiple_of(k * step, step), step)
             for i in range(parts):
                 out_refs[i][:, at] = total[i * share : (i + 1) * share].astype(BF16)
-            return carry
-
-        lax.fori_loop(0, steps, body, 0)
+
+        stream_weights(w_refs, w_buf, w_sem, start, step, depth // step, compute)()
 
     vmem, anywhere = pl.BlockSpec(memory_space=pltpu.VMEM), pl.BlockSpec(memory_space=pl.ANY)
     return pl.pallas_call(
@@ -295,11 +303,8 @@
         in_specs=[vmem] * 3 + [anywhere] * 3,
         out_specs=[vmem] * parts,
         out_shape=[jax.ShapeDtypeStruct((share, depth), BF16)] * parts,
-        scratch_shapes=[
-            pltpu.VMEM((steps, 3, step, group), BF16),
-            pltpu.SemaphoreType.DMA((steps, 3)),
-        ],
-        compiler_params=pltpu.CompilerParams(vmem_limit_bytes=VMEM_BYTES),
+        scratch_shapes=weight_scratch(step, group),
+        compiler_params=pltpu.CompilerParams(vmem_limit_bytes=BWD_VMEM),
         cost_estimate=pl.CostEstimate(
             flops=6 * rows * depth * group, bytes_accessed=6 * depth * group, transcendentals=0
         ),
@@ -313,21 +318,20 @@
     paired = tp == 8
     own_rows, width = inputs.shape
     taps = filter_taps.shape[0]
-    order = row_order(tp, paired)
     depth = width // FWD_CHUNKS
     acc = None
     for i in range(FWD_CHUNKS):
         pieces = gather_rows(inputs[:, i * depth : (i + 1) * depth], paired)
         last = i == FWD_CHUNKS - 1
-        out = forward_chunk(pieces, weights, i * depth, depth, acc, last, order, out_grad, taps)
+        out = forward_chunk(pieces, weights, i * depth, depth, acc, last, tp, paired, out_grad, taps)
         acc = out[0]
     query, keys, values, product, conv_in_grad, tail, head = out
     before = from_behind(tail, "ctx", 1)
     after = from_behind(head, "ctx", -1)
     mixed, query_grad, keys_grad, values_grad, local_taps = middle(
-        query, keys, values, product, conv_in_grad, before, after, filter_taps, out_grad, order
+        query, keys, values, product, conv_in_grad, before, after, filter_taps, out_grad, tp, paired
     )
-    filter_grad = lax.psum(local_taps, "ctx").astype(F32)
+    filter_grad = sum_over(local_taps, "ctx")
     depth = width // BWD_CHUNKS
     summed = []
     for i in range(BWD_CHUNKS):

time: 184 us -> 123 us (0.67)
  Pallas kernels: 75 us -> 50.1 us
  waiting for transfers between devices: 65.2 us -> 45.1 us
  between operations: 14.3 us -> 0.85 us
  local copies, waits for them, and re-layouts: 5.8 us -> 2.79 us
  starting transfers between devices: 19.5 us -> 21.7 us
    psum x1 -> x0, waiting for transfers between devices: 22 us -> none  [on_device(): filter_grad = lax.psum(local_taps, 'ctx').astype(F32)]
    pallas_call x2, Pallas kernels: 39.9 us -> 22.7 us  [forward_chunk(): pl.pallas_call(kernel, in_specs=in_specs, out_specs=[vmem] * len(out_shap...]
    pallas_call x2, Pallas kernels: 26.4 us -> 20.2 us  [backward_chunk(): pl.pallas_call(kernel, in_specs=[vmem] * 3 + [anywhere] * 3, out_specs=[v...]
    ppermute x0 -> x2, waiting for transfers between devices: none -> 3.7 us  [sum_over(): total = mine.astype(F32) + lax.ppermute(mine, axis, route).astype(F32)]
    ppermute x0 -> x2, starting transfers between devices: none -> 2.64 us  [sum_over(): total = mine.astype(F32) + lax.ppermute(mine, axis, route).astype(F32)]
    unnamed x24 -> x14, local copies, waits for them, and re-layouts: 3.91 us -> 1.65 us
  transfers between devices with their start and end apart: 17 -> 18, of which waited for: 10 -> 10; matrix products, arithmetic and copies ran while one was open for 2% -> 1% of each run, Pallas kernels for 18% -> 25%
where the time goes in v2:
time: 123 us
  Pallas kernels  50.1 us (41%)
  waiting for transfers between devices  45.1 us (37%)
  starting transfers between devices  21.7 us (18%)
  local copies, waits for them, and re-layouts  2.79 us (2%)
  other arithmetic  2.65 us (2%)
    ppermute x14, waiting for transfers between devices, swap(): lax.ppermute(block, 'tp', [(i, i ^ offsets[i % 2]) for i in range(8)])  32.4 us
    pallas_call x2, Pallas kernels, forward_chunk(): pl.pallas_call(kernel, in_specs=in_specs, out_specs=[vmem] * len(out_shap...  22.7 us
    pallas_call x2, Pallas kernels, backward_chunk(): pl.pallas_call(kernel, in_specs=[vmem] * 3 + [anywhere] * 3, out_specs=[v...  20.2 us
    ppermute x14, starting transfers between devices, swap(): lax.ppermute(block, 'tp', [(i, i ^ offsets[i % 2]) for i in range(8)])  13.8 us
    ppermute x2, waiting for transfers between devices, from_behind(): return lax.ppermute(block, axis, route)  9.02 us
    pallas_call x1, Pallas kernels, middle(): pl.pallas_call(kernel, grid=(group // width,), in_specs=[whole(m) for m i...  7.2 us
    ppermute x2, starting transfers between devices, from_behind(): return lax.ppermute(block, axis, route)  5.29 us
    ppermute x2, waiting for transfers between devices, sum_over(): total = mine.astype(F32) + lax.ppermute(mine, axis, route).astype(F32)  3.7 us
  transfers between devices with their start and end apart: 18, of which 10 were waited for; matrix products, arithmetic and copies ran while one was open for 1% of the time, Pallas kernels for 25%

profile of v2, /device:TPU:0, one launch (start us, length us, event | category | flops | bytes accessed | tf_op | source)
XLA Modules:
  0.0 123.2 jit_solution(5648522441212554697)
XLA Ops:
  1.7 3.0 %collective-permute-start.4 = (bf16[32,4096]{1,0:T(8,128)(2,1)S(1)}, bf16[32,4096]{1,0:T(8,128)(2,1)S(1)}, u32[]{:S(2)}, u32[]{:S(2)}) collective-permute-start(bf16[32,4096]{1,0:T(8,128)(2,1)S(1)} %get-tuple-element.35), channel_id=1, source_target_pairs={{0,2},{1,5},{2,0},{3,7},{4,6},{5,1},{6,4},{7,3},{8,10},{9,13},{10,... | collective-permute-start | bytes 786440 | tf_op jit(solution)/shard_map/ppermute | solution.py:28
  4.8 4.3 %collective-permute-done.4 = bf16[32,4096]{1,0:T(8,128)(2,1)S(1)} collective-permute-done((bf16[32,4096]{1,0:T(8,128)(2,1)S(1)}, bf16[32,4096]{1,0:T(8,128)(2,1)S(1)}, u32[]{:S(2)}, u32[]{:S(2)}) %collective-permute-start.4) | collective-permute-done | bytes 262176 | tf_op jit(solution)/shard_map/ppermute | solution.py:28
  9.1 2.1 %collective-permute-start.5 = (bf16[64,4096]{1,0:T(8,128)(2,1)S(1)}, bf16[64,4096]{1,0:T(8,128)(2,1)S(1)}, u32[]{:S(2)}, u32[]{:S(2)}) collective-permute-start(bf16[64,4096]{1,0:T(8,128)(2,1)S(1)} %pad_maximum_fusion.1.refs_0_), channel_id=1, source_target_pairs={{0,4},{1,3},{2,6},{3,1},{4,0},{5,7},{6,2},{7,5},{8,12},{9,11},{10,... | collective-permute-start | bytes 1572872 | tf_op jit(solution)/shard_map/ppermute | solution.py:28
  11.2 1.4 %collective-permute-done = bf16[32,4096]{1,0:T(8,128)(2,1)S(1)} collective-permute-done((bf16[32,4096]{1,0:T(8,128)(2,1)S(1)}, bf16[32,4096]{1,0:T(8,128)(2,1)S(1)}, u32[]{:S(2)}, u32[]{:S(2)}) %collective-permute-start) | collective-permute-done | bytes 262176 | tf_op jit(solution)/shard_map/ppermute | solution.py:28
  12.7 2.4 %collective-permute-start.1 = (bf16[64,4096]{1,0:T(8,128)(2,1)S(1)}, bf16[64,4096]{1,0:T(8,128)(2,1)S(1)}, u32[]{:S(2)}, u32[]{:S(2)}) collective-permute-start(bf16[64,4096]{1,0:T(8,128)(2,1)S(1)} %pad_maximum_fusion.refs_0_), channel_id=1, source_target_pairs={{0,4},{1,3},{2,6},{3,1},{4,0},{5,7},{6,2},{7,5},{8,12},{9,11},{10,... | collective-permute-start | bytes 1572872 | tf_op jit(solution)/shard_map/ppermute | solution.py:28
  15.1 3.3 %collective-permute-done.5.refs_1_ = bf16[64,4096]{1,0:T(8,128)(2,1)S(1)} collective-permute-done((bf16[64,4096]{1,0:T(8,128)(2,1)S(1)}, bf16[64,4096]{1,0:T(8,128)(2,1)S(1)}, u32[]{:S(2)}, u32[]{:S(2)}) %collective-permute-start.5) | collective-permute-done | bytes 524320 | tf_op jit(solution)/shard_map/ppermute | solution.py:28
  18.9 5.1 %collective-permute-done.1.refs_1_ = bf16[64,4096]{1,0:T(8,128)(2,1)S(1)} collective-permute-done((bf16[64,4096]{1,0:T(8,128)(2,1)S(1)}, bf16[64,4096]{1,0:T(8,128)(2,1)S(1)}, u32[]{:S(2)}, u32[]{:S(2)}) %collective-permute-start.1) | collective-permute-done | bytes 524320 | tf_op jit(solution)/shard_map/ppermute | solution.py:28
  24.0 10.1 %project.2.refs_7_ = f32[256,3072]{1,0:T(8,128)S(1)} custom-call(bf16[64,4096]{1,0:T(8,128)(2,1)S(1)} %pad_maximum_fusion.1.refs_0_, bf16[64,4096]{1,0:T(8,128)(2,1)S(1)} %collective-permute-done.5.refs_1_, bf16[64,4096]{1,0:T(8,128)(2,1)S(1)} %collective-permute-done.6.refs_2_, bf16[64,4096]{1,0:T(8,128)(2,1)S(1)} %collective-permute-done.7.refs_3_, ...), custom_call_target="tpu_custom_call" | custom-call | flops 6442450944 | bytes 25165824 | tf_op jit(solution)/shard_map/project/pallas_call | solution.py:172
  34.1 1.6 %copy-done = f32[256,3072]{1,0:T(8,128)} copy-done((f32[256,3072]{1,0:T(8,128)}, f32[256,3072]{1,0:T(8,128)S(1)}, u32[]{:S(2)}) %copy-start) | copy-done | bytes 3145752
  35.7 12.6 %project.3 = (bf16[256,1024]{1,0:T(8,128)(2,1)S(1)}, bf16[256,1024]{1,0:T(8,128)(2,1)S(1)}, bf16[256,1024]{1,0:T(8,128)(2,1)S(1)}, bf16[256,1024]{1,0:T(8,128)(2...) custom-call(bf16[64,4096]{1,0:T(8,128)(2,1)S(1)} %pad_maximum_fusion.refs_0_, ...), custom_call_target="tpu_custom_call" | custom-call | flops 6442450944 | bytes 25165824 | tf_op jit(solution)/shard_map/project/pallas_call | solution.py:172
  48.4 4.0 %collective-permute-start.8 = (bf16[128,1024]{1,0:T(8,128)(2,1)S(1)}, bf16[128,1024]{1,0:T(8,128)(2,1)S(1)}, u32[]{:S(2)}, u32[]{:S(2)}) collective-permute-start(bf16[128,1024]{1,0:T(8,128)(2,1)S(1)} %get-tuple-element.24), channel_id=1, source_target_pairs={{0,8},{8,16},{16,24},{1,9},{9,17},{17,25},{2,10},{10,18},{18,26},{... | collective-permute-start | bytes 786440 | tf_op jit(solution)/shard_map/ppermute | solution.py:23
  53.7 4.9 %collective-permute-done.8.before_ref = bf16[128,1024]{1,0:T(8,128)(2,1)S(1)} collective-permute-done((bf16[128,1024]{1,0:T(8,128)(2,1)S(1)}, bf16[128,1024]{1,0:T(8,128)(2,1)S(1)}, u32[]{:S(2)}, u32[]{:S(2)}) %collective-permute-start.8) | collective-permute-done | bytes 262176 | tf_op jit(solution)/shard_map/ppermute | solution.py:23
  58.6 4.1 %collective-permute-done.9.after_ref = bf16[128,1024]{1,0:T(8,128)(2,1)S(1)} collective-permute-done((bf16[128,1024]{1,0:T(8,128)(2,1)S(1)}, bf16[128,1024]{1,0:T(8,128)(2,1)S(1)}, u32[]{:S(2)}, u32[]{:S(2)}) %collective-permute-start.9) | collective-permute-done | bytes 262176 | tf_op jit(solution)/shard_map/ppermute | solution.py:23
  62.8 7.2 %filter.1 = (bf16[256,1024]{1,0:T(8,128)(2,1)}, bf16[256,1024]{1,0:T(8,128)(2,1)S(1)}, bf16[256,1024]{1,0:T(8,128)(2,1)S(1)}, bf16[256,1024]{1,0:T(8,128)(2,1)S(1)}, bf16[128,1024]{1,0:T(8,128)(2,1)S(1)}) custom-call(bf16[384,384]{1,0:T(8,128)(2,1)S(1)} %copy-done.6, bf16[384,384]{1,0:T(8,128)(2,1)S(1)} %copy-done.5, bf16[640,384]{1,0:T(8,128)(2,1)S(1)} %copy-done.4, ...), custom_call_target="tpu_custom_call" | custom-call | flops 3000000000 | bytes 8000000 | tf_op jit(solution)/shard_map/filter/pallas_call | solution.py:265
  70.0 1.6 %collective-permute-start.16 = (bf16[128,1024]{1,0:T(8,128)(2,1)S(1)}, bf16[128,1024]{1,0:T(8,128)(2,1)S(1)}, u32[]{:S(2)}, u32[]{:S(2)}) collective-permute-start(bf16[128,1024]{1,0:T(8,128)(2,1)S(1)} %get-tuple-element.34), channel_id=1, source_target_pairs={{0,8},{8,0},{16,24},{24,16},{1,9},{9,1},{17,25},{25,17},{2,10},{10... | collective-permute-start | bytes 786440 | tf_op jit(solution)/shard_map/ppermute | solution.py:55
  71.5 10.1 %project_back.2 = (bf16[128,4096]{1,0:T(8,128)(2,1)S(1)}, bf16[128,4096]{1,0:T(8,128)(2,1)S(1)}) custom-call(bf16[256,1024]{1,0:T(8,128)(2,1)S(1)} %get-tuple-element.27.refs_0_, bf16[256,1024]{1,0:T(8,128)(2,1)S(1)} %get-tuple-element.28.refs_1_, bf16[256,1024]{1,0:T(8,128)(2,1)S(1)} %get-tuple-element.29.refs_2_, bf16[8192,1024]{1,0:T(8,128)(2,1)} %refs_3_.3, ...), custom_call_target="tpu_custom_call" | custom-call | flops 6442450944 | bytes 25165824 | tf_op jit(solution)/shard_map/project_back/pallas_call | solution.py:301
  82.9 10.1 %project_back.3 = (bf16[128,4096]{1,0:T(8,128)(2,1)S(1)}, bf16[128,4096]{1,0:T(8,128)(2,1)S(1)}) custom-call(bf16[256,1024]{1,0:T(8,128)(2,1)S(1)} %get-tuple-element.27.refs_0_, bf16[256,1024]{1,0:T(8,128)(2,1)S(1)} %get-tuple-element.28.refs_1_, bf16[256,1024]{1,0:T(8,128)(2,1)S(1)} %get-tuple-element.29.refs_2_, bf16[8192,1024]{1,0:T(8,128)(2,1)} %refs_3_.3, ...), custom_call_target="tpu_custom_call" | custom-call | flops 6442450944 | bytes 25165824 | tf_op jit(solution)/shard_map/project_back/pallas_call | solution.py:301
  93.3 3.7 %collective-permute-done.17 = bf16[128,1024]{1,0:T(8,128)(2,1)S(1)} collective-permute-done((bf16[128,1024]{1,0:T(8,128)(2,1)S(1)}, bf16[128,1024]{1,0:T(8,128)(2,1)S(1)}, u32[]{:S(2)}, u32[]{:S(2)}) %collective-permute-start.17) | collective-permute-done | bytes 262176 | tf_op jit(solution)/shard_map/ppermute | solution.py:55
  98.1 1.6 %collective-permute-start.11 = (bf16[64,4096]{1,0:T(8,128)(2,1)S(1)}, bf16[64,4096]{1,0:T(8,128)(2,1)S(1)}, u32[]{:S(2)}, u32[]{:S(2)}) collective-permute-start(bf16[64,4096]{1,0:T(8,128)(2,1)S(1)} %slice.49), channel_id=1, source_target_pairs={{0,4},{1,3},{2,6},{3,1},{4,0},{5,7},{6,2},{7,5},{8,12},{9,11},{10,... | collective-permute-start | bytes 1572872 | tf_op jit(solution)/shard_map/ppermute | solution.py:28
  100.6 6.8 %collective-permute-done.11 = bf16[64,4096]{1,0:T(8,128)(2,1)S(1)} collective-permute-done((bf16[64,4096]{1,0:T(8,128)(2,1)S(1)}, bf16[64,4096]{1,0:T(8,128)(2,1)S(1)}, u32[]{:S(2)}, u32[]{:S(2)}) %collective-permute-start.11) | collective-permute-done | bytes 524320 | tf_op jit(solution)/shard_map/ppermute | solution.py:28
  107.5 1.6 %collective-permute-start.12 = (bf16[32,4096]{1,0:T(8,128)(2,1)S(1)}, bf16[32,4096]{1,0:T(8,128)(2,1)S(1)}, u32[]{:S(2)}, u32[]{:S(2)}) collective-permute-start(bf16[32,4096]{1,0:T(8,128)(2,1)S(1)} %add_convert_fusion.6), channel_id=1, source_target_pairs={{0,2},{1,5},{2,0},{3,7},{4,6},{5,1},{6,4},{7,3},{8,10},{9,13},{10,... | collective-permute-start | bytes 786440 | tf_op jit(solution)/shard_map/ppermute | solution.py:28
  109.0 6.8 %collective-permute-done.14 = bf16[64,4096]{1,0:T(8,128)(2,1)S(1)} collective-permute-done((bf16[64,4096]{1,0:T(8,128)(2,1)S(1)}, bf16[64,4096]{1,0:T(8,128)(2,1)S(1)}, u32[]{:S(2)}, u32[]{:S(2)}) %collective-permute-start.14) | collective-permute-done | bytes 524320 | tf_op jit(solution)/shard_map/ppermute | solution.py:28
  115.9 1.6 %collective-permute-start.15 = (bf16[32,4096]{1,0:T(8,128)(2,1)S(1)}, bf16[32,4096]{1,0:T(8,128)(2,1)S(1)}, u32[]{:S(2)}, u32[]{:S(2)}) collective-permute-start(bf16[32,4096]{1,0:T(8,128)(2,1)S(1)} %add_convert_fusion.4), channel_id=1, source_target_pairs={{0,2},{1,5},{2,0},{3,7},{4,6},{5,1},{6,4},{7,3},{8,10},{9,13},{10,... | collective-permute-start | bytes 786440 | tf_op jit(solution)/shard_map/ppermute | solution.py:28
  117.6 4.8 %collective-permute-done.15 = bf16[32,4096]{1,0:T(8,128)(2,1)S(1)} collective-permute-done((bf16[32,4096]{1,0:T(8,128)(2,1)S(1)}, bf16[32,4096]{1,0:T(8,128)(2,1)S(1)}, u32[]{:S(2)}, u32[]{:S(2)}) %collective-permute-start.15) | collective-permute-done | bytes 262176 | tf_op jit(solution)/shard_map/ppermute | solution.py:28
  (45 shorter events, 7.7 us)
Async XLA Ops:
  1.7 7.4 %collective-permute-start.4 = (bf16[32,4096]{1,0:T(8,128)(2,1)S(1)}, bf16[32,4096]{1,0:T(8,128)(2,1)S(1)}, u32[]{:S(2)}, u32[]{:S(2)}) collective-permute-start(bf16[32,4096]{1,0:T(8,128)(2,1)S(1)} %get-tuple-element.35), channel_id=1, source_target_pairs={{0,2},{1,5},{2,0},{3,7},{4,6},{5,1},{6,4},{7,3},{8,10},{9,13},{10,... | collective-permute-start | bytes 786440 | tf_op jit(solution)/shard_map/ppermute | solution.py:28
  4.7 7.9 %collective-permute-start = (bf16[32,4096]{1,0:T(8,128)(2,1)S(1)}, bf16[32,4096]{1,0:T(8,128)(2,1)S(1)}, u32[]{:S(2)}, u32[]{:S(2)}) collective-permute-start(bf16[32,4096]{1,0:T(8,128)(2,1)S(1)} %get-tuple-element.36), channel_id=1, source_target_pairs={{0,2},{1,5},{2,0},{3,7},{4,6},{5,1},{6,4},{7,3},{8,10},{9,13},{10,... | collective-permute-start | bytes 786440 | tf_op jit(solution)/shard_map/ppermute | solution.py:28
  9.1 9.3 %collective-permute-start.5 = (bf16[64,4096]{1,0:T(8,128)(2,1)S(1)}, bf16[64,4096]{1,0:T(8,128)(2,1)S(1)}, u32[]{:S(2)}, u32[]{:S(2)}) collective-permute-start(bf16[64,4096]{1,0:T(8,128)(2,1)S(1)} %pad_maximum_fusion.1.refs_0_), channel_id=1, source_target_pairs={{0,4},{1,3},{2,6},{3,1},{4,0},{5,7},{6,2},{7,5},{8,12},{9,11},{10,... | collective-permute-start | bytes 1572872 | tf_op jit(solution)/shard_map/ppermute | solution.py:28
  12.7 23.1 %copy-start.1 = (bf16[256,1024]{1,0:T(8,128)(2,1)S(1)}, bf16[256,1024]{1,0:T(8,128)(2,1)}, u32[]{:S(2)}) copy-start(bf16[256,1024]{1,0:T(8,128)(2,1)} %grad_ref.1) | copy-start | bytes 1572868
  12.7 11.3 %collective-permute-start.1 = (bf16[64,4096]{1,0:T(8,128)(2,1)S(1)}, bf16[64,4096]{1,0:T(8,128)(2,1)S(1)}, u32[]{:S(2)}, u32[]{:S(2)}) collective-permute-start(bf16[64,4096]{1,0:T(8,128)(2,1)S(1)} %pad_maximum_fusion.refs_0_), channel_id=1, source_target_pairs={{0,4},{1,3},{2,6},{3,1},{4,0},{5,7},{6,2},{7,5},{8,12},{9,11},{10,... | collective-permute-start | bytes 1572872 | tf_op jit(solution)/shard_map/ppermute | solution.py:28
  15.1 8.9 %collective-permute-start.6 = (bf16[64,4096]{1,0:T(8,128)(2,1)S(1)}, bf16[64,4096]{1,0:T(8,128)(2,1)S(1)}, u32[]{:S(2)}, u32[]{:S(2)}) collective-permute-start(bf16[64,4096]{1,0:T(8,128)(2,1)S(1)} %pad_maximum_fusion.1.refs_0_), channel_id=1, source_target_pairs={{0,1},{1,0},{2,3},{3,2},{4,5},{5,4},{6,7},{7,6},{8,9},{9,8},{10,11... | collective-permute-start | bytes 1572872 | tf_op jit(solution)/shard_map/ppermute | solution.py:28
  18.4 5.6 %collective-permute-start.7 = (bf16[64,4096]{1,0:T(8,128)(2,1)S(1)}, bf16[64,4096]{1,0:T(8,128)(2,1)S(1)}, u32[]{:S(2)}, u32[]{:S(2)}) collective-permute-start(bf16[64,4096]{1,0:T(8,128)(2,1)S(1)} %collective-permute-done.5.refs_1_), channel_id=1, source_target_pairs={{0,1},{1,0},{2,3},{3,2},{4,5},{5,4},{6,7},{7,6},{8,9},{9,8},{10,11... | collective-permute-start | bytes 1572872 | tf_op jit(solution)/shard_map/ppermute | solution.py:28
  18.4 17.3 %collective-permute-start.2 = (bf16[64,4096]{1,0:T(8,128)(2,1)S(1)}, bf16[64,4096]{1,0:T(8,128)(2,1)S(1)}, u32[]{:S(2)}, u32[]{:S(2)}) collective-permute-start(bf16[64,4096]{1,0:T(8,128)(2,1)S(1)} %pad_maximum_fusion.refs_0_), channel_id=1, source_target_pairs={{0,1},{1,0},{2,3},{3,2},{4,5},{5,4},{6,7},{7,6},{8,9},{9,8},{10,11... | collective-permute-start | bytes 1572872 | tf_op jit(solution)/shard_map/ppermute | solution.py:28
  24.0 11.7 %collective-permute-start.3 = (bf16[64,4096]{1,0:T(8,128)(2,1)S(1)}, bf16[64,4096]{1,0:T(8,128)(2,1)S(1)}, u32[]{:S(2)}, u32[]{:S(2)}) collective-permute-start(bf16[64,4096]{1,0:T(8,128)(2,1)S(1)} %collective-permute-done.1.refs_1_), channel_id=1, source_target_pairs={{0,1},{1,0},{2,3},{3,2},{4,5},{5,4},{6,7},{7,6},{8,9},{9,8},{10,11... | collective-permute-start | bytes 1572872 | tf_op jit(solution)/shard_map/ppermute | solution.py:28
  35.7 27.0 %copy-start.2 = (f32[128,1024]{1,0:T(8,128)S(1)}, f32[128,1024]{1,0:T(8,128)}, u32[]{:S(2)}) copy-start(f32[128,1024]{1,0:T(8,128)} %taps_ref.1) | copy-start | bytes 1572868
  35.7 27.0 %copy-start.3 = (bf16[640,384]{1,0:T(8,128)(2,1)S(1)}, bf16[640,384]{1,0:T(8,128)(2,1)}, u32[]{:S(2)}) copy-start(bf16[640,384]{1,0:T(8,128)(2,1)} %constant.11.clone.bl_ref) | copy-start | bytes 1474564
  35.7 27.0 %copy-start.4 = (bf16[640,384]{1,0:T(8,128)(2,1)S(1)}, bf16[640,384]{1,0:T(8,128)(2,1)}, u32[]{:S(2)}) copy-start(bf16[640,384]{1,0:T(8,128)(2,1)} %constant.10.clone.bh_ref) | copy-start | bytes 1474564
  35.7 27.0 %copy-start.5 = (bf16[384,384]{1,0:T(8,128)(2,1)S(1)}, bf16[384,384]{1,0:T(8,128)(2,1)}, u32[]{:S(2)}) copy-start(bf16[384,384]{1,0:T(8,128)(2,1)} %constant.9.clone.tl_ref) | copy-start | bytes 884740
  35.7 27.0 %copy-start.6 = (bf16[384,384]{1,0:T(8,128)(2,1)S(1)}, bf16[384,384]{1,0:T(8,128)(2,1)}, u32[]{:S(2)}) copy-start(bf16[384,384]{1,0:T(8,128)(2,1)} %constant.8.clone.th_ref) | copy-start | bytes 884740
  48.4 10.2 %collective-permute-start.8 = (bf16[128,1024]{1,0:T(8,128)(2,1)S(1)}, bf16[128,1024]{1,0:T(8,128)(2,1)S(1)}, u32[]{:S(2)}, u32[]{:S(2)}) collective-permute-start(bf16[128,1024]{1,0:T(8,128)(2,1)S(1)} %get-tuple-element.24), channel_id=1, source_target_pairs={{0,8},{8,16},{16,24},{1,9},{9,17},{17,25},{2,10},{10,18},{18,26},{... | collective-permute-start | bytes 786440 | tf_op jit(solution)/shard_map/ppermute | solution.py:23
  52.4 10.3 %collective-permute-start.9 = (bf16[128,1024]{1,0:T(8,128)(2,1)S(1)}, bf16[128,1024]{1,0:T(8,128)(2,1)S(1)}, u32[]{:S(2)}, u32[]{:S(2)}) collective-permute-start(bf16[128,1024]{1,0:T(8,128)(2,1)S(1)} %get-tuple-element.25), channel_id=1, source_target_pairs={{8,0},{16,8},{24,16},{9,1},{17,9},{25,17},{10,2},{18,10},{26,18},{... | collective-permute-start | bytes 786440 | tf_op jit(solution)/shard_map/ppermute | solution.py:23
  70.0 11.8 %collective-permute-start.16 = (bf16[128,1024]{1,0:T(8,128)(2,1)S(1)}, bf16[128,1024]{1,0:T(8,128)(2,1)S(1)}, u32[]{:S(2)}, u32[]{:S(2)}) collective-permute-start(bf16[128,1024]{1,0:T(8,128)(2,1)S(1)} %get-tuple-element.34), channel_id=1, source_target_pairs={{0,8},{8,0},{16,24},{24,16},{1,9},{9,1},{17,25},{25,17},{2,10},{10... | collective-permute-start | bytes 786440 | tf_op jit(solution)/shard_map/ppermute | solution.py:55
  81.7 16.2 %collective-permute-start.10 = (bf16[128,4096]{1,0:T(8,128)(2,1)S(1)}, bf16[128,4096]{1,0:T(8,128)(2,1)S(1)}, u32[]{:S(2)}, u32[]{:S(2)}) collective-permute-start(bf16[128,4096]{1,0:T(8,128)(2,1)S(1)} %get-tuple-element.31), channel_id=1, source_target_pairs={{0,1},{1,0},{2,3},{3,2},{4,5},{5,4},{6,7},{7,6},{8,9},{9,8},{10,11... | collective-permute-start | bytes 3145736 | tf_op jit(solution)/shard_map/ppermute | solution.py:28
  81.8 15.2 %collective-permute-start.17 = (bf16[128,1024]{1,0:T(8,128)(2,1)S(1)}, bf16[128,1024]{1,0:T(8,128)(2,1)S(1)}, u32[]{:S(2)}, u32[]{:S(2)}) collective-permute-start(bf16[128,1024]{1,0:T(8,128)(2,1)S(1)} %add_convert_fusion.2), channel_id=1, source_target_pairs={{0,16},{8,24},{16,0},{24,8},{1,17},{9,25},{17,1},{25,9},{2,18},{10... | collective-permute-start | bytes 786440 | tf_op jit(solution)/shard_map/ppermute | solution.py:55
  93.0 6.7 %collective-permute-start.13 = (bf16[128,4096]{1,0:T(8,128)(2,1)S(1)}, bf16[128,4096]{1,0:T(8,128)(2,1)S(1)}, u32[]{:S(2)}, u32[]{:S(2)}) collective-permute-start(bf16[128,4096]{1,0:T(8,128)(2,1)S(1)} %get-tuple-element.33), channel_id=1, source_target_pairs={{0,1},{1,0},{2,3},{3,2},{4,5},{5,4},{6,7},{7,6},{8,9},{9,8},{10,11... | collective-permute-start | bytes 3145736 | tf_op jit(solution)/shard_map/ppermute | solution.py:28
  98.1 9.2 %collective-permute-start.11 = (bf16[64,4096]{1,0:T(8,128)(2,1)S(1)}, bf16[64,4096]{1,0:T(8,128)(2,1)S(1)}, u32[]{:S(2)}, u32[]{:S(2)}) collective-permute-start(bf16[64,4096]{1,0:T(8,128)(2,1)S(1)} %slice.49), channel_id=1, source_target_pairs={{0,4},{1,3},{2,6},{3,1},{4,0},{5,7},{6,2},{7,5},{8,12},{9,11},{10,... | collective-permute-start | bytes 1572872 | tf_op jit(solution)/shard_map/ppermute | solution.py:28
  100.0 15.8 %collective-permute-start.14 = (bf16[64,4096]{1,0:T(8,128)(2,1)S(1)}, bf16[64,4096]{1,0:T(8,128)(2,1)S(1)}, u32[]{:S(2)}, u32[]{:S(2)}) collective-permute-start(bf16[64,4096]{1,0:T(8,128)(2,1)S(1)} %slice.54), channel_id=1, source_target_pairs={{0,4},{1,3},{2,6},{3,1},{4,0},{5,7},{6,2},{7,5},{8,12},{9,11},{10,... | collective-permute-start | bytes 1572872 | tf_op jit(solution)/shard_map/ppermute | solution.py:28
  107.5 10.0 %collective-permute-start.12 = (bf16[32,4096]{1,0:T(8,128)(2,1)S(1)}, bf16[32,4096]{1,0:T(8,128)(2,1)S(1)}, u32[]{:S(2)}, u32[]{:S(2)}) collective-permute-start(bf16[32,4096]{1,0:T(8,128)(2,1)S(1)} %add_convert_fusion.6), channel_id=1, source_target_pairs={{0,2},{1,5},{2,0},{3,7},{4,6},{5,1},{6,4},{7,3},{8,10},{9,13},{10,... | collective-permute-start | bytes 786440 | tf_op jit(solution)/shard_map/ppermute | solution.py:28
  115.9 6.4 %collective-permute-start.15 = (bf16[32,4096]{1,0:T(8,128)(2,1)S(1)}, bf16[32,4096]{1,0:T(8,128)(2,1)S(1)}, u32[]{:S(2)}, u32[]{:S(2)}) collective-permute-start(bf16[32,4096]{1,0:T(8,128)(2,1)S(1)} %add_convert_fusion.4), channel_id=1, source_target_pairs={{0,2},{1,5},{2,0},{3,7},{4,6},{5,1},{6,4},{7,3},{8,10},{9,13},{10,... | collective-permute-start | bytes 786440 | tf_op jit(solution)/shard_map/ppermute | solution.py:28
  (1 other events, 1.6 us)

commit v3 on v0

v3 whole, which is shorter than its diff:
```python
import math

import jax
import jax.numpy as jnp
import numpy as np
from jax import lax
from jax.experimental import pallas as pl
from jax.experimental.pallas import tpu as pltpu
from jax.sharding import PartitionSpec as P

F32 = jnp.float32
BF16 = jnp.bfloat16
FWD_VMEM = 42 * 2**20
BWD_VMEM = 42 * 2**20
MID_VMEM = 24 * 2**20
SLOTS = 3
FWD_PARTS = (4, 4)
BWD_PARTS = (4, 2, 2)
EXACT = True


def bounds(width, parts):
    edges = np.cumsum((0,) + parts) * width // sum(parts)
    return [(int(a), int(b)) for a, b in zip(edges[:-1], edges[1:])]


def from_behind(block, axis, distance):
    devices = range(lax.axis_size(axis))
    route = [(i - distance, i) for i in devices if i - distance in devices]
    return lax.ppermute(block, axis, route)


def swap(block, way):
    offsets = {0: (1, 1), 1: (2, 4), 2: (4, 2)}[way]
    return lax.ppermute(block, "tp", [(i, i ^ offsets[i % 2]) for i in range(8)])


def row_order(tp, paired):
    if not paired:
        return list(range(tp))
    me = lax.axis_index("tp")
    first = 2 + 2 * (me % 2)
    second = 6 - first
    own = [me, me ^ first, me ^ second, me ^ 6]
    other = me ^ 1
    return own + [other, other ^ second, other ^ first, other ^ 6]


def block_rows(index, own):
    start = index * own
    return pl.ds(start if isinstance(start, int) else pl.multiple_of(start, own), own)


def gather_rows(block, chunks, paired):
    if not paired:
        return [[lax.all_gather(block[:, a:b], "tp", axis=0, tiled=True)] for a, b in chunks]
    first = swap(block, 1)
    pieces = []
    for a, b in chunks:
        near = jnp.concatenate([block[:, a:b], first[:, a:b]], axis=0)
        far = swap(near, 2)
        pieces.append([near, far, swap(near, 0), swap(far, 0)])
    return pieces


def scatter_rows(pieces, totals, own):
    far, first, count = [], [], len(pieces)
    for i in range(count + 1):
        if i < count:
            if i >= len(totals):
                keep, give = pieces[i]
                theirs = swap(give, 0)
                totals.append(add_up(keep, once(theirs, first[-1]) if first else theirs))
            far.append(swap(totals[i][2 * own :], 2))
        if i > 0:
            there = once(far[i - 1], totals[i]) if i < count else far[i - 1]
            first.append(add_up(totals[i - 1][own : 2 * own], there[own:]))
    near = [swap(f, 1) for f in first]
    return [add_up(t[:own], f[:own], n) for t, f, n in zip(totals, far, near)], first[-1]


def once(value, *others):
    return lax.optimization_barrier((value, others))[0]


def add_up(*terms):
    return sum(t.astype(F32) for t in terms).astype(BF16)


def add_pair(total, axis, distance, *others):
    route = [(i, i ^ distance) for i in range(lax.axis_size(axis))]
    mine = total.astype(BF16)
    theirs = lax.ppermute(mine, axis, route)
    return mine.astype(F32) + (once(theirs, *others) if others else theirs).astype(F32)


def step_rows(depth, count):
    step = 512 if count > 1 else 1024
    while depth % step:
        step //= 2
    return step


def stream_weights(w_refs, w_buf, w_sem, start, step, steps, compute):
    count = len(w_refs)

    def copy(k, m):
        slot = lax.rem(k, SLOTS)
        rows = pl.ds(start + k * step, step)
        return pltpu.make_async_copy(w_refs[m].at[rows, :], w_buf.at[slot, m], w_sem.at[slot, m])

    for k in range(min(SLOTS - 1, steps)):
        for m in range(count):
            copy(k, m).start()

    def body(k, carry):
        @pl.when(k + SLOTS - 1 < steps)
        def _():
            for m in range(count):
                copy(k + SLOTS - 1, m).start()

        for m in range(count):
            copy(k, m).wait()
        compute(k, lax.rem(k, SLOTS))
        return carry

    return lambda: lax.fori_loop(0, steps, body, 0)


def weight_scratch(count, step, group):
    return [pltpu.VMEM((SLOTS, count, step, group), BF16), pltpu.SemaphoreType.DMA((SLOTS, count))]


def matmul_cost(rows, depth, group, count):
    return pl.CostEstimate(
        flops=2 * count * rows * depth * group, bytes_accessed=2 * count * depth * group, transcendentals=0
    )


VMEM = pl.BlockSpec(memory_space=pltpu.VMEM)
ANYWHERE = pl.BlockSpec(memory_space=pl.ANY)


def project(pieces, weights, chunk, acc, tp, paired, out_grad, taps, finish):
    rows = sum(p.shape[0] for p in pieces)
    count = len(weights)
    group = weights[0].shape[1]
    start, depth = chunk[0], chunk[1] - chunk[0]
    step = step_rows(depth, count)
    own = rows // tp
    n_x = len(pieces)
    has_acc = acc is not None
    pair = count == 2

    def kernel(*refs):
        x_refs, w_refs, refs = refs[:n_x], refs[n_x : n_x + count], refs[n_x + count :]
        if has_acc:
            acc_refs, refs = refs[:count], refs[count:]
        if finish:
            if not pair:
                grad_ref, refs = refs[0], refs[1:]
            outs, made_ref, edge_ref, totals = refs[:count], refs[count], refs[count + 1], refs[count + 2 : 2 * count + 2]
        else:
            totals = refs[:count]
        x_buf, w_buf, w_sem = refs[-3:]

        def compute(k, slot):
            x = x_buf[:, pl.ds(pl.multiple_of(k * step, step), step)]
            for m in range(count):
                totals[m][...] += jnp.dot(x, w_buf[slot, m], preferred_element_type=F32)

        run = stream_weights(w_refs, w_buf, w_sem, start, step, depth // step, compute)
        at = 0
        for piece in x_refs:
            x_buf[at : at + piece.shape[0], :] = piece[...]
            at += piece.shape[0]
        for m in range(count):
            totals[m][...] = acc_refs[m][...] if has_acc else jnp.zeros_like(totals[m])
        run()
        if finish:
            for b, index in enumerate(row_order(tp, paired)):
                here = block_rows(index, own)
                part = [total[b * own : (b + 1) * own, :].astype(BF16) for total in totals]
                for out, value in zip(outs, part):
                    out[here, :] = value
                other = part[1] if pair else grad_ref[here, :]
                made_ref[here, :] = (part[0].astype(F32) * other.astype(F32)).astype(BF16)
            edge_ref[...] = made_ref[rows - taps :, :] if pair else made_ref[:taps, :]

    in_specs = [VMEM] * n_x + [ANYWHERE] * count
    args = [*pieces, *weights]
    if has_acc:
        in_specs += [VMEM] * count
        args += acc
    totals = (rows, group)
    scratch = [pltpu.VMEM((rows, depth), BF16), *weight_scratch(count, step, group)]
    full = jax.ShapeDtypeStruct((rows, group), BF16)
    if finish:
        if not pair:
            in_specs.append(VMEM)
            args.append(out_grad)
        out_shape = [full] * (count + 1) + [jax.ShapeDtypeStruct((taps, group), BF16)]
        scratch = [pltpu.VMEM(totals, F32)] * count + scratch
    else:
        out_shape = [jax.ShapeDtypeStruct(totals, F32)] * count
    return pl.pallas_call(
        kernel,
        in_specs=in_specs,
        out_specs=[VMEM] * len(out_shape),
        out_shape=out_shape,
        scratch_shapes=scratch,
        compiler_params=pltpu.CompilerParams(vmem_limit_bytes=FWD_VMEM),
        cost_estimate=matmul_cost(rows, depth, group, count),
        name="project",
    )(*args)


LANES = 128


def constant(matrix):
    stacked = np.concatenate(np.split(matrix, matrix.shape[1] // LANES, axis=1), axis=0)
    high = stacked.astype(jnp.bfloat16)
    low = (stacked - high.astype(np.float64)).astype(jnp.bfloat16)
    return jnp.asarray(high), jnp.asarray(low)


def transforms(length, taps):
    size = length + taps
    angle = 2 * np.pi / size * np.outer(np.arange(size // 2) + 0.5, np.arange(size))
    there = np.concatenate([np.cos(angle), -np.sin(angle)], axis=0)
    back = there.T * (2.0 / size)
    lags = back[np.arange(taps, 0, -1)]
    return [*constant(there), *constant(np.concatenate([back[taps:], back[:length], lags], axis=0))]


def window_of(mats):
    return math.isqrt(mats[0].shape[0] * mats[0].shape[1])


def part_of(ref, size, rows, cols):
    height = ref.shape[0] // (size // LANES)
    blocks = range(cols[0] // LANES, cols[1] // LANES)
    return jnp.concatenate([ref[b * height + rows[0] : b * height + rows[1], :] for b in blocks], axis=1)


def dot_there(mats, x, start):
    size = window_of(mats)
    cols = (start, start + x.shape[0])
    y = jnp.dot(part_of(mats[0], size, (0, size), cols), x, preferred_element_type=F32)
    if EXACT:
        y = y + jnp.dot(part_of(mats[1], size, (0, size), cols), x, preferred_element_type=F32)
    return y


def dot_back(mats, rows, re, im):
    y = jnp.concatenate([re, im], axis=0)
    size = y.shape[0]
    high = y.astype(BF16)
    back = part_of(mats[2], size, rows, (0, size))
    out = jnp.dot(back, high, preferred_element_type=F32)
    if EXACT:
        low = (y - high.astype(F32)).astype(BF16)
        out = out + jnp.dot(back, low, preferred_element_type=F32)
        out = out + jnp.dot(part_of(mats[3], size, rows, (0, size)), high, preferred_element_type=F32)
    return out


def by_columns(kernel, mats, arrays, out_shape, scratch, flops, name):
    group = arrays[0].shape[1]
    width = min(256, group)

    def cols(a):
        return pl.BlockSpec((a.shape[0], width), lambda i: (0, i))

    def body(*refs):
        kernel(refs[: len(mats)], *refs[len(mats) :])

    return pl.pallas_call(
        body,
        grid=(group // width,),
        in_specs=[pl.BlockSpec(m.shape, lambda i: (0, 0)) for m in mats] + [cols(a) for a in arrays],
        out_specs=[cols(a) for a in out_shape],
        out_shape=out_shape,
        scratch_shapes=[pltpu.VMEM((rows, width), BF16) for rows in scratch],
        compiler_params=pltpu.CompilerParams(vmem_limit_bytes=MID_VMEM),
        cost_estimate=pl.CostEstimate(
            flops=int(flops * group),
            bytes_accessed=sum(a.size * a.dtype.itemsize for a in [*arrays, *out_shape]),
            transcendentals=0,
        ),
        name=name,
    )(*mats, *arrays)


def transform_taps(filter_taps, mats):
    taps, group = filter_taps.shape
    size = window_of(mats)

    def kernel(mat_refs, taps_ref, out_ref):
        f = taps_ref[...]
        high = f.astype(BF16)
        out = dot_there(mat_refs, high, 0)
        if EXACT:
            low = (f - high.astype(F32)).astype(BF16)
            out = out + jnp.dot(part_of(mat_refs[0], size, (0, size), (0, taps)), low, preferred_element_type=F32)
        out_ref[...] = out

    out = [jax.ShapeDtypeStruct((size, group), F32)]
    return by_columns(kernel, mats[:2], [filter_taps], out, [], 6 * size * taps, "taps")[0]


def transform_rows(product, conv_in_grad, mats, taps):
    length, group = product.shape
    size = window_of(mats)

    def kernel(mat_refs, p_ref, c_ref, p_out, c_out):
        p_out[...] = dot_there(mat_refs, p_ref[...], taps)
        c_out[...] = dot_there(mat_refs, c_ref[...], 0)

    out = [jax.ShapeDtypeStruct((size, group), F32)] * 2
    return by_columns(kernel, mats[:2], [product, conv_in_grad], out, [], 8 * size * length, "transform")


def in_row_order(out_ref, scratch, own, tp, paired):
    for b, index in enumerate(row_order(tp, paired)):
        out_ref[b * own : (b + 1) * own, :] = scratch[block_rows(index, own), :]


def filter_forward(spectra, before, query, out_grad, mats, tp, paired):
    length, group = query.shape
    taps = before.shape[0]
    half = (length + taps) // 2

    def kernel(mat_refs, p_ref, c_ref, h_ref, before_ref, q_ref, grad_ref, mixed_ref, qg_ref, fg_ref, sq):
        p = p_ref[...] + dot_there(mat_refs, before_ref[...], 0)
        pr, pi, hr, hi = p[:half], p[half:], h_ref[:half, :], h_ref[half:, :]
        conv = dot_back(mat_refs, (0, length), pr * hr - pi * hi, pr * hi + pi * hr)
        mixed_ref[...] = (q_ref[...].astype(F32) * conv).astype(BF16)
        sq[...] = (grad_ref[...].astype(F32) * conv).astype(BF16)
        in_row_order(qg_ref, sq, length // tp, tp, paired)
        cr, ci = c_ref[:half, :], c_ref[half:, :]
        lags = (2 * length, 2 * length + taps)
        fg_ref[...] = dot_back(mat_refs, lags, cr * pr + ci * pi, cr * pi - ci * pr).astype(BF16)

    full = jax.ShapeDtypeStruct((length, group), BF16)
    out = [full, full, jax.ShapeDtypeStruct((taps, group), BF16)]
    flops = 2 * half * 2 * (2 * taps + 3 * (length + taps))
    return by_columns(kernel, mats, [*spectra, before, query, out_grad], out, [length], flops, "conv")


def filter_backward(spectra, after, keys, values, mats, tp, paired):
    length, group = keys.shape
    taps = after.shape[0]
    half = (length + taps) // 2

    def kernel(mat_refs, c_ref, h_ref, after_ref, k_ref, v_ref, kg_ref, vg_ref, sk, sv):
        g = c_ref[...] + dot_there(mat_refs, after_ref[...], length)
        gr, gi, hr, hi = g[:half], g[half:], h_ref[:half, :], h_ref[half:, :]
        product_grad = dot_back(mat_refs, (length, 2 * length), hr * gr + hi * gi, hr * gi - hi * gr)
        sk[...] = (product_grad * v_ref[...].astype(F32)).astype(BF16)
        sv[...] = (product_grad * k_ref[...].astype(F32)).astype(BF16)
        in_row_order(kg_ref, sk, length // tp, tp, paired)
        in_row_order(vg_ref, sv, length // tp, tp, paired)

    out = [jax.ShapeDtypeStruct((length, group), BF16)] * 2
    flops = 2 * half * 2 * (2 * taps + 3 * length)
    return by_columns(kernel, mats, [*spectra, after, keys, values], out, [length, length], flops, "conv_back")


def project_back(grads, weights, chunk, acc, parts):
    rows, group = grads[0].shape
    count = len(grads)
    start, depth = chunk[0], chunk[1] - chunk[0]
    step = step_rows(depth, count)
    n_out = max(parts, 1)
    share = rows // n_out
    has_acc = acc is not None

    def kernel(*refs):
        g_refs, w_refs, refs = refs[:count], refs[count : 2 * count], refs[2 * count :]
        if has_acc:
            acc_ref, refs = refs[0], refs[1:]
        out_refs, (w_buf, w_sem) = refs[:n_out], refs[n_out:]

        def compute(k, slot):
            at = pl.ds(pl.multiple_of(k * step, step), step)
            total = acc_ref[:, at] if has_acc else None
            for m in range(count):
                term = lax.dot_general(
                    g_refs[m][...], w_buf[slot, m], (((1,), (1,)), ((), ())), preferred_element_type=F32
                )
                total = term if total is None else total + term
            for i in range(n_out):
                out_refs[i][:, at] = total[i * share : (i + 1) * share].astype(out_refs[i].dtype)

        stream_weights(w_refs, w_buf, w_sem, start, step, depth // step, compute)()

    args = [*grads, *weights] + ([acc] if has_acc else [])
    return pl.pallas_call(
        kernel,
        in_specs=[VMEM] * count + [ANYWHERE] * count + [VMEM] * has_acc,
        out_specs=[VMEM] * n_out,
        out_shape=[jax.ShapeDtypeStruct((share, depth), BF16 if parts else F32)] * n_out,
        scratch_shapes=weight_scratch(count, step, group),
        compiler_params=pltpu.CompilerParams(vmem_limit_bytes=BWD_VMEM),
        cost_estimate=matmul_cost(rows, depth, group, count),
        name="project_back",
    )(*args)


def on_device(inputs, query_weight, key_weight, value_weight, filter_taps, out_grad):
    tp = lax.axis_size("tp")
    paired = tp == 8
    own_rows, width = inputs.shape
    taps = filter_taps.shape[0]
    mats = transforms(own_rows * tp, taps)
    h = transform_taps(filter_taps, mats)
    chunks = bounds(width, FWD_PARTS)
    gathered = gather_rows(inputs, chunks, paired)
    pair = (key_weight, value_weight)
    acc = [None] * 3
    for pieces, chunk in zip(gathered[:-1], chunks[:-1]):
        pieces[0] = once(pieces[0], h)
        acc = project(
            pieces, (query_weight, *pair), chunk, None if acc[0] is None else acc, tp, paired, None, taps, False
        )
    keys, values, product, tail = project(
        gathered[-1], pair, chunks[-1], acc[1:], tp, paired, None, taps, True
    )
    before = from_behind(tail, "ctx", 1)
    query, conv_in_grad, head = project(
        gathered[-1], (query_weight,), chunks[-1], [once(acc[0], product)], tp, paired, out_grad, taps, True
    )
    after = from_behind(head, "ctx", -1)
    p, c = transform_rows(product, conv_in_grad, mats, taps)
    mixed, query_grad, local_taps = filter_forward((p, c, h), before, query, out_grad, mats, tp, paired)
    chunks = bounds(width, BWD_PARTS)
    partial = project_back((query_grad,), (query_weight,), chunks[0], None, 0)[0]
    keys_grad, values_grad = filter_backward((c, h), once(after, partial), keys, values, mats, tp, paired)
    size = lax.axis_size("ctx")
    distances = [2**i for i in range(size.bit_length() - 1)] if size & (size - 1) == 0 else []
    pieces, totals = [], []
    for i, chunk in enumerate(chunks):
        if i == 0:
            pieces.append(project_back((keys_grad, values_grad), pair, chunk, partial, 2 if paired else 1))
            continue
        ready = [pieces[-1][0]]
        if len(distances) > 1:
            local_taps = add_pair(local_taps, "ctx", distances.pop(0))
            ready.append(local_taps)
        if paired and i > 1:
            totals.append(add_up(pieces[i - 2][0], swap(pieces[i - 2][1], 0)))
            ready.append(totals[-1])
        grads = (once(query_grad, *ready), keys_grad, values_grad)
        pieces.append(project_back(grads, (query_weight, *pair), chunk, None, 2 if paired else 1))
    if paired:
        summed, last = scatter_rows(pieces, totals, own_rows)
    else:
        summed = [lax.psum_scatter(p, "tp", scatter_dimension=0, tiled=True) for (p,) in pieces]
        last = summed[-1]
    if distances:
        for distance in distances:
            local_taps = add_pair(local_taps, "ctx", distance, last)
    else:
        local_taps = lax.psum(local_taps, "ctx").astype(F32)
    return mixed, jnp.concatenate(summed, axis=1), local_taps


def solution(mesh):
    in_specs = (
        P(("ctx", "tp"), None),
        P(None, "tp"),
        P(None, "tp"),
        P(None, "tp"),
        P(None, "tp"),
        P("ctx", "tp"),
    )
    out_specs = (P("ctx", "tp"), P(("ctx", "tp"), None), P(None, "tp"))
    return jax.shard_map(
        on_device, mesh=mesh, in_specs=in_specs, out_specs=out_specs, check_vma=False
    )
```

time: 276 us -> 118 us (0.43)
  matrix products: 99.5 us -> 0 us
  waiting for transfers between devices: 90.5 us -> 27.7 us
  Pallas kernels: 0 us -> 60.4 us
  other arithmetic: 44.3 us -> 2.66 us
  starting transfers between devices: 4.99 us -> 24.7 us
  local copies, waits for them, and re-layouts: 20.6 us -> 1.21 us
  between operations: 14.9 us -> 0.96 us
    dot_general x6 -> x0, matrix products: 99.5 us -> none  [the longest x3 44.5 us: contract(): lax.dot_general(left, right, (((1,), (1,)), ((), ())), preferred_element_...]
    pallas_call x0 -> x11, Pallas kernels: none -> 60.4 us  [the longest x4 24.8 us: project_back(): pl.pallas_call(kernel, in_specs=[VMEM] * count + [ANYWHERE] * count + [VM...]
    reduce_scatter x1 -> x0, waiting for transfers between devices: 51.8 us -> none  [on_device(): lax.psum_scatter((total + contract(values_rows, value_weight)).astype(jnp...]
    all_gather x1 -> x0, waiting for transfers between devices: 34.6 us -> none  [on_device(): piece = lax.all_gather(inputs, 'tp', axis=0, tiled=True)]
    ppermute x0 -> x18, waiting for transfers between devices: none -> 27.7 us  [the longest x16 25.6 us: swap(): lax.ppermute(block, 'tp', [(i, i ^ offsets[i % 2]) for i in range(8)])]
    add x1, other arithmetic: 24 us -> 0.86 us  [add_pair(): mine.astype(F32) + (once(theirs, *others) if others else theirs).astype(F32)]
    ppermute x0 -> x18, starting transfers between devices: none -> 19.2 us  [the longest x16 13.9 us: swap(): lax.ppermute(block, 'tp', [(i, i ^ offsets[i % 2]) for i in range(8)])]
    reduce_sum x8 -> x0, other arithmetic: 18.2 us -> none  [tap_products(): rows_out.append(jnp.sum(grad_rows * padded[start:start + length], axis=0))]
  transfers between devices with their start and end apart: 5 -> 20, of which waited for: 3 -> 9; matrix products, arithmetic and copies ran while one was open for 29% -> 2% of each run, Pallas kernels for 0% -> 34%
where the time goes in v3:
time: 118 us
  Pallas kernels  60.4 us (51%)
  waiting for transfers between devices  27.7 us (23%)
  starting transfers between devices  24.7 us (21%)
  other arithmetic  2.66 us (2%)
  local copies, waits for them, and re-layouts  1.21 us (1%)
    ppermute x16, waiting for transfers between devices, swap(): lax.ppermute(block, 'tp', [(i, i ^ offsets[i % 2]) for i in range(8)])  25.6 us
    pallas_call x4, Pallas kernels, project_back(): pl.pallas_call(kernel, in_specs=[VMEM] * count + [ANYWHERE] * count + [VM...  24.8 us
    pallas_call x3, Pallas kernels, project(): pl.pallas_call(kernel, in_specs=in_specs, out_specs=[VMEM] * len(out_shap...  23.2 us
    ppermute x16, starting transfers between devices, swap(): lax.ppermute(block, 'tp', [(i, i ^ offsets[i % 2]) for i in range(8)])  13.9 us
    pallas_call x4, Pallas kernels, by_columns(): pl.pallas_call(body, grid=(group // width,), in_specs=[pl.BlockSpec(m.sha...  12.3 us
    ppermute x2, starting transfers between devices, from_behind(): return lax.ppermute(block, axis, route)  5.42 us
    ppermute x2, starting transfers between devices, add_pair(): theirs = lax.ppermute(mine, axis, route)  5.32 us
  transfers between devices with their start and end apart: 20, of which 9 were waited for; matrix products, arithmetic and copies ran while one was open for 2% of the time, Pallas kernels for 34%

profile of v3, /device:TPU:0, one launch (start us, length us, event | category | flops | bytes accessed | tf_op | source)
XLA Modules:
  0.0 117.6 jit_solution(3356375358653269647)
XLA Ops:
  0.7 3.0 %collective-permute-start = (bf16[32,8192]{1,0:T(8,128)(2,1)}, bf16[32,8192]{1,0:T(8,128)(2,1)S(1)}, u32[]{:S(2)}, u32[]{:S(2)}) collective-permute-start(bf16[32,8192]{1,0:T(8,128)(2,1)} %param.10), channel_id=1, source_target_pairs={{0,2},{1,5},{2,0},{3,7},{4,6},{5,1},{6,4},{7,3},{8,10},{9,13},{10,... | collective-permute-start | bytes 1572872 | tf_op jit(solution)/shard_map/ppermute | solution.py:35
  4.7 6.3 %collective-permute-done = bf16[32,8192]{1,0:T(8,128)(2,1)S(1)} collective-permute-done((bf16[32,8192]{1,0:T(8,128)(2,1)}, bf16[32,8192]{1,0:T(8,128)(2,1)S(1)}, u32[]{:S(2)}, u32[]{:S(2)}) %collective-permute-start) | collective-permute-done | bytes 524320 | tf_op jit(solution)/shard_map/ppermute | solution.py:35
  11.1 2.1 %collective-permute-start.4 = (bf16[64,4096]{1,0:T(8,128)(2,1)S(1)}, bf16[64,4096]{1,0:T(8,128)(2,1)S(1)}, u32[]{:S(2)}, u32[]{:S(2)}) collective-permute-start(bf16[64,4096]{1,0:T(8,128)(2,1)S(1)} %pad_maximum_fusion.1.refs_0_), channel_id=1, source_target_pairs={{0,4},{1,3},{2,6},{3,1},{4,0},{5,7},{6,2},{7,5},{8,12},{9,11},{10,... | collective-permute-start | bytes 1572872 | tf_op jit(solution)/shard_map/ppermute | solution.py:35
  13.4 7.0 %collective-permute-done.4.refs_1_ = bf16[64,4096]{1,0:T(8,128)(2,1)S(1)} collective-permute-done((bf16[64,4096]{1,0:T(8,128)(2,1)S(1)}, bf16[64,4096]{1,0:T(8,128)(2,1)S(1)}, u32[]{:S(2)}, u32[]{:S(2)}) %collective-permute-start.4) | collective-permute-done | bytes 524320 | tf_op jit(solution)/shard_map/ppermute | solution.py:35
  22.3 3.7 %collective-permute-done.1.refs_1_ = bf16[64,4096]{1,0:T(8,128)(2,1)S(1)} collective-permute-done((bf16[64,4096]{1,0:T(8,128)(2,1)S(1)}, bf16[64,4096]{1,0:T(8,128)(2,1)S(1)}, u32[]{:S(2)}, u32[]{:S(2)}) %collective-permute-start.1) | collective-permute-done | bytes 524320 | tf_op jit(solution)/shard_map/ppermute | solution.py:35
  26.0 10.1 %project.3 = (f32[256,1024]{1,0:T(8,128)S(1)}, f32[256,1024]{1,0:T(8,128)S(1)}, f32[256,1024]{1,0:T(8,128)S(1)}) custom-call(bf16[64,4096]{1,0:T(8,128)(2,1)S(1)} %pad_maximum_fusion.1.refs_0_, bf16[64,4096]{1,0:T(8,128)(2,1)S(1)} %collective-permute-done.4.refs_1_, bf16[64,4096]{1,0:T(8,128)(2,1)S(1)} %collective-permute-done.5.refs_2_, ...), custom_call_target="tpu_custom_call" | custom-call | flops 6442450944 | bytes 25165824 | tf_op jit(solution)/shard_map/project/pallas_call | solution.py:206
  36.1 8.2 %project.4 = (bf16[256,1024]{1,0:T(8,128)(2,1)S(1)}, bf16[256,1024]{1,0:T(8,128)(2,1)S(1)}, bf16[256,1024]{1,0:T(8,128)(2,1)S(1)}, bf16[128,1024]{1,0:T(8,128)(2,1)S(1)}) custom-call(bf16[64,4096]{1,0:T(8,128)(2,1)S(1)} %pad_maximum_fusion.refs_0_, bf16[64,4096]{1,0:T(8,128)(2,1)S(1)} %collective-permute-done.1.refs_1_, ...), custom_call_target="tpu_custom_call" | custom-call | flops 4294967296 | bytes 16777216 | tf_op jit(solution)/shard_map/project/pallas_call | solution.py:206
  44.3 4.0 %collective-permute-start.7 = (bf16[128,1024]{1,0:T(8,128)(2,1)S(1)}, bf16[128,1024]{1,0:T(8,128)(2,1)S(1)}, u32[]{:S(2)}, u32[]{:S(2)}) collective-permute-start(bf16[128,1024]{1,0:T(8,128)(2,1)S(1)} %get-tuple-element.44), channel_id=1, source_target_pairs={{0,8},{8,16},{16,24},{1,9},{9,17},{17,25},{2,10},{10,18},{18,26},{... | collective-permute-start | bytes 786440 | tf_op jit(solution)/shard_map/ppermute | solution.py:30
  48.4 5.0 %project.5 = (bf16[256,1024]{1,0:T(8,128)(2,1)S(1)}, bf16[256,1024]{1,0:T(8,128)(2,1)S(1)}, bf16[128,1024]{1,0:T(8,128)(2,1)S(1)}) custom-call(bf16[64,4096]{1,0:T(8,128)(2,1)S(1)} %pad_maximum_fusion.refs_0_, bf16[64,4096]{1,0:T(8,128)(2,1)S(1)} %collective-permute-done.1.refs_1_, bf16[64,4096]{1,0:T(8,128)(2,1)S(1)} %collective-permute-done.2.refs_2_, ...), custom_call_target="tpu_custom_call" | custom-call | flops 2147483648 | bytes 8388608 | tf_op jit(solution)/shard_map/project/pallas_call | solution.py:206
  54.8 1.9 %transform.1 = (f32[384,1024]{1,0:T(8,128)S(1)}, f32[384,1024]{1,0:T(8,128)S(1)}) custom-call(bf16[1152,128]{1,0:T(8,128)(2,1)S(1)} %copy-done, bf16[1152,128]{1,0:T(8,128)(2,1)S(1)} %copy-done.1, bf16[256,1024]{1,0:T(8,128)(2,1)S(1)} %get-tuple-element.38.refs_2_, bf16[256,1024]{1,0:T(8,128)(2,1)S(1)} %get-tuple-element.41.refs_3_), custom_call_target="tpu_custom_call" | custom-call | flops 805306368 | bytes 4194304 | tf_op jit(solution)/shard_map/transform/pallas_call | solution.py:279
  56.7 5.2 %conv.1 = (bf16[256,1024]{1,0:T(8,128)(2,1)}, bf16[256,1024]{1,0:T(8,128)(2,1)S(1)}, bf16[128,1024]{1,0:T(8,128)(2,1)S(1)}) custom-call(bf16[1152,128]{1,0:T(8,128)(2,1)S(1)} %copy-done, bf16[1152,128]{1,0:T(8,128)(2,1)S(1)} %copy-done.1, bf16[1920,128]{1,0:T(8,128)(2,1)S(1)} %copy-done.3, bf16[1920,128]{1,0:T(8,128)(2,1)S(1)} %copy-done.4, ...), custom_call_target="tpu_custom_call" | custom-call | flops 1107296256 | bytes 7340032 | tf_op jit(solution)/shard_map/conv/pallas_call | solution.py:279
  61.9 4.8 %project_back.4.refs_4_ = f32[256,4096]{1,0:T(8,128)S(1)} custom-call(bf16[256,1024]{1,0:T(8,128)(2,1)S(1)} %get-tuple-element.61.refs_0_, bf16[8192,1024]{1,0:T(8,128)(2,1)} %refs_3_.7), custom_call_target="tpu_custom_call" | custom-call | flops 2147483648 | bytes 8388608 | tf_op jit(solution)/shard_map/project_back/pallas_call | solution.py:400
  66.8 3.9 %conv_back.1 = (bf16[256,1024]{1,0:T(8,128)(2,1)S(1)}, bf16[256,1024]{1,0:T(8,128)(2,1)S(1)}) custom-call(bf16[1152,128]{1,0:T(8,128)(2,1)S(1)} %copy-done, bf16[1152,128]{1,0:T(8,128)(2,1)S(1)} %copy-done.1, bf16[1920,128]{1,0:T(8,128)(2,1)S(1)} %copy-done.3, bf16[1920,128]{1,0:T(8,128)(2,1)S(1)} %copy-done.4, ...), custom_call_target="tpu_custom_call" | custom-call | flops 805306368 | bytes 5505024 | tf_op jit(solution)/shard_map/conv_back/pallas_call | solution.py:279
  70.7 8.0 %project_back.5 = (bf16[128,4096]{1,0:T(8,128)(2,1)S(1)}, bf16[128,4096]{1,0:T(8,128)(2,1)S(1)}) custom-call(bf16[256,1024]{1,0:T(8,128)(2,1)S(1)} %get-tuple-element.52.refs_0_.refs_1_, bf16[256,1024]{1,0:T(8,128)(2,1)S(1)} %get-tuple-element.53.refs_1_.refs_2_, bf16[8192,1024]{1,0:T(8,128)(2,1)} %refs_4_.9, bf16[8192,1024]{1,0:T(8,128)(2,1)} %refs_5_.7, ...), custom_call_target="tpu_custom_call" | custom-call | flops 4294967296 | bytes 16777216 | tf_op jit(solution)/shard_map/project_back/pallas_call | solution.py:400
  78.9 6.0 %project_back.6 = (bf16[128,2048]{1,0:T(8,128)(2,1)S(1)}, bf16[128,2048]{1,0:T(8,128)(2,1)S(1)}) custom-call(bf16[256,1024]{1,0:T(8,128)(2,1)S(1)} %get-tuple-element.61.refs_0_, bf16[256,1024]{1,0:T(8,128)(2,1)S(1)} %get-tuple-element.52.refs_0_.refs_1_, bf16[256,1024]{1,0:T(8,128)(2,1)S(1)} %get-tuple-element.53.refs_1_.refs_2_, ...), custom_call_target="tpu_custom_call" | custom-call | flops 3221225472 | bytes 12582912 | tf_op jit(solution)/shard_map/project_back/pallas_call | solution.py:400
  85.3 2.7 %collective-permute-start.11 = (bf16[128,1024]{1,0:T(8,128)(2,1)S(1)}, bf16[128,1024]{1,0:T(8,128)(2,1)S(1)}, u32[]{:S(2)}, u32[]{:S(2)}) collective-permute-start(bf16[128,1024]{1,0:T(8,128)(2,1)S(1)} %get-tuple-element.56), channel_id=1, source_target_pairs={{0,8},{8,0},{16,24},{24,16},{1,9},{9,1},{17,25},{25,17},{2,10},{10... | collective-permute-start | bytes 786440 | tf_op jit(solution)/shard_map/ppermute | solution.py:93
  88.3 1.6 %collective-permute-start.10 = (bf16[64,4096]{1,0:T(8,128)(2,1)S(1)}, bf16[64,4096]{1,0:T(8,128)(2,1)S(1)}, u32[]{:S(2)}, u32[]{:S(2)}) collective-permute-start(bf16[64,4096]{1,0:T(8,128)(2,1)S(1)} %slice.79), channel_id=1, source_target_pairs={{0,4},{1,3},{2,6},{3,1},{4,0},{5,7},{6,2},{7,5},{8,12},{9,11},{10,... | collective-permute-start | bytes 1572872 | tf_op jit(solution)/shard_map/ppermute | solution.py:35
  90.6 6.0 %project_back.7 = (bf16[128,2048]{1,0:T(8,128)(2,1)S(1)}, bf16[128,2048]{1,0:T(8,128)(2,1)S(1)}) custom-call(bf16[256,1024]{1,0:T(8,128)(2,1)S(1)} %get-tuple-element.61.refs_0_, bf16[256,1024]{1,0:T(8,128)(2,1)S(1)} %get-tuple-element.52.refs_0_.refs_1_, bf16[256,1024]{1,0:T(8,128)(2,1)S(1)} %get-tuple-element.53.refs_1_.refs_2_, ...), custom_call_target="tpu_custom_call" | custom-call | flops 3221225472 | bytes 12582912 | tf_op jit(solution)/shard_map/project_back/pallas_call | solution.py:400
  98.7 1.6 %collective-permute-done.14 = bf16[64,2048]{1,0:T(8,128)(2,1)S(1)} collective-permute-done((bf16[64,2048]{1,0:T(8,128)(2,1)S(1)}, bf16[64,2048]{1,0:T(8,128)(2,1)S(1)}, u32[]{:S(2)}, u32[]{:S(2)}) %collective-permute-start.14) | collective-permute-done | bytes 262176 | tf_op jit(solution)/shard_map/ppermute | solution.py:35
  100.4 1.6 %collective-permute-start.16 = (bf16[32,2048]{1,0:T(8,128)(2,1)S(1)}, bf16[32,2048]{1,0:T(8,128)(2,1)S(1)}, u32[]{:S(2)}, u32[]{:S(2)}) collective-permute-start(bf16[32,2048]{1,0:T(8,128)(2,1)S(1)} %add_convert_fusion.8), channel_id=1, source_target_pairs={{0,2},{1,5},{2,0},{3,7},{4,6},{5,1},{6,4},{7,3},{8,10},{9,13},{10,... | collective-permute-start | bytes 393224 | tf_op jit(solution)/shard_map/ppermute | solution.py:35
  102.0 2.7 %collective-permute-start.19 = (bf16[128,1024]{1,0:T(8,128)(2,1)S(1)}, bf16[128,1024]{1,0:T(8,128)(2,1)S(1)}, u32[]{:S(2)}, u32[]{:S(2)}) collective-permute-start(bf16[128,1024]{1,0:T(8,128)(2,1)S(1)} %fusion), channel_id=1, source_target_pairs={{0,16},{8,24},{16,0},{24,8},{1,17},{9,25},{17,1},{25,9},{2,18},{10... | collective-permute-start | bytes 786440 | tf_op jit(solution)/shard_map/ppermute | solution.py:93
  106.9 4.8 %collective-permute-done.17 = bf16[64,2048]{1,0:T(8,128)(2,1)S(1)} collective-permute-done((bf16[64,2048]{1,0:T(8,128)(2,1)S(1)}, bf16[64,2048]{1,0:T(8,128)(2,1)S(1)}, u32[]{:S(2)}, u32[]{:S(2)}) %collective-permute-start.17) | collective-permute-done | bytes 262176 | tf_op jit(solution)/shard_map/ppermute | solution.py:35
  111.7 1.6 %collective-permute-start.18 = (bf16[32,2048]{1,0:T(8,128)(2,1)S(1)}, bf16[32,2048]{1,0:T(8,128)(2,1)S(1)}, u32[]{:S(2)}, u32[]{:S(2)}) collective-permute-start(bf16[32,2048]{1,0:T(8,128)(2,1)S(1)} %add_convert_fusion.6), channel_id=1, source_target_pairs={{0,2},{1,5},{2,0},{3,7},{4,6},{5,1},{6,4},{7,3},{8,10},{9,13},{10,... | collective-permute-start | bytes 393224 | tf_op jit(solution)/shard_map/ppermute | solution.py:35
  113.2 2.1 %collective-permute-done.19 = bf16[128,1024]{1,0:T(8,128)(2,1)S(1)} collective-permute-done((bf16[128,1024]{1,0:T(8,128)(2,1)S(1)}, bf16[128,1024]{1,0:T(8,128)(2,1)S(1)}, u32[]{:S(2)}, u32[]{:S(2)}) %collective-permute-start.19) | collective-permute-done | bytes 262176 | tf_op jit(solution)/shard_map/ppermute | solution.py:93
  (58 shorter events, 13.1 us)
Async XLA Ops:
  0.6 19.8 %copy-start = (bf16[1152,128]{1,0:T(8,128)(2,1)S(1)}, bf16[1152,128]{1,0:T(8,128)(2,1)}, u32[]{:S(2)}) copy-start(bf16[1152,128]{1,0:T(8,128)(2,1)} %constant.8.clone.refs_0_) | copy-start | bytes 884740
  0.6 19.8 %copy-start.1 = (bf16[1152,128]{1,0:T(8,128)(2,1)S(1)}, bf16[1152,128]{1,0:T(8,128)(2,1)}, u32[]{:S(2)}) copy-start(bf16[1152,128]{1,0:T(8,128)(2,1)} %constant.9.clone.refs_1_) | copy-start | bytes 884740
  0.7 19.8 %copy-start.5 = (f32[128,1024]{1,0:T(8,128)S(1)}, f32[128,1024]{1,0:T(8,128)}, u32[]{:S(2)}) copy-start(f32[128,1024]{1,0:T(8,128)} %refs_2_.4) | copy-start | bytes 1572868
  0.7 10.4 %collective-permute-start = (bf16[32,8192]{1,0:T(8,128)(2,1)}, bf16[32,8192]{1,0:T(8,128)(2,1)S(1)}, u32[]{:S(2)}, u32[]{:S(2)}) collective-permute-start(bf16[32,8192]{1,0:T(8,128)(2,1)} %param.10), channel_id=1, source_target_pairs={{0,2},{1,5},{2,0},{3,7},{4,6},{5,1},{6,4},{7,3},{8,10},{9,13},{10,... | collective-permute-start | bytes 1572872 | tf_op jit(solution)/shard_map/ppermute | solution.py:35
  11.1 9.3 %collective-permute-start.4 = (bf16[64,4096]{1,0:T(8,128)(2,1)S(1)}, bf16[64,4096]{1,0:T(8,128)(2,1)S(1)}, u32[]{:S(2)}, u32[]{:S(2)}) collective-permute-start(bf16[64,4096]{1,0:T(8,128)(2,1)S(1)} %pad_maximum_fusion.1.refs_0_), channel_id=1, source_target_pairs={{0,4},{1,3},{2,6},{3,1},{4,0},{5,7},{6,2},{7,5},{8,12},{9,11},{10,... | collective-permute-start | bytes 1572872 | tf_op jit(solution)/shard_map/ppermute | solution.py:35
  13.3 12.7 %collective-permute-start.1 = (bf16[64,4096]{1,0:T(8,128)(2,1)S(1)}, bf16[64,4096]{1,0:T(8,128)(2,1)S(1)}, u32[]{:S(2)}, u32[]{:S(2)}) collective-permute-start(bf16[64,4096]{1,0:T(8,128)(2,1)S(1)} %pad_maximum_fusion.refs_0_), channel_id=1, source_target_pairs={{0,4},{1,3},{2,6},{3,1},{4,0},{5,7},{6,2},{7,5},{8,12},{9,11},{10,... | collective-permute-start | bytes 1572872 | tf_op jit(solution)/shard_map/ppermute | solution.py:35
  13.4 12.7 %collective-permute-start.5 = (bf16[64,4096]{1,0:T(8,128)(2,1)S(1)}, bf16[64,4096]{1,0:T(8,128)(2,1)S(1)}, u32[]{:S(2)}, u32[]{:S(2)}) collective-permute-start(bf16[64,4096]{1,0:T(8,128)(2,1)S(1)} %pad_maximum_fusion.1.refs_0_), channel_id=1, source_target_pairs={{0,1},{1,0},{2,3},{3,2},{4,5},{5,4},{6,7},{7,6},{8,9},{9,8},{10,11... | collective-permute-start | bytes 1572872 | tf_op jit(solution)/shard_map/ppermute | solution.py:35
  20.4 5.6 %collective-permute-start.6 = (bf16[64,4096]{1,0:T(8,128)(2,1)S(1)}, bf16[64,4096]{1,0:T(8,128)(2,1)S(1)}, u32[]{:S(2)}, u32[]{:S(2)}) collective-permute-start(bf16[64,4096]{1,0:T(8,128)(2,1)S(1)} %collective-permute-done.4.refs_1_), channel_id=1, source_target_pairs={{0,1},{1,0},{2,3},{3,2},{4,5},{5,4},{6,7},{7,6},{8,9},{9,8},{10,11... | collective-permute-start | bytes 1572872 | tf_op jit(solution)/shard_map/ppermute | solution.py:35
  21.8 14.3 %collective-permute-start.2 = (bf16[64,4096]{1,0:T(8,128)(2,1)S(1)}, bf16[64,4096]{1,0:T(8,128)(2,1)S(1)}, u32[]{:S(2)}, u32[]{:S(2)}) collective-permute-start(bf16[64,4096]{1,0:T(8,128)(2,1)S(1)} %pad_maximum_fusion.refs_0_), channel_id=1, source_target_pairs={{0,1},{1,0},{2,3},{3,2},{4,5},{5,4},{6,7},{7,6},{8,9},{9,8},{10,11... | collective-permute-start | bytes 1572872 | tf_op jit(solution)/shard_map/ppermute | solution.py:35
  26.0 10.1 %collective-permute-start.3 = (bf16[64,4096]{1,0:T(8,128)(2,1)S(1)}, bf16[64,4096]{1,0:T(8,128)(2,1)S(1)}, u32[]{:S(2)}, u32[]{:S(2)}) collective-permute-start(bf16[64,4096]{1,0:T(8,128)(2,1)S(1)} %collective-permute-done.1.refs_1_), channel_id=1, source_target_pairs={{0,1},{1,0},{2,3},{3,2},{4,5},{5,4},{6,7},{7,6},{8,9},{9,8},{10,11... | collective-permute-start | bytes 1572872 | tf_op jit(solution)/shard_map/ppermute | solution.py:35
  36.1 12.2 %copy-start.2 = (bf16[256,1024]{1,0:T(8,128)(2,1)S(1)}, bf16[256,1024]{1,0:T(8,128)(2,1)}, u32[]{:S(2)}) copy-start(bf16[256,1024]{1,0:T(8,128)(2,1)} %refs_9_.1) | copy-start | bytes 1572868
  44.3 12.4 %collective-permute-start.7 = (bf16[128,1024]{1,0:T(8,128)(2,1)S(1)}, bf16[128,1024]{1,0:T(8,128)(2,1)S(1)}, u32[]{:S(2)}, u32[]{:S(2)}) collective-permute-start(bf16[128,1024]{1,0:T(8,128)(2,1)S(1)} %get-tuple-element.44), channel_id=1, source_target_pairs={{0,8},{8,16},{16,24},{1,9},{9,17},{17,25},{2,10},{10,18},{18,26},{... | collective-permute-start | bytes 786440 | tf_op jit(solution)/shard_map/ppermute | solution.py:30
  53.4 13.4 %collective-permute-start.8 = (bf16[128,1024]{1,0:T(8,128)(2,1)S(1)}, bf16[128,1024]{1,0:T(8,128)(2,1)S(1)}, u32[]{:S(2)}, u32[]{:S(2)}) collective-permute-start(bf16[128,1024]{1,0:T(8,128)(2,1)S(1)} %get-tuple-element.47), channel_id=1, source_target_pairs={{8,0},{16,8},{24,16},{9,1},{17,9},{25,17},{10,2},{18,10},{26,18},{... | collective-permute-start | bytes 786440 | tf_op jit(solution)/shard_map/ppermute | solution.py:30
  78.6 9.3 %collective-permute-start.9 = (bf16[128,4096]{1,0:T(8,128)(2,1)S(1)}, bf16[128,4096]{1,0:T(8,128)(2,1)S(1)}, u32[]{:S(2)}, u32[]{:S(2)}) collective-permute-start(bf16[128,4096]{1,0:T(8,128)(2,1)S(1)} %get-tuple-element.55), channel_id=1, source_target_pairs={{0,1},{1,0},{2,3},{3,2},{4,5},{5,4},{6,7},{7,6},{8,9},{9,8},{10,11... | collective-permute-start | bytes 3145736 | tf_op jit(solution)/shard_map/ppermute | solution.py:35
  85.0 4.9 %collective-permute-start.12 = (bf16[128,2048]{1,0:T(8,128)(2,1)S(1)}, bf16[128,2048]{1,0:T(8,128)(2,1)S(1)}, u32[]{:S(2)}, u32[]{:S(2)}) collective-permute-start(bf16[128,2048]{1,0:T(8,128)(2,1)S(1)} %get-tuple-element.59), channel_id=1, source_target_pairs={{0,1},{1,0},{2,3},{3,2},{4,5},{5,4},{6,7},{7,6},{8,9},{9,8},{10,11... | collective-permute-start | bytes 1572872 | tf_op jit(solution)/shard_map/ppermute | solution.py:35
  85.3 16.6 %collective-permute-start.11 = (bf16[128,1024]{1,0:T(8,128)(2,1)S(1)}, bf16[128,1024]{1,0:T(8,128)(2,1)S(1)}, u32[]{:S(2)}, u32[]{:S(2)}) collective-permute-start(bf16[128,1024]{1,0:T(8,128)(2,1)S(1)} %get-tuple-element.56), channel_id=1, source_target_pairs={{0,8},{8,0},{16,24},{24,16},{1,9},{9,1},{17,25},{25,17},{2,10},{10... | collective-permute-start | bytes 786440 | tf_op jit(solution)/shard_map/ppermute | solution.py:93
  88.3 9.2 %collective-permute-start.10 = (bf16[64,4096]{1,0:T(8,128)(2,1)S(1)}, bf16[64,4096]{1,0:T(8,128)(2,1)S(1)}, u32[]{:S(2)}, u32[]{:S(2)}) collective-permute-start(bf16[64,4096]{1,0:T(8,128)(2,1)S(1)} %slice.79), channel_id=1, source_target_pairs={{0,4},{1,3},{2,6},{3,1},{4,0},{5,7},{6,2},{7,5},{8,12},{9,11},{10,... | collective-permute-start | bytes 1572872 | tf_op jit(solution)/shard_map/ppermute | solution.py:35
  90.0 10.3 %collective-permute-start.14 = (bf16[64,2048]{1,0:T(8,128)(2,1)S(1)}, bf16[64,2048]{1,0:T(8,128)(2,1)S(1)}, u32[]{:S(2)}, u32[]{:S(2)}) collective-permute-start(bf16[64,2048]{1,0:T(8,128)(2,1)S(1)} %slice.83), channel_id=1, source_target_pairs={{0,4},{1,3},{2,6},{3,1},{4,0},{5,7},{6,2},{7,5},{8,12},{9,11},{10,... | collective-permute-start | bytes 786440 | tf_op jit(solution)/shard_map/ppermute | solution.py:35
  96.6 2.0 %collective-permute-start.15 = (bf16[128,2048]{1,0:T(8,128)(2,1)S(1)}, bf16[128,2048]{1,0:T(8,128)(2,1)S(1)}, u32[]{:S(2)}, u32[]{:S(2)}) collective-permute-start(bf16[128,2048]{1,0:T(8,128)(2,1)S(1)} %get-tuple-element.63), channel_id=1, source_target_pairs={{0,1},{1,0},{2,3},{3,2},{4,5},{5,4},{6,7},{7,6},{8,9},{9,8},{10,11... | collective-permute-start | bytes 1572872 | tf_op jit(solution)/shard_map/ppermute | solution.py:35
  100.4 6.4 %collective-permute-start.16 = (bf16[32,2048]{1,0:T(8,128)(2,1)S(1)}, bf16[32,2048]{1,0:T(8,128)(2,1)S(1)}, u32[]{:S(2)}, u32[]{:S(2)}) collective-permute-start(bf16[32,2048]{1,0:T(8,128)(2,1)S(1)} %add_convert_fusion.8), channel_id=1, source_target_pairs={{0,2},{1,5},{2,0},{3,7},{4,6},{5,1},{6,4},{7,3},{8,10},{9,13},{10,... | collective-permute-start | bytes 393224 | tf_op jit(solution)/shard_map/ppermute | solution.py:35
  102.0 13.3 %collective-permute-start.19 = (bf16[128,1024]{1,0:T(8,128)(2,1)S(1)}, bf16[128,1024]{1,0:T(8,128)(2,1)S(1)}, u32[]{:S(2)}, u32[]{:S(2)}) collective-permute-start(bf16[128,1024]{1,0:T(8,128)(2,1)S(1)} %fusion), channel_id=1, source_target_pairs={{0,16},{8,24},{16,0},{24,8},{1,17},{9,25},{17,1},{25,9},{2,18},{10... | collective-permute-start | bytes 786440 | tf_op jit(solution)/shard_map/ppermute | solution.py:93
  104.7 10.6 %collective-permute-start.13 = (bf16[32,4096]{1,0:T(8,128)(2,1)S(1)}, bf16[32,4096]{1,0:T(8,128)(2,1)S(1)}, u32[]{:S(2)}, u32[]{:S(2)}) collective-permute-start(bf16[32,4096]{1,0:T(8,128)(2,1)S(1)} %add_convert_fusion.4), channel_id=1, source_target_pairs={{0,2},{1,5},{2,0},{3,7},{4,6},{5,1},{6,4},{7,3},{8,10},{9,13},{10,... | collective-permute-start | bytes 786440 | tf_op jit(solution)/shard_map/ppermute | solution.py:35
  105.3 6.4 %collective-permute-start.17 = (bf16[64,2048]{1,0:T(8,128)(2,1)S(1)}, bf16[64,2048]{1,0:T(8,128)(2,1)S(1)}, u32[]{:S(2)}, u32[]{:S(2)}) collective-permute-start(bf16[64,2048]{1,0:T(8,128)(2,1)S(1)} %slice.87), channel_id=1, source_target_pairs={{0,4},{1,3},{2,6},{3,1},{4,0},{5,7},{6,2},{7,5},{8,12},{9,11},{10,... | collective-permute-start | bytes 786440 | tf_op jit(solution)/shard_map/ppermute | solution.py:35
  111.7 5.0 %collective-permute-start.18 = (bf16[32,2048]{1,0:T(8,128)(2,1)S(1)}, bf16[32,2048]{1,0:T(8,128)(2,1)S(1)}, u32[]{:S(2)}, u32[]{:S(2)}) collective-permute-start(bf16[32,2048]{1,0:T(8,128)(2,1)S(1)} %add_convert_fusion.6), channel_id=1, source_target_pairs={{0,2},{1,5},{2,0},{3,7},{4,6},{5,1},{6,4},{7,3},{8,10},{9,13},{10,... | collective-permute-start | bytes 393224 | tf_op jit(solution)/shard_map/ppermute | solution.py:35
  (2 other events, 6.8 us)

commit v4 on v3

v4 whole, which is shorter than its diff:
```python
import math

import jax
import jax.numpy as jnp
import numpy as np
from jax import lax
from jax.experimental import pallas as pl
from jax.experimental.pallas import tpu as pltpu
from jax.sharding import PartitionSpec as P

F32 = jnp.float32
BF16 = jnp.bfloat16
FWD_VMEM = 42 * 2**20
BWD_VMEM = 42 * 2**20
MIX_VMEM = 35 * 2**20
MID_VMEM = 24 * 2**20
FWD_PARTS = (2, 6)
BWD_PARTS = (4, 3, 1)


def bounds(width, parts):
    edges = np.cumsum((0,) + parts) * width // sum(parts)
    return [(int(a), int(b)) for a, b in zip(edges[:-1], edges[1:])]


def from_behind(block, axis, distance):
    devices = range(lax.axis_size(axis))
    route = [(i - distance, i) for i in devices if i - distance in devices]
    return lax.ppermute(block, axis, route)


def swap(block, way):
    offsets = {0: (1, 1), 1: (2, 4), 2: (4, 2)}[way]
    return lax.ppermute(block, "tp", [(i, i ^ offsets[i % 2]) for i in range(8)])


def row_order(tp, paired):
    if not paired:
        return list(range(tp))
    me = lax.axis_index("tp")
    first = 2 + 2 * (me % 2)
    second = 6 - first
    own = [me, me ^ first, me ^ second, me ^ 6]
    other = me ^ 1
    return own + [other, other ^ second, other ^ first, other ^ 6]


def block_rows(index, own):
    start = index * own
    return pl.ds(start if isinstance(start, int) else pl.multiple_of(start, own), own)


def once(value, *others):
    return lax.optimization_barrier((value, others))[0]


def add_up(*terms):
    return sum(t.astype(F32) for t in terms).astype(BF16)


def add_pair(total, axis, distance, *others):
    route = [(i, i ^ distance) for i in range(lax.axis_size(axis))]
    mine = total.astype(BF16)
    theirs = lax.ppermute(mine, axis, route)
    return mine.astype(F32) + (once(theirs, *others) if others else theirs).astype(F32)


def gather_rows(block, chunks, paired, *others):
    if not paired:
        return [[lax.all_gather(block[:, a:b], "tp", axis=0, tiled=True)] for a, b in chunks]
    first, pieces = once(swap(block, 1), *others), []
    for a, b in chunks:
        near = jnp.concatenate([block[:, a:b], first[:, a:b]], axis=0)
        pieces.append([near, swap(near, 2), swap(near, 0)])
    return pieces


def scatter_rows(pieces, totals, own):
    far, first, count = [], [], len(pieces)
    for i in range(count + 1):
        if i < count:
            if i >= len(totals):
                totals.append(chip_sums(pieces[i], own, first[-1:]))
            far.append(swap(totals[i][1], 2))
        if i > 0:
            there = once(far[i - 1], totals[i][1]) if i < count else far[i - 1]
            first.append(add_up(totals[i - 1][0][own:], there[own:]))
    near = [swap(f, 1) for f in first]
    return [add_up(t[:own], f[:own], n) for (t, _), f, n in zip(totals, far, near)], first


def chip_sums(piece, own, others=()):
    keep, give = piece
    theirs = swap(give, 0)
    if others:
        theirs = once(theirs, *others)
    far = add_up(keep[2 * own :], theirs[2 * own :])
    return add_up(keep[: 2 * own], theirs[: 2 * own]), far


def step_rows(depth, count):
    step = 512 if count > 1 else 1024
    while depth % step:
        step //= 2
    return step


def stream_weights(w_refs, w_buf, w_sem, start, steps, compute):
    count = len(w_refs)
    slots, _, step, _ = w_buf.shape
    ahead = min(slots - 1, steps)

    def copy(k, m):
        slot = lax.rem(k, slots)
        rows = pl.ds(start + k * step, step)
        return pltpu.make_async_copy(w_refs[m].at[rows, :], w_buf.at[slot, m], w_sem.at[slot, m])

    for k in range(ahead):
        for m in range(count):
            copy(k, m).start()

    def body(k, carry):
        @pl.when(k + ahead < steps)
        def _():
            for m in range(count):
                copy(k + ahead, m).start()

        for m in range(count):
            copy(k, m).wait()
        compute(k, lax.rem(k, slots))
        return carry

    return lambda: lax.fori_loop(0, steps, body, 0)


def weight_scratch(count, step, group, slots=3):
    return [pltpu.VMEM((slots, count, step, group), BF16), pltpu.SemaphoreType.DMA((slots, count))]


def contract(left, right):
    return lax.dot_general(left, right, (((1,), (1,)), ((), ())), preferred_element_type=F32)


def matmul_cost(rows, depth, group, count):
    return pl.CostEstimate(
        flops=2 * count * rows * depth * group, bytes_accessed=2 * count * depth * group, transcendentals=0
    )


VMEM = pl.BlockSpec(memory_space=pltpu.VMEM)
ANYWHERE = pl.BlockSpec(memory_space=pl.ANY)


def project(pieces, weights, chunk, acc, tp, paired, taps, finish, out_grad=None, product=None, mats=()):
    rows = sum(p.shape[0] for p in pieces)
    count = len(weights)
    group = weights[0].shape[1]
    start, depth = chunk[0], chunk[1] - chunk[0]
    step = step_rows(depth, count)
    own = rows // tp
    n_x = len(pieces)
    has_acc = acc is not None
    pair = count == 2

    def kernel(*refs):
        x_refs, w_refs, refs = refs[:n_x], refs[n_x : n_x + count], refs[n_x + count :]
        if has_acc:
            acc_refs, refs = refs[:count], refs[count:]
        if finish:
            if not pair:
                grad_ref, prod_ref, mat_refs, refs = refs[0], refs[1], refs[2 : 2 + len(mats)], refs[2 + len(mats) :]
            outs, made_ref, edge_ref, refs = refs[:count], refs[count], refs[count + 1], refs[count + 2 :]
            if not pair:
                spectrum_ref, refs = refs[0], refs[1:]
            totals = refs[:count]
        else:
            totals = refs[:count]
        x_buf, w_buf, w_sem = refs[-3:]

        def compute(k, slot):
            x = x_buf[:, pl.ds(pl.multiple_of(k * step, step), step)]
            for m in range(count):
                totals[m][...] += jnp.dot(x, w_buf[slot, m], preferred_element_type=F32)

        run = stream_weights(w_refs, w_buf, w_sem, start, depth // step, compute)
        at = 0
        for piece in x_refs:
            x_buf[at : at + piece.shape[0], :] = piece[...]
            at += piece.shape[0]
        for m in range(count):
            totals[m][...] = acc_refs[m][...] if has_acc else jnp.zeros_like(totals[m])
        if finish and not pair:
            for cols in column_blocks(group):
                spectrum_ref[:, cols] = dot_there(mat_refs, prod_ref[:, cols], taps)
        run()
        if finish:
            for b, index in enumerate(row_order(tp, paired)):
                here = block_rows(index, own)
                part = [total[b * own : (b + 1) * own, :].astype(BF16) for total in totals]
                for out, value in zip(outs, part):
                    out[here, :] = value
                other = part[1] if pair else grad_ref[here, :]
                made_ref[here, :] = (part[0].astype(F32) * other.astype(F32)).astype(BF16)
            edge_ref[...] = made_ref[rows - taps :, :] if pair else made_ref[:taps, :]

    in_specs = [VMEM] * n_x + [ANYWHERE] * count
    args = [*pieces, *weights]
    if has_acc:
        in_specs += [VMEM] * count
        args += acc
    totals = (rows, group)
    scratch = [pltpu.VMEM((rows, depth), BF16), *weight_scratch(count, step, group)]
    full = jax.ShapeDtypeStruct((rows, group), BF16)
    if finish:
        if not pair:
            in_specs += [VMEM] * (2 + len(mats))
            args += [out_grad, product, *mats]
        out_shape = [full] * (count + 1) + [jax.ShapeDtypeStruct((taps, group), BF16)]
        if not pair:
            out_shape.append(jax.ShapeDtypeStruct((rows + taps, group), F32))
        scratch = [pltpu.VMEM(totals, F32)] * count + scratch
    else:
        out_shape = [jax.ShapeDtypeStruct(totals, F32)] * count
    return pl.pallas_call(
        kernel,
        in_specs=in_specs,
        out_specs=[VMEM] * len(out_shape),
        out_shape=out_shape,
        scratch_shapes=scratch,
        compiler_params=pltpu.CompilerParams(vmem_limit_bytes=FWD_VMEM),
        cost_estimate=matmul_cost(rows, depth, group, count),
        name="project",
    )(*args)


LANES = 128


def constant(matrix):
    stacked = np.concatenate(np.split(matrix, matrix.shape[1] // LANES, axis=1), axis=0)
    high = stacked.astype(jnp.bfloat16)
    low = (stacked - high.astype(np.float64)).astype(jnp.bfloat16)
    return jnp.asarray(high), jnp.asarray(low)


def transforms(length, taps):
    size = length + taps
    angle = 2 * np.pi / size * np.outer(np.arange(size // 2) + 0.5, np.arange(size))
    there = np.concatenate([np.cos(angle), -np.sin(angle)], axis=0)
    back = there.T * (2.0 / size)
    lags = back[np.arange(taps, 0, -1)]
    return [*constant(there), constant(np.concatenate([back[taps:], back[:length], lags], axis=0))[0]]


def window_of(mats):
    return math.isqrt(mats[0].shape[0] * mats[0].shape[1])


def part_of(ref, size, rows, cols):
    height = ref.shape[0] // (size // LANES)
    blocks = range(cols[0] // LANES, cols[1] // LANES)
    return jnp.concatenate([ref[b * height + rows[0] : b * height + rows[1], :] for b in blocks], axis=1)


def dot_there(mats, x, start):
    size = window_of(mats)
    cols = (start, start + x.shape[0])
    return jnp.dot(part_of(mats[0], size, (0, size), cols), x, preferred_element_type=F32)


def dot_back(mats, rows, re, im):
    y = jnp.concatenate([re, im], axis=0).astype(BF16)
    size = y.shape[0]
    return jnp.dot(part_of(mats[1], size, rows, (0, size)), y, preferred_element_type=F32)


def column_blocks(group):
    width = min(256, group)
    return [slice(a, a + width) for a in range(0, group, width)]


def transform_taps(filter_taps, there):
    taps, group = filter_taps.shape
    size = window_of(there)

    def kernel(high_ref, low_ref, taps_ref, out_ref):
        cols = ((0, size), (0, taps))
        high, low = part_of(high_ref, size, *cols), part_of(low_ref, size, *cols)
        f = taps_ref[...]
        f_high = f.astype(BF16)
        f_low = (f - f_high.astype(F32)).astype(BF16)
        out = jnp.dot(high, f_low, preferred_element_type=F32) + jnp.dot(low, f_high, preferred_element_type=F32)
        out_ref[...] = out + jnp.dot(high, f_high, preferred_element_type=F32)

    return pl.pallas_call(
        kernel,
        in_specs=[VMEM] * 3,
        out_specs=VMEM,
        out_shape=jax.ShapeDtypeStruct((size, group), F32),
        compiler_params=pltpu.CompilerParams(vmem_limit_bytes=MID_VMEM),
        cost_estimate=pl.CostEstimate(flops=6 * size * taps * group, bytes_accessed=4 * size * group, transcendentals=0),
        name="taps",
    )(*there, filter_taps)


def in_row_order(out_ref, scratch, own, tp, paired):
    for b, index in enumerate(row_order(tp, paired)):
        out_ref[b * own : (b + 1) * own, :] = scratch[block_rows(index, own), :]


def filter_forward(spectra, before, query, conv_in_grad, out_grad, mats, weight, chunk, tp, paired):
    length, group = query.shape
    taps = before.shape[0]
    half = (length + taps) // 2
    start, depth = chunk[0], chunk[1] - chunk[0]
    step = step_rows(depth, 1)

    def kernel(there, back, p_ref, h_ref, before_ref, q_ref, cig_ref, grad_ref, w_ref, mixed_ref, qg_ref, fg_ref, c_ref,
               total_ref, sq, w_buf, w_sem):
        def compute(k, slot):
            at = pl.ds(pl.multiple_of(k * step, step), step)
            total_ref[:, at] = contract(qg_ref[...], w_buf[slot, 0])

        run = stream_weights([w_ref], w_buf, w_sem, start, depth // step, compute)
        mat_refs = (there, back)
        for cols in column_blocks(group):
            p = p_ref[:, cols] + dot_there(mat_refs, before_ref[:, cols], 0)
            c = dot_there(mat_refs, cig_ref[:, cols], 0)
            c_ref[:, cols] = c
            h = h_ref[:, cols]
            pr, pi, cr, ci, hr, hi = p[:half], p[half:], c[:half], c[half:], h[:half], h[half:]
            conv = dot_back(mat_refs, (0, length), pr * hr - pi * hi, pr * hi + pi * hr)
            mixed_ref[:, cols] = (q_ref[:, cols].astype(F32) * conv).astype(BF16)
            sq[:, cols] = (grad_ref[:, cols].astype(F32) * conv).astype(BF16)
            lags = (2 * length, 2 * length + taps)
            fg_ref[:, cols] = dot_back(mat_refs, lags, cr * pr + ci * pi, cr * pi - ci * pr).astype(BF16)
        in_row_order(qg_ref, sq, length // tp, tp, paired)
        run()

    full = jax.ShapeDtypeStruct((length, group), BF16)
    out_shape = [
        full,
        full,
        jax.ShapeDtypeStruct((taps, group), BF16),
        jax.ShapeDtypeStruct((length + taps, group), F32),
        jax.ShapeDtypeStruct((length, depth), F32),
    ]
    return pl.pallas_call(
        kernel,
        in_specs=[VMEM] * 8 + [ANYWHERE],
        out_specs=[VMEM] * 5,
        out_shape=out_shape,
        scratch_shapes=[pltpu.VMEM((length, group), BF16), *weight_scratch(1, step, group, 5)],
        compiler_params=pltpu.CompilerParams(vmem_limit_bytes=MIX_VMEM),
        cost_estimate=matmul_cost(length, depth + 2048, group, 1),
        name="conv",
    )(*mats, *spectra, before, query, conv_in_grad, out_grad, weight)


def filter_backward(spectra, after, keys, values, mats, weights, chunk, partial, tp, paired):
    length, group = keys.shape
    taps = after.shape[0]
    half = (length + taps) // 2
    start, depth = chunk[0], chunk[1] - chunk[0]
    step = step_rows(depth, 2)
    parts = 2 if paired else 1
    share = length // parts

    def kernel(*refs):
        there, back, c_ref, h_ref, after_ref, k_ref, v_ref, partial_ref, *refs = refs
        w_refs, out_refs, (kg_ref, vg_ref, sk, sv, w_buf, w_sem) = refs[:2], refs[2 : 2 + parts], refs[2 + parts :]

        def compute(k, slot):
            at = pl.ds(pl.multiple_of(k * step, step), step)
            total = partial_ref[:, at] + contract(kg_ref[...], w_buf[slot, 0]) + contract(vg_ref[...], w_buf[slot, 1])
            for i in range(parts):
                out_refs[i][:, at] = total[i * share : (i + 1) * share].astype(BF16)

        run = stream_weights(w_refs, w_buf, w_sem, start, depth // step, compute)
        mat_refs = (there, back)
        for cols in column_blocks(group):
            g = c_ref[:, cols] + dot_there(mat_refs, after_ref[:, cols], length)
            h = h_ref[:, cols]
            gr, gi, hr, hi = g[:half], g[half:], h[:half], h[half:]
            product_grad = dot_back(mat_refs, (length, 2 * length), hr * gr + hi * gi, hr * gi - hi * gr)
            sk[:, cols] = (product_grad * v_ref[:, cols].astype(F32)).astype(BF16)
            sv[:, cols] = (product_grad * k_ref[:, cols].astype(F32)).astype(BF16)
        in_row_order(kg_ref, sk, length // tp, tp, paired)
        in_row_order(vg_ref, sv, length // tp, tp, paired)
        run()

    full = jax.ShapeDtypeStruct((length, group), BF16)
    return pl.pallas_call(
        kernel,
        in_specs=[VMEM] * 8 + [ANYWHERE] * 2,
        out_specs=[VMEM] * (parts + 2),
        out_shape=[jax.ShapeDtypeStruct((share, depth), BF16)] * parts + [full] * 2,
        scratch_shapes=[pltpu.VMEM((length, group), BF16)] * 2 + weight_scratch(2, step, group, 5),
        compiler_params=pltpu.CompilerParams(vmem_limit_bytes=MIX_VMEM),
        cost_estimate=matmul_cost(length, depth + 1024, group, 2),
        name="conv_back",
    )(*mats, *spectra, after, keys, values, partial, *weights)


def project_back(grads, weights, chunk, parts, ready):
    rows, group = grads[0].shape
    count = len(grads)
    start, depth = chunk[0], chunk[1] - chunk[0]
    step = step_rows(depth, count)
    share = rows // parts
    n_in = 2 * count + len(ready)

    def kernel(*refs):
        g_refs, w_refs = refs[:count], refs[count : 2 * count]
        out_refs, (w_buf, w_sem) = refs[n_in : n_in + parts], refs[n_in + parts :]

        def compute(k, slot):
            at = pl.ds(pl.multiple_of(k * step, step), step)
            total = contract(g_refs[0][...], w_buf[slot, 0])
            for m in range(1, count):
                total = total + contract(g_refs[m][...], w_buf[slot, m])
            for i in range(parts):
                out_refs[i][:, at] = total[i * share : (i + 1) * share].astype(BF16)

        stream_weights(w_refs, w_buf, w_sem, start, depth // step, compute)()

    return pl.pallas_call(
        kernel,
        in_specs=[VMEM] * count + [ANYWHERE] * count + [VMEM] * len(ready),
        out_specs=[VMEM] * parts,
        out_shape=[jax.ShapeDtypeStruct((share, depth), BF16)] * parts,
        scratch_shapes=weight_scratch(count, step, group),
        compiler_params=pltpu.CompilerParams(vmem_limit_bytes=BWD_VMEM),
        cost_estimate=matmul_cost(rows, depth, group, count),
        name="project_back",
    )(*grads, *weights, *ready)


def on_device(inputs, query_weight, key_weight, value_weight, filter_taps, out_grad):
    tp = lax.axis_size("tp")
    paired = tp == 8
    own_rows, width = inputs.shape
    taps = filter_taps.shape[0]
    there, there_low, back = transforms(own_rows * tp, taps)
    mats = (there, back)
    h = transform_taps(filter_taps, (there, there_low))
    chunks = bounds(width, FWD_PARTS)
    gathered = gather_rows(inputs, chunks, paired, h)
    pair = (key_weight, value_weight)
    acc = None
    for i, (pieces, chunk) in enumerate(zip(gathered, chunks)):
        if paired:
            if i + 1 < len(chunks):
                pieces[0] = once(pieces[0], gathered[i + 1][0])
            pieces.append(swap(once(pieces[1], acc[0]) if acc else pieces[1], 0))
        if i + 1 < len(chunks):
            acc = project(pieces, (query_weight, *pair), chunk, acc, tp, paired, taps, False)
    keys, values, product, tail = project(pieces, pair, chunk, acc[1:], tp, paired, taps, True)
    before = from_behind(tail, "ctx", 1)
    query, conv_in_grad, head, p = project(
        pieces, (query_weight,), chunk, acc[:1], tp, paired, taps, True, out_grad, product, mats
    )
    after = from_behind(head, "ctx", -1)
    chunks = bounds(width, BWD_PARTS)
    mixed, query_grad, local_taps, c, partial = filter_forward(
        (p, h), before, query, conv_in_grad, out_grad, mats, query_weight, chunks[0], tp, paired
    )
    *piece, keys_grad, values_grad = filter_backward(
        (c, h), after, keys, values, mats, pair, chunks[0], partial, tp, paired
    )
    size = lax.axis_size("ctx")
    distances = [2**i for i in range(size.bit_length() - 1)] if size & (size - 1) == 0 else []
    pieces, totals = [piece], []
    grads, weights = (query_grad, keys_grad, values_grad), (query_weight, *pair)
    for i, chunk in enumerate(chunks[1:]):
        ready = []
        if i == 1 and distances:
            local_taps = add_pair(local_taps, "ctx", distances.pop(0))
            ready.append(local_taps)
        if paired and i > 0:
            totals.append(chip_sums(pieces[i - 1], own_rows))
            ready.append(totals[-1][1])
        pieces.append(project_back(grads, weights, chunk, 2 if paired else 1, ready))
    if paired:
        summed, last = scatter_rows(pieces, totals, own_rows)
    else:
        summed = [lax.psum_scatter(p, "tp", scatter_dimension=0, tiled=True) for (p,) in pieces]
        last = summed
    for distance in distances:
        local_taps = add_pair(local_taps, "ctx", distance, *last)
    if size & (size - 1):
        local_taps = lax.psum(local_taps, "ctx")
    return mixed, jnp.concatenate(summed, axis=1), local_taps.astype(F32)


def solution(mesh):
    in_specs = (
        P(("ctx", "tp"), None),
        P(None, "tp"),
        P(None, "tp"),
        P(None, "tp"),
        P(None, "tp"),
        P("ctx", "tp"),
    )
    out_specs = (P("ctx", "tp"), P(("ctx", "tp"), None), P(None, "tp"))
    return jax.shard_map(
        on_device, mesh=mesh, in_specs=in_specs, out_specs=out_specs, check_vma=False
    )
```

time: 118 us -> 105 us (0.89)
  Pallas kernels: 60.4 us -> 50.9 us
  waiting for transfers between devices: 27.7 us -> 21.6 us
  local copies, waits for them, and re-layouts: 1.21 us -> 4.98 us
  starting transfers between devices: 24.7 us -> 23.1 us
    pallas_call x4 -> x2, Pallas kernels: 24.8 us -> 12 us  [project_back(): pl.pallas_call(kernel, in_specs=[VMEM] * count + [ANYWHERE] * count + [VM...]
    ppermute x16, waiting for transfers between devices: 25.6 us -> 19.1 us  [swap(): lax.ppermute(block, 'tp', [(i, i ^ offsets[i % 2]) for i in range(8)])]
    unnamed x12, local copies, waits for them, and re-layouts: 0.04 us -> 2.97 us
    pallas_call x4 -> x3, Pallas kernels: 12.3 us -> 14.9 us  [the longest x1 8.09 us: filter_backward(): pl.pallas_call(kernel, in_specs=[VMEM] * 8 + [ANYWHERE] * 2, out_specs=[V...]
    ppermute x2, waiting for transfers between devices: 0.01 us -> 2.44 us  [from_behind(): return lax.ppermute(block, axis, route)]
    ppermute x2, starting transfers between devices: 5.32 us -> 3.06 us  [add_pair(): theirs = lax.ppermute(mine, axis, route)]
    ppermute x2, waiting for transfers between devices: 2.07 us -> 0.01 us  [add_pair(): theirs = lax.ppermute(mine, axis, route)]
  transfers between devices with their start and end apart: 20 -> 20, of which waited for: 9 -> 11; matrix products, arithmetic and copies ran while one was open for 2% -> 4% of each run, Pallas kernels for 34% -> 30%
where the time goes in v4:
time: 105 us; the launch traced here: 104 us
  Pallas kernels  50.9 us (48%)
  starting transfers between devices  23.1 us (22%)
  waiting for transfers between devices  21.6 us (21%)
  local copies, waits for them, and re-layouts  4.98 us (5%)
  other arithmetic  2.66 us (3%)
    pallas_call x3, Pallas kernels, project(): pl.pallas_call(kernel, in_specs=in_specs, out_specs=[VMEM] * len(out_shap...  24 us
    ppermute x16, waiting for transfers between devices, swap(): lax.ppermute(block, 'tp', [(i, i ^ offsets[i % 2]) for i in range(8)])  19.1 us
    ppermute x16, starting transfers between devices, swap(): lax.ppermute(block, 'tp', [(i, i ^ offsets[i % 2]) for i in range(8)])  14.6 us
    pallas_call x2, Pallas kernels, project_back(): pl.pallas_call(kernel, in_specs=[VMEM] * count + [ANYWHERE] * count + [VM...  12 us
    pallas_call x1, Pallas kernels, filter_backward(): pl.pallas_call(kernel, in_specs=[VMEM] * 8 + [ANYWHERE] * 2, out_specs=[V...  8.09 us
    pallas_call x1, Pallas kernels, filter_forward(): pl.pallas_call(kernel, in_specs=[VMEM] * 8 + [ANYWHERE], out_specs=[VMEM]...  6.02 us
    ppermute x2, starting transfers between devices, from_behind(): return lax.ppermute(block, axis, route)  5.47 us
    ppermute x2, starting transfers between devices, add_pair(): theirs = lax.ppermute(mine, axis, route)  3.06 us
  transfers between devices with their start and end apart: 20, of which 11 were waited for; matrix products, arithmetic and copies ran while one was open for 4% of the time, Pallas kernels for 30%

profile of v4, /device:TPU:0, one launch (start us, length us, event | category | flops | bytes accessed | tf_op | source)
XLA Modules:
  0.0 104.1 jit_solution(17567995804052313604)
XLA Ops:
  0.6 3.0 %collective-permute-start = (bf16[32,8192]{1,0:T(8,128)(2,1)}, bf16[32,8192]{1,0:T(8,128)(2,1)S(1)}, u32[]{:S(2)}, u32[]{:S(2)}) collective-permute-start(bf16[32,8192]{1,0:T(8,128)(2,1)} %param.9), channel_id=1, source_target_pairs={{0,2},{1,5},{2,0},{3,7},{4,6},{5,1},{6,4},{7,3},{8,10},{9,13},{10,... | collective-permute-start | bytes 1572872 | tf_op jit(solution)/shard_map/ppermute | solution.py:34
  9.3 1.7 %collective-permute-done = bf16[32,8192]{1,0:T(8,128)(2,1)S(1)} collective-permute-done((bf16[32,8192]{1,0:T(8,128)(2,1)}, bf16[32,8192]{1,0:T(8,128)(2,1)S(1)}, u32[]{:S(2)}, u32[]{:S(2)}) %collective-permute-start) | collective-permute-done | bytes 524320 | tf_op jit(solution)/shard_map/ppermute | solution.py:34
  11.1 2.1 %collective-permute-start.3 = (bf16[64,2048]{1,0:T(8,128)(2,1)S(1)}, bf16[64,2048]{1,0:T(8,128)(2,1)S(1)}, u32[]{:S(2)}, u32[]{:S(2)}) collective-permute-start(bf16[64,2048]{1,0:T(8,128)(2,1)S(1)} %pad_maximum_fusion.2.refs_0_), channel_id=1, source_target_pairs={{0,4},{1,3},{2,6},{3,1},{4,0},{5,7},{6,2},{7,5},{8,12},{9,11},{10,... | collective-permute-start | bytes 786440 | tf_op jit(solution)/shard_map/ppermute | solution.py:34
  13.4 4.1 %collective-permute-done.3.refs_1_ = bf16[64,2048]{1,0:T(8,128)(2,1)S(1)} collective-permute-done((bf16[64,2048]{1,0:T(8,128)(2,1)S(1)}, bf16[64,2048]{1,0:T(8,128)(2,1)S(1)}, u32[]{:S(2)}, u32[]{:S(2)}) %collective-permute-start.3) | collective-permute-done | bytes 262176 | tf_op jit(solution)/shard_map/ppermute | solution.py:34
  19.1 6.0 %project.3 = (f32[256,1024]{1,0:T(8,128)S(1)}, f32[256,1024]{1,0:T(8,128)S(1)}, f32[256,1024]{1,0:T(8,128)S(1)}) custom-call(bf16[64,2048]{1,0:T(8,128)(2,1)S(1)} %pad_maximum_fusion.2.refs_0_, bf16[64,2048]{1,0:T(8,128)(2,1)S(1)} %collective-permute-done.3.refs_1_, bf16[64,2048]{1,0:T(8,128)(2,1)S(1)} %collective-permute-done.4.refs_2_, ...), custom_call_target="tpu_custom_call" | custom-call | flops 3221225472 | bytes 12582912 | tf_op jit(solution)/shard_map/project/pallas_call | solution.py:224
  26.0 2.3 %collective-permute-done.6.refs_3_ = bf16[64,6144]{1,0:T(8,128)(2,1)S(1)} collective-permute-done((bf16[64,6144]{1,0:T(8,128)(2,1)S(1)}, bf16[64,6144]{1,0:T(8,128)(2,1)S(1)}, u32[]{:S(2)}, u32[]{:S(2)}) %collective-permute-start.6) | collective-permute-done | bytes 786464 | tf_op jit(solution)/shard_map/ppermute | solution.py:34
  28.3 11.5 %project.4 = (bf16[256,1024]{1,0:T(8,128)(2,1)S(1)}, bf16[256,1024]{1,0:T(8,128)(2,1)S(1)}, bf16[256,1024]{1,0:T(8,128)(2,1)S(1)}, bf16[128,1024]{1,0:T(8,128)(2,1)S(1)}) custom-call(bf16[64,6144]{1,0:T(8,128)(2,1)S(1)} %pad_maximum_fusion.refs_0_, bf16[64,6144]{1,0:T(8,128)(2,1)S(1)} %collective-permute-done.1.refs_1_, ...), custom_call_target="tpu_custom_call" | custom-call | flops 6442450944 | bytes 25165824 | tf_op jit(solution)/shard_map/project/pallas_call | solution.py:224
  39.8 4.0 %collective-permute-start.7 = (bf16[128,1024]{1,0:T(8,128)(2,1)S(1)}, bf16[128,1024]{1,0:T(8,128)(2,1)S(1)}, u32[]{:S(2)}, u32[]{:S(2)}) collective-permute-start(bf16[128,1024]{1,0:T(8,128)(2,1)S(1)} %get-tuple-element.42), channel_id=1, source_target_pairs={{0,8},{8,16},{16,24},{1,9},{9,17},{17,25},{2,10},{10,18},{18,26},{... | collective-permute-start | bytes 786440 | tf_op jit(solution)/shard_map/ppermute | solution.py:29
  43.8 6.5 %project.5 = (bf16[256,1024]{1,0:T(8,128)(2,1)S(1)}, bf16[256,1024]{1,0:T(8,128)(2,1)S(1)}, bf16[128,1024]{1,0:T(8,128)(2,1)S(1)}, f32[384,1024]{1,0:T(8,128)S(1)}) custom-call(bf16[64,6144]{1,0:T(8,128)(2,1)S(1)} %pad_maximum_fusion.refs_0_, bf16[64,6144]{1,0:T(8,128)(2,1)S(1)} %collective-permute-done.1.refs_1_, ...), custom_call_target="tpu_custom_call" | custom-call | flops 3221225472 | bytes 12582912 | tf_op jit(solution)/shard_map/project/pallas_call | solution.py:224
  50.3 1.5 %collective-permute-start.8 = (bf16[128,1024]{1,0:T(8,128)(2,1)S(1)}, bf16[128,1024]{1,0:T(8,128)(2,1)S(1)}, u32[]{:S(2)}, u32[]{:S(2)}) collective-permute-start(bf16[128,1024]{1,0:T(8,128)(2,1)S(1)} %get-tuple-element.47), channel_id=1, source_target_pairs={{8,0},{16,8},{24,16},{9,1},{17,9},{25,17},{10,2},{18,10},{26,18},{... | collective-permute-start | bytes 786440 | tf_op jit(solution)/shard_map/ppermute | solution.py:29
  51.8 6.0 %conv.1 = (bf16[256,1024]{1,0:T(8,128)(2,1)}, bf16[256,1024]{1,0:T(8,128)(2,1)S(1)}, bf16[128,1024]{1,0:T(8,128)(2,1)S(1)}, f32[384,1024]{1,0:T(8,128)S(1)}, f32[256,4096]{1,0:T(8,128)S(1)}) custom-call(bf16[1152,128]{1,0:T(8,128)(2,1)S(1)} %copy-done.1, bf16[1920,128]{1,0:T(8,128)(2,1)S(1)} %copy-done.2, f32[384,1024]{1,0:T(8,128)S(1)} %get-tuple-element.41.p_ref, ...), custom_call_target="tpu_custom_call" | custom-call | flops 3221225472 | bytes 12582912 | tf_op jit(solution)/shard_map/conv/pallas_call | solution.py:348
  57.9 2.4 %collective-permute-done.8.refs_4_ = bf16[128,1024]{1,0:T(8,128)(2,1)S(1)} collective-permute-done((bf16[128,1024]{1,0:T(8,128)(2,1)S(1)}, bf16[128,1024]{1,0:T(8,128)(2,1)S(1)}, u32[]{:S(2)}, u32[]{:S(2)}) %collective-permute-start.8) | collective-permute-done | bytes 262176 | tf_op jit(solution)/shard_map/ppermute | solution.py:29
  60.3 8.1 %conv_back.1 = (bf16[128,4096]{1,0:T(8,128)(2,1)S(1)}, bf16[128,4096]{1,0:T(8,128)(2,1)S(1)}, bf16[256,1024]{1,0:T(8,128)(2,1)S(1)}, bf16[256,1024]{1,0:T(8,128)(2,1)S(1)}) custom-call(bf16[1152,128]{1,0:T(8,128)(2,1)S(1)} %copy-done.1, bf16[1920,128]{1,0:T(8,128)(2,1)S(1)} %copy-done.2, f32[384,1024]{1,0:T(8,128)S(1)} %get-tuple-element.46.refs_2_, ...), custom_call_target="tpu_custom_call" | custom-call | flops 5368709120 | bytes 20971520 | tf_op jit(solution)/shard_map/conv_back/pallas_call | solution.py:393
  68.5 1.6 %collective-permute-start.14 = (bf16[128,1024]{1,0:T(8,128)(2,1)S(1)}, bf16[128,1024]{1,0:T(8,128)(2,1)S(1)}, u32[]{:S(2)}, u32[]{:S(2)}) collective-permute-start(bf16[128,1024]{1,0:T(8,128)(2,1)S(1)} %get-tuple-element.59), channel_id=1, source_target_pairs={{0,8},{8,0},{16,24},{24,16},{1,9},{9,1},{17,25},{25,17},{2,10},{10... | collective-permute-start | bytes 786440 | tf_op jit(solution)/shard_map/ppermute | solution.py:64
  70.1 8.1 %project_back.2 = (bf16[128,3072]{1,0:T(8,128)(2,1)S(1)}, bf16[128,3072]{1,0:T(8,128)(2,1)S(1)}) custom-call(bf16[256,1024]{1,0:T(8,128)(2,1)S(1)} %get-tuple-element.53.refs_0_, bf16[256,1024]{1,0:T(8,128)(2,1)S(1)} %get-tuple-element.54.refs_1_, bf16[256,1024]{1,0:T(8,128)(2,1)S(1)} %get-tuple-element.55.refs_2_, bf16[8192,1024]{1,0:T(8,128)(2,1)} %refs_3_.3, ...), custom_call_target="tpu_custom_call" | custom-call | flops 4831838208 | bytes 18874368 | tf_op jit(solution)/shard_map/project_back/pallas_call | solution.py:427
  78.5 1.4 %collective-permute-start.19 = (bf16[128,1024]{1,0:T(8,128)(2,1)S(1)}, bf16[128,1024]{1,0:T(8,128)(2,1)S(1)}, u32[]{:S(2)}, u32[]{:S(2)}) collective-permute-start(bf16[128,1024]{1,0:T(8,128)(2,1)S(1)} %get-tuple-element.69), channel_id=1, source_target_pairs={{0,16},{8,24},{16,0},{24,8},{1,17},{9,25},{17,1},{25,9},{2,18},{10... | collective-permute-start | bytes 786440 | tf_op jit(solution)/shard_map/ppermute | solution.py:64
  80.2 1.6 %collective-permute-start.10 = (bf16[64,4096]{1,0:T(8,128)(2,1)S(1)}, bf16[64,4096]{1,0:T(8,128)(2,1)S(1)}, u32[]{:S(2)}, u32[]{:S(2)}) collective-permute-start(bf16[64,4096]{1,0:T(8,128)(2,1)S(1)} %get-tuple-element.66.refs_7_), channel_id=1, source_target_pairs={{0,4},{1,3},{2,6},{3,1},{4,0},{5,7},{6,2},{7,5},{8,12},{9,11},{10,... | collective-permute-start | bytes 1572872 | tf_op jit(solution)/shard_map/ppermute | solution.py:34
  82.5 4.0 %project_back.3 = (bf16[128,1024]{1,0:T(8,128)(2,1)S(1)}, bf16[128,1024]{1,0:T(8,128)(2,1)S(1)}) custom-call(bf16[256,1024]{1,0:T(8,128)(2,1)S(1)} %get-tuple-element.53.refs_0_, bf16[256,1024]{1,0:T(8,128)(2,1)S(1)} %get-tuple-element.54.refs_1_, bf16[256,1024]{1,0:T(8,128)(2,1)S(1)} %get-tuple-element.55.refs_2_, bf16[8192,1024]{1,0:T(8,128)(2,1)} %refs_3_.3, ...), custom_call_target="tpu_custom_call" | custom-call | flops 1610612736 | bytes 6291456 | tf_op jit(solution)/shard_map/project_back/pallas_call | solution.py:427
  86.6 2.8 %collective-permute-done.10 = bf16[64,4096]{1,0:T(8,128)(2,1)S(1)} collective-permute-done((bf16[64,4096]{1,0:T(8,128)(2,1)S(1)}, bf16[64,4096]{1,0:T(8,128)(2,1)S(1)}, u32[]{:S(2)}, u32[]{:S(2)}) %collective-permute-start.10) | collective-permute-done | bytes 524320 | tf_op jit(solution)/shard_map/ppermute | solution.py:34
  89.5 1.6 %collective-permute-start.12 = (bf16[32,4096]{1,0:T(8,128)(2,1)S(1)}, bf16[32,4096]{1,0:T(8,128)(2,1)S(1)}, u32[]{:S(2)}, u32[]{:S(2)}) collective-permute-start(bf16[32,4096]{1,0:T(8,128)(2,1)S(1)} %add_convert_fusion.5), channel_id=1, source_target_pairs={{0,2},{1,5},{2,0},{3,7},{4,6},{5,1},{6,4},{7,3},{8,10},{9,13},{10,... | collective-permute-start | bytes 786440 | tf_op jit(solution)/shard_map/ppermute | solution.py:34
  91.1 1.6 %collective-permute-start.17 = (bf16[64,1024]{1,0:T(8,128)(2,1)S(1)}, bf16[64,1024]{1,0:T(8,128)(2,1)S(1)}, u32[]{:S(2)}, u32[]{:S(2)}) collective-permute-start(bf16[64,1024]{1,0:T(8,128)(2,1)S(1)} %get-tuple-element.72), channel_id=1, source_target_pairs={{0,4},{1,3},{2,6},{3,1},{4,0},{5,7},{6,2},{7,5},{8,12},{9,11},{10,... | collective-permute-start | bytes 393224 | tf_op jit(solution)/shard_map/ppermute | solution.py:34
  92.7 3.2 %collective-permute-done.13 = bf16[64,3072]{1,0:T(8,128)(2,1)S(1)} collective-permute-done((bf16[64,3072]{1,0:T(8,128)(2,1)S(1)}, bf16[64,3072]{1,0:T(8,128)(2,1)S(1)}, u32[]{:S(2)}, u32[]{:S(2)}) %collective-permute-start.13) | collective-permute-done | bytes 393248 | tf_op jit(solution)/shard_map/ppermute | solution.py:34
  96.0 1.6 %collective-permute-start.16 = (bf16[32,3072]{1,0:T(8,128)(2,1)S(1)}, bf16[32,3072]{1,0:T(8,128)(2,1)S(1)}, u32[]{:S(2)}, u32[]{:S(2)}) collective-permute-start(bf16[32,3072]{1,0:T(8,128)(2,1)S(1)} %add_convert_fusion.7), channel_id=1, source_target_pairs={{0,2},{1,5},{2,0},{3,7},{4,6},{5,1},{6,4},{7,3},{8,10},{9,13},{10,... | collective-permute-start | bytes 589832 | tf_op jit(solution)/shard_map/ppermute | solution.py:34
  98.8 1.6 %collective-permute-start.18 = (bf16[32,1024]{1,0:T(8,128)(2,1)S(1)}, bf16[32,1024]{1,0:T(8,128)(2,1)S(1)}, u32[]{:S(2)}, u32[]{:S(2)}) collective-permute-start(bf16[32,1024]{1,0:T(8,128)(2,1)S(1)} %add_convert_fusion.11), channel_id=1, source_target_pairs={{0,2},{1,5},{2,0},{3,7},{4,6},{5,1},{6,4},{7,3},{8,10},{9,13},{10,... | collective-permute-start | bytes 196616 | tf_op jit(solution)/shard_map/ppermute | solution.py:34
  (54 shorter events, 14.9 us)
Async XLA Ops:
  0.6 10.4 %collective-permute-start = (bf16[32,8192]{1,0:T(8,128)(2,1)}, bf16[32,8192]{1,0:T(8,128)(2,1)S(1)}, u32[]{:S(2)}, u32[]{:S(2)}) collective-permute-start(bf16[32,8192]{1,0:T(8,128)(2,1)} %param.9), channel_id=1, source_target_pairs={{0,2},{1,5},{2,0},{3,7},{4,6},{5,1},{6,4},{7,3},{8,10},{9,13},{10,... | collective-permute-start | bytes 1572872 | tf_op jit(solution)/shard_map/ppermute | solution.py:34
  6.6 1.0 %copy-start.4 = (f32[128,1024]{1,0:T(8,128)S(1)}, f32[128,1024]{1,0:T(8,128)}, u32[]{:S(2)}) copy-start(f32[128,1024]{1,0:T(8,128)} %taps_ref.1) | copy-start | bytes 1572868
  11.1 6.5 %collective-permute-start.3 = (bf16[64,2048]{1,0:T(8,128)(2,1)S(1)}, bf16[64,2048]{1,0:T(8,128)(2,1)S(1)}, u32[]{:S(2)}, u32[]{:S(2)}) collective-permute-start(bf16[64,2048]{1,0:T(8,128)(2,1)S(1)} %pad_maximum_fusion.2.refs_0_), channel_id=1, source_target_pairs={{0,4},{1,3},{2,6},{3,1},{4,0},{5,7},{6,2},{7,5},{8,12},{9,11},{10,... | collective-permute-start | bytes 786440 | tf_op jit(solution)/shard_map/ppermute | solution.py:34
  13.2 12.7 %collective-permute-start.1 = (bf16[64,6144]{1,0:T(8,128)(2,1)S(1)}, bf16[64,6144]{1,0:T(8,128)(2,1)S(1)}, u32[]{:S(2)}, u32[]{:S(2)}) collective-permute-start(bf16[64,6144]{1,0:T(8,128)(2,1)S(1)} %pad_maximum_fusion.refs_0_), channel_id=1, source_target_pairs={{0,4},{1,3},{2,6},{3,1},{4,0},{5,7},{6,2},{7,5},{8,12},{9,11},{10,... | collective-permute-start | bytes 2359304 | tf_op jit(solution)/shard_map/ppermute | solution.py:34
  13.3 4.7 %collective-permute-start.4 = (bf16[64,2048]{1,0:T(8,128)(2,1)S(1)}, bf16[64,2048]{1,0:T(8,128)(2,1)S(1)}, u32[]{:S(2)}, u32[]{:S(2)}) collective-permute-start(bf16[64,2048]{1,0:T(8,128)(2,1)S(1)} %pad_maximum_fusion.2.refs_0_), channel_id=1, source_target_pairs={{0,1},{1,0},{2,3},{3,2},{4,5},{5,4},{6,7},{7,6},{8,9},{9,8},{10,11... | collective-permute-start | bytes 786440 | tf_op jit(solution)/shard_map/ppermute | solution.py:34
  17.5 1.5 %collective-permute-start.5 = (bf16[64,2048]{1,0:T(8,128)(2,1)S(1)}, bf16[64,2048]{1,0:T(8,128)(2,1)S(1)}, u32[]{:S(2)}, u32[]{:S(2)}) collective-permute-start(bf16[64,2048]{1,0:T(8,128)(2,1)S(1)} %collective-permute-done.3.refs_1_), channel_id=1, source_target_pairs={{0,1},{1,0},{2,3},{3,2},{4,5},{5,4},{6,7},{7,6},{8,9},{9,8},{10,11... | collective-permute-start | bytes 786440 | tf_op jit(solution)/shard_map/ppermute | solution.py:34
  17.6 8.4 %collective-permute-start.2 = (bf16[64,6144]{1,0:T(8,128)(2,1)S(1)}, bf16[64,6144]{1,0:T(8,128)(2,1)S(1)}, u32[]{:S(2)}, u32[]{:S(2)}) collective-permute-start(bf16[64,6144]{1,0:T(8,128)(2,1)S(1)} %pad_maximum_fusion.refs_0_), channel_id=1, source_target_pairs={{0,1},{1,0},{2,3},{3,2},{4,5},{5,4},{6,7},{7,6},{8,9},{9,8},{10,11... | collective-permute-start | bytes 2359304 | tf_op jit(solution)/shard_map/ppermute | solution.py:34
  26.0 2.3 %collective-permute-start.6 = (bf16[64,6144]{1,0:T(8,128)(2,1)S(1)}, bf16[64,6144]{1,0:T(8,128)(2,1)S(1)}, u32[]{:S(2)}, u32[]{:S(2)}) collective-permute-start(bf16[64,6144]{1,0:T(8,128)(2,1)S(1)} %collective-permute-done.1.refs_1_), channel_id=1, source_target_pairs={{0,1},{1,0},{2,3},{3,2},{4,5},{5,4},{6,7},{7,6},{8,9},{9,8},{10,11... | collective-permute-start | bytes 2359304 | tf_op jit(solution)/shard_map/ppermute | solution.py:34
  28.3 15.5 %copy-start.1 = (bf16[1152,128]{1,0:T(8,128)(2,1)S(1)}, bf16[1152,128]{1,0:T(8,128)(2,1)}, u32[]{:S(2)}) copy-start(bf16[1152,128]{1,0:T(8,128)(2,1)} %constant.6.clone.high_ref.refs_8_.there.refs_0_) | copy-start | bytes 884740
  28.3 15.6 %copy-start.2 = (bf16[1920,128]{1,0:T(8,128)(2,1)S(1)}, bf16[1920,128]{1,0:T(8,128)(2,1)}, u32[]{:S(2)}) copy-start(bf16[1920,128]{1,0:T(8,128)(2,1)} %constant.8.clone.refs_9_.back.refs_1_) | copy-start | bytes 1474564
  28.3 15.6 %copy-start.3 = (bf16[256,1024]{1,0:T(8,128)(2,1)S(1)}, bf16[256,1024]{1,0:T(8,128)(2,1)}, u32[]{:S(2)}) copy-start(bf16[256,1024]{1,0:T(8,128)(2,1)} %grad_ref.1) | copy-start | bytes 1572868
  39.8 12.0 %collective-permute-start.7 = (bf16[128,1024]{1,0:T(8,128)(2,1)S(1)}, bf16[128,1024]{1,0:T(8,128)(2,1)S(1)}, u32[]{:S(2)}, u32[]{:S(2)}) collective-permute-start(bf16[128,1024]{1,0:T(8,128)(2,1)S(1)} %get-tuple-element.42), channel_id=1, source_target_pairs={{0,8},{8,16},{16,24},{1,9},{9,17},{17,25},{2,10},{10,18},{18,26},{... | collective-permute-start | bytes 786440 | tf_op jit(solution)/shard_map/ppermute | solution.py:29
  50.3 10.0 %collective-permute-start.8 = (bf16[128,1024]{1,0:T(8,128)(2,1)S(1)}, bf16[128,1024]{1,0:T(8,128)(2,1)S(1)}, u32[]{:S(2)}, u32[]{:S(2)}) collective-permute-start(bf16[128,1024]{1,0:T(8,128)(2,1)S(1)} %get-tuple-element.47), channel_id=1, source_target_pairs={{8,0},{16,8},{24,16},{9,1},{17,9},{25,17},{10,2},{18,10},{26,18},{... | collective-permute-start | bytes 786440 | tf_op jit(solution)/shard_map/ppermute | solution.py:29
  68.4 11.5 %collective-permute-start.9 = (bf16[128,4096]{1,0:T(8,128)(2,1)S(1)}, bf16[128,4096]{1,0:T(8,128)(2,1)S(1)}, u32[]{:S(2)}, u32[]{:S(2)}) collective-permute-start(bf16[128,4096]{1,0:T(8,128)(2,1)S(1)} %get-tuple-element.52), channel_id=1, source_target_pairs={{0,1},{1,0},{2,3},{3,2},{4,5},{5,4},{6,7},{7,6},{8,9},{9,8},{10,11... | collective-permute-start | bytes 3145736 | tf_op jit(solution)/shard_map/ppermute | solution.py:34
  68.5 9.9 %collective-permute-start.14 = (bf16[128,1024]{1,0:T(8,128)(2,1)S(1)}, bf16[128,1024]{1,0:T(8,128)(2,1)S(1)}, u32[]{:S(2)}, u32[]{:S(2)}) collective-permute-start(bf16[128,1024]{1,0:T(8,128)(2,1)S(1)} %get-tuple-element.59), channel_id=1, source_target_pairs={{0,8},{8,0},{16,24},{24,16},{1,9},{9,1},{17,25},{25,17},{2,10},{10... | collective-permute-start | bytes 786440 | tf_op jit(solution)/shard_map/ppermute | solution.py:64
  78.2 3.6 %collective-permute-start.11 = (bf16[128,3072]{1,0:T(8,128)(2,1)S(1)}, bf16[128,3072]{1,0:T(8,128)(2,1)S(1)}, u32[]{:S(2)}, u32[]{:S(2)}) collective-permute-start(bf16[128,3072]{1,0:T(8,128)(2,1)S(1)} %get-tuple-element.57), channel_id=1, source_target_pairs={{0,1},{1,0},{2,3},{3,2},{4,5},{5,4},{6,7},{7,6},{8,9},{9,8},{10,11... | collective-permute-start | bytes 2359304 | tf_op jit(solution)/shard_map/ppermute | solution.py:34
  78.5 21.9 %collective-permute-start.19 = (bf16[128,1024]{1,0:T(8,128)(2,1)S(1)}, bf16[128,1024]{1,0:T(8,128)(2,1)S(1)}, u32[]{:S(2)}, u32[]{:S(2)}) collective-permute-start(bf16[128,1024]{1,0:T(8,128)(2,1)S(1)} %get-tuple-element.69), channel_id=1, source_target_pairs={{0,16},{8,24},{16,0},{24,8},{1,17},{9,25},{17,1},{25,9},{2,18},{10... | collective-permute-start | bytes 786440 | tf_op jit(solution)/shard_map/ppermute | solution.py:64
  80.2 9.2 %collective-permute-start.10 = (bf16[64,4096]{1,0:T(8,128)(2,1)S(1)}, bf16[64,4096]{1,0:T(8,128)(2,1)S(1)}, u32[]{:S(2)}, u32[]{:S(2)}) collective-permute-start(bf16[64,4096]{1,0:T(8,128)(2,1)S(1)} %get-tuple-element.66.refs_7_), channel_id=1, source_target_pairs={{0,4},{1,3},{2,6},{3,1},{4,0},{5,7},{6,2},{7,5},{8,12},{9,11},{10,... | collective-permute-start | bytes 1572872 | tf_op jit(solution)/shard_map/ppermute | solution.py:34
  81.9 14.0 %collective-permute-start.13 = (bf16[64,3072]{1,0:T(8,128)(2,1)S(1)}, bf16[64,3072]{1,0:T(8,128)(2,1)S(1)}, u32[]{:S(2)}, u32[]{:S(2)}) collective-permute-start(bf16[64,3072]{1,0:T(8,128)(2,1)S(1)} %get-tuple-element.68), channel_id=1, source_target_pairs={{0,4},{1,3},{2,6},{3,1},{4,0},{5,7},{6,2},{7,5},{8,12},{9,11},{10,... | collective-permute-start | bytes 1179656 | tf_op jit(solution)/shard_map/ppermute | solution.py:34
  86.5 4.5 %collective-permute-start.15 = (bf16[128,1024]{1,0:T(8,128)(2,1)S(1)}, bf16[128,1024]{1,0:T(8,128)(2,1)S(1)}, u32[]{:S(2)}, u32[]{:S(2)}) collective-permute-start(bf16[128,1024]{1,0:T(8,128)(2,1)S(1)} %get-tuple-element.61), channel_id=1, source_target_pairs={{0,1},{1,0},{2,3},{3,2},{4,5},{5,4},{6,7},{7,6},{8,9},{9,8},{10,11... | collective-permute-start | bytes 786440 | tf_op jit(solution)/shard_map/ppermute | solution.py:34
  89.5 13.7 %collective-permute-start.12 = (bf16[32,4096]{1,0:T(8,128)(2,1)S(1)}, bf16[32,4096]{1,0:T(8,128)(2,1)S(1)}, u32[]{:S(2)}, u32[]{:S(2)}) collective-permute-start(bf16[32,4096]{1,0:T(8,128)(2,1)S(1)} %add_convert_fusion.5), channel_id=1, source_target_pairs={{0,2},{1,5},{2,0},{3,7},{4,6},{5,1},{6,4},{7,3},{8,10},{9,13},{10,... | collective-permute-start | bytes 786440 | tf_op jit(solution)/shard_map/ppermute | solution.py:34
  91.1 7.7 %collective-permute-start.17 = (bf16[64,1024]{1,0:T(8,128)(2,1)S(1)}, bf16[64,1024]{1,0:T(8,128)(2,1)S(1)}, u32[]{:S(2)}, u32[]{:S(2)}) collective-permute-start(bf16[64,1024]{1,0:T(8,128)(2,1)S(1)} %get-tuple-element.72), channel_id=1, source_target_pairs={{0,4},{1,3},{2,6},{3,1},{4,0},{5,7},{6,2},{7,5},{8,12},{9,11},{10,... | collective-permute-start | bytes 393224 | tf_op jit(solution)/shard_map/ppermute | solution.py:34
  96.0 5.7 %collective-permute-start.16 = (bf16[32,3072]{1,0:T(8,128)(2,1)S(1)}, bf16[32,3072]{1,0:T(8,128)(2,1)S(1)}, u32[]{:S(2)}, u32[]{:S(2)}) collective-permute-start(bf16[32,3072]{1,0:T(8,128)(2,1)S(1)} %add_convert_fusion.7), channel_id=1, source_target_pairs={{0,2},{1,5},{2,0},{3,7},{4,6},{5,1},{6,4},{7,3},{8,10},{9,13},{10,... | collective-permute-start | bytes 589832 | tf_op jit(solution)/shard_map/ppermute | solution.py:34
  98.8 4.3 %collective-permute-start.18 = (bf16[32,1024]{1,0:T(8,128)(2,1)S(1)}, bf16[32,1024]{1,0:T(8,128)(2,1)S(1)}, u32[]{:S(2)}, u32[]{:S(2)}) collective-permute-start(bf16[32,1024]{1,0:T(8,128)(2,1)S(1)} %add_convert_fusion.11), channel_id=1, source_target_pairs={{0,2},{1,5},{2,0},{3,7},{4,6},{5,1},{6,4},{7,3},{8,10},{9,13},{10,... | collective-permute-start | bytes 196616 | tf_op jit(solution)/shard_map/ppermute | solution.py:34
  (2 other events, 1.9 us)

commit v5 on v4

--- a/solution.py
+++ b/solution.py
@@ -15,7 +15,7 @@
 MIX_VMEM = 35 * 2**20
 MID_VMEM = 24 * 2**20
 FWD_PARTS = (2, 6)
-BWD_PARTS = (4, 3, 1)
+BWD_PARTS = (5, 3)
 
 
 def bounds(width, parts):
@@ -76,15 +76,12 @@
 
 
 def scatter_rows(pieces, totals, own):
-    far, first, count = [], [], len(pieces)
-    for i in range(count + 1):
-        if i < count:
-            if i >= len(totals):
-                totals.append(chip_sums(pieces[i], own, first[-1:]))
-            far.append(swap(totals[i][1], 2))
-        if i > 0:
-            there = once(far[i - 1], totals[i][1]) if i < count else far[i - 1]
-            first.append(add_up(totals[i - 1][0][own:], there[own:]))
+    far, first = [swap(t[1], 2) for t in totals], []
+    first.append(add_up(totals[0][0][own:], far[0][own:]))
+    for piece in pieces[1:]:
+        totals.append(chip_sums(piece, own, first[-1:]))
+        far.append(swap(totals[-1][1], 2))
+        first.append(add_up(totals[-1][0][own:], far[-1][own:]))
     near = [swap(f, 1) for f in first]
     return [add_up(t[:own], f[:own], n) for (t, _), f, n in zip(totals, far, near)], first
 
@@ -469,18 +466,17 @@
         (c, h), after, keys, values, mats, pair, chunks[0], partial, tp, paired
     )
     size = lax.axis_size("ctx")
-    distances = [2**i for i in range(size.bit_length() - 1)] if size & (size - 1) == 0 else []
+    distances = [2**i for i in reversed(range(size.bit_length() - 1))] if size & (size - 1) == 0 else []
     pieces, totals = [piece], []
     grads, weights = (query_grad, keys_grad, values_grad), (query_weight, *pair)
     for i, chunk in enumerate(chunks[1:]):
         ready = []
-        if i == 1 and distances:
-            local_taps = add_pair(local_taps, "ctx", distances.pop(0))
-            ready.append(local_taps)
-        if paired and i > 0:
-            totals.append(chip_sums(pieces[i - 1], own_rows))
+        if paired:
+            totals.append(chip_sums(pieces[i], own_rows))
             ready.append(totals[-1][1])
         pieces.append(project_back(grads, weights, chunk, 2 if paired else 1, ready))
+    if distances:
+        local_taps = add_pair(local_taps, "ctx", distances.pop(0), pieces[-1][0])
     if paired:
         summed, last = scatter_rows(pieces, totals, own_rows)
     else:

time: 105 us -> 103 us (0.981)
  waiting for transfers between devices: 21.6 us -> 26.2 us
  starting transfers between devices: 23.1 us -> 20.3 us
  Pallas kernels: 50.9 us -> 49.2 us
    pallas_call x2 -> x1, Pallas kernels: 12 us -> 8.06 us  [project_back(): pl.pallas_call(kernel, in_specs=[VMEM] * count + [ANYWHERE] * count + [VM...]
    ppermute x16 -> x13, waiting for transfers between devices: 19.1 us -> 22.1 us  [swap(): lax.ppermute(block, 'tp', [(i, i ^ offsets[i % 2]) for i in range(8)])]
    ppermute x16 -> x13, starting transfers between devices: 14.6 us -> 12.2 us  [swap(): lax.ppermute(block, 'tp', [(i, i ^ offsets[i % 2]) for i in range(8)])]
    ppermute x2, waiting for transfers between devices: 0.01 us -> 2.24 us  [add_pair(): theirs = lax.ppermute(mine, axis, route)]
    pallas_call x1, Pallas kernels: 8.09 us -> 9.59 us  [filter_backward(): pl.pallas_call(kernel, in_specs=[VMEM] * 8 + [ANYWHERE] * 2, out_specs=[V...]
  transfers between devices with their start and end apart: 20 -> 17, of which waited for: 11 -> 12; matrix products, arithmetic and copies ran while one was open for 4% -> 4% of each run, Pallas kernels for 30% -> 27%
where the time goes in v5:
time: 103 us
  Pallas kernels  49.2 us (48%)
  waiting for transfers between devices  26.2 us (25%)
  starting transfers between devices  20.3 us (20%)
  local copies, waits for them, and re-layouts  3.94 us (4%)
  other arithmetic  2.64 us (3%)
    pallas_call x3, Pallas kernels, project(): pl.pallas_call(kernel, in_specs=in_specs, out_specs=[VMEM] * len(out_shap...  24 us
    ppermute x13, waiting for transfers between devices, swap(): lax.ppermute(block, 'tp', [(i, i ^ offsets[i % 2]) for i in range(8)])  22.1 us
    ppermute x13, starting transfers between devices, swap(): lax.ppermute(block, 'tp', [(i, i ^ offsets[i % 2]) for i in range(8)])  12.2 us
    pallas_call x1, Pallas kernels, filter_backward(): pl.pallas_call(kernel, in_specs=[VMEM] * 8 + [ANYWHERE] * 2, out_specs=[V...  9.59 us
    pallas_call x1, Pallas kernels, project_back(): pl.pallas_call(kernel, in_specs=[VMEM] * count + [ANYWHERE] * count + [VM...  8.06 us
    pallas_call x1, Pallas kernels, filter_forward(): pl.pallas_call(kernel, in_specs=[VMEM] * 8 + [ANYWHERE], out_specs=[VMEM]...  6.76 us
    ppermute x2, starting transfers between devices, from_behind(): return lax.ppermute(block, axis, route)  5.3 us
    ppermute x2, starting transfers between devices, add_pair(): theirs = lax.ppermute(mine, axis, route)  2.72 us
  transfers between devices with their start and end apart: 17, of which 12 were waited for; matrix products, arithmetic and copies ran while one was open for 4% of the time, Pallas kernels for 27%

profile of v5, /device:TPU:0, one launch (start us, length us, event | category | flops | bytes accessed | tf_op | source)
XLA Modules:
  0.0 103.1 jit_solution(9108056538741919018)
XLA Ops:
  0.6 3.0 %collective-permute-start = (bf16[32,8192]{1,0:T(8,128)(2,1)}, bf16[32,8192]{1,0:T(8,128)(2,1)S(1)}, u32[]{:S(2)}, u32[]{:S(2)}) collective-permute-start(bf16[32,8192]{1,0:T(8,128)(2,1)} %param.9), channel_id=1, source_target_pairs={{0,2},{1,5},{2,0},{3,7},{4,6},{5,1},{6,4},{7,3},{8,10},{9,13},{10,... | collective-permute-start | bytes 1572872 | tf_op jit(solution)/shard_map/ppermute | solution.py:34
  3.6 1.1 %slice.60 = bf16[32,6144]{1,0:T(8,128)(2,1)S(1)} slice(bf16[32,8192]{1,0:T(8,128)(2,1)} %param.9), slice={[0:32], [2048:8192]} | slice | bytes 786432 | tf_op jit(solution)/shard_map/slice | solution.py:73
  8.3 2.7 %collective-permute-done = bf16[32,8192]{1,0:T(8,128)(2,1)S(1)} collective-permute-done((bf16[32,8192]{1,0:T(8,128)(2,1)}, bf16[32,8192]{1,0:T(8,128)(2,1)S(1)}, u32[]{:S(2)}, u32[]{:S(2)}) %collective-permute-start) | collective-permute-done | bytes 524320 | tf_op jit(solution)/shard_map/ppermute | solution.py:34
  11.1 2.1 %collective-permute-start.3 = (bf16[64,2048]{1,0:T(8,128)(2,1)S(1)}, bf16[64,2048]{1,0:T(8,128)(2,1)S(1)}, u32[]{:S(2)}, u32[]{:S(2)}) collective-permute-start(bf16[64,2048]{1,0:T(8,128)(2,1)S(1)} %pad_maximum_fusion.2.refs_0_), channel_id=1, source_target_pairs={{0,4},{1,3},{2,6},{3,1},{4,0},{5,7},{6,2},{7,5},{8,12},{9,11},{10,... | collective-permute-start | bytes 786440 | tf_op jit(solution)/shard_map/ppermute | solution.py:34
  13.4 4.1 %collective-permute-done.3.refs_1_ = bf16[64,2048]{1,0:T(8,128)(2,1)S(1)} collective-permute-done((bf16[64,2048]{1,0:T(8,128)(2,1)S(1)}, bf16[64,2048]{1,0:T(8,128)(2,1)S(1)}, u32[]{:S(2)}, u32[]{:S(2)}) %collective-permute-start.3) | collective-permute-done | bytes 262176 | tf_op jit(solution)/shard_map/ppermute | solution.py:34
  19.1 6.0 %project.3 = (f32[256,1024]{1,0:T(8,128)S(1)}, f32[256,1024]{1,0:T(8,128)S(1)}, f32[256,1024]{1,0:T(8,128)S(1)}) custom-call(bf16[64,2048]{1,0:T(8,128)(2,1)S(1)} %pad_maximum_fusion.2.refs_0_, bf16[64,2048]{1,0:T(8,128)(2,1)S(1)} %collective-permute-done.3.refs_1_, bf16[64,2048]{1,0:T(8,128)(2,1)S(1)} %collective-permute-done.4.refs_2_, ...), custom_call_target="tpu_custom_call" | custom-call | flops 3221225472 | bytes 12582912 | tf_op jit(solution)/shard_map/project/pallas_call | solution.py:221
  26.0 2.3 %collective-permute-done.6.refs_3_ = bf16[64,6144]{1,0:T(8,128)(2,1)S(1)} collective-permute-done((bf16[64,6144]{1,0:T(8,128)(2,1)S(1)}, bf16[64,6144]{1,0:T(8,128)(2,1)S(1)}, u32[]{:S(2)}, u32[]{:S(2)}) %collective-permute-start.6) | collective-permute-done | bytes 786464 | tf_op jit(solution)/shard_map/ppermute | solution.py:34
  28.3 11.5 %project.4 = (bf16[256,1024]{1,0:T(8,128)(2,1)S(1)}, bf16[256,1024]{1,0:T(8,128)(2,1)S(1)}, bf16[256,1024]{1,0:T(8,128)(2,1)S(1)}, bf16[128,1024]{1,0:T(8,128)(2,1)S(1)}) custom-call(bf16[64,6144]{1,0:T(8,128)(2,1)S(1)} %pad_maximum_fusion.refs_0_, bf16[64,6144]{1,0:T(8,128)(2,1)S(1)} %collective-permute-done.1.refs_1_, ...), custom_call_target="tpu_custom_call" | custom-call | flops 6442450944 | bytes 25165824 | tf_op jit(solution)/shard_map/project/pallas_call | solution.py:221
  39.8 4.0 %collective-permute-start.7 = (bf16[128,1024]{1,0:T(8,128)(2,1)S(1)}, bf16[128,1024]{1,0:T(8,128)(2,1)S(1)}, u32[]{:S(2)}, u32[]{:S(2)}) collective-permute-start(bf16[128,1024]{1,0:T(8,128)(2,1)S(1)} %get-tuple-element.39), channel_id=1, source_target_pairs={{0,8},{8,16},{16,24},{1,9},{9,17},{17,25},{2,10},{10,18},{18,26},{... | collective-permute-start | bytes 786440 | tf_op jit(solution)/shard_map/ppermute | solution.py:29
  43.9 6.5 %project.5 = (bf16[256,1024]{1,0:T(8,128)(2,1)S(1)}, bf16[256,1024]{1,0:T(8,128)(2,1)S(1)}, bf16[128,1024]{1,0:T(8,128)(2,1)S(1)}, f32[384,1024]{1,0:T(8,128)S(1)}) custom-call(bf16[64,6144]{1,0:T(8,128)(2,1)S(1)} %pad_maximum_fusion.refs_0_, bf16[64,6144]{1,0:T(8,128)(2,1)S(1)} %collective-permute-done.1.refs_1_, ...), custom_call_target="tpu_custom_call" | custom-call | flops 3221225472 | bytes 12582912 | tf_op jit(solution)/shard_map/project/pallas_call | solution.py:221
  50.4 1.3 %collective-permute-start.8 = (bf16[128,1024]{1,0:T(8,128)(2,1)S(1)}, bf16[128,1024]{1,0:T(8,128)(2,1)S(1)}, u32[]{:S(2)}, u32[]{:S(2)}) collective-permute-start(bf16[128,1024]{1,0:T(8,128)(2,1)S(1)} %get-tuple-element.44), channel_id=1, source_target_pairs={{8,0},{16,8},{24,16},{9,1},{17,9},{25,17},{10,2},{18,10},{26,18},{... | collective-permute-start | bytes 786440 | tf_op jit(solution)/shard_map/ppermute | solution.py:29
  51.7 6.8 %conv.1 = (bf16[256,1024]{1,0:T(8,128)(2,1)}, bf16[256,1024]{1,0:T(8,128)(2,1)S(1)}, bf16[128,1024]{1,0:T(8,128)(2,1)S(1)}, f32[384,1024]{1,0:T(8,128)S(1)}, f32[256,5120]{1,0:T(8,128)S(1)}) custom-call(bf16[1152,128]{1,0:T(8,128)(2,1)S(1)} %copy-done.1, bf16[1920,128]{1,0:T(8,128)(2,1)S(1)} %copy-done.2, f32[384,1024]{1,0:T(8,128)S(1)} %get-tuple-element.38.p_ref, ...), custom_call_target="tpu_custom_call" | custom-call | flops 3758096384 | bytes 14680064 | tf_op jit(solution)/shard_map/conv/pallas_call | solution.py:345
  58.4 1.9 %collective-permute-done.8.refs_4_ = bf16[128,1024]{1,0:T(8,128)(2,1)S(1)} collective-permute-done((bf16[128,1024]{1,0:T(8,128)(2,1)S(1)}, bf16[128,1024]{1,0:T(8,128)(2,1)S(1)}, u32[]{:S(2)}, u32[]{:S(2)}) %collective-permute-start.8) | collective-permute-done | bytes 262176 | tf_op jit(solution)/shard_map/ppermute | solution.py:29
  60.3 9.6 %conv_back.1 = (bf16[128,5120]{1,0:T(8,128)(2,1)S(1)}, bf16[128,5120]{1,0:T(8,128)(2,1)S(1)}, bf16[256,1024]{1,0:T(8,128)(2,1)S(1)}, bf16[256,1024]{1,0:T(8,128)(2,1)S(1)}) custom-call(bf16[1152,128]{1,0:T(8,128)(2,1)S(1)} %copy-done.1, bf16[1920,128]{1,0:T(8,128)(2,1)S(1)} %copy-done.2, f32[384,1024]{1,0:T(8,128)S(1)} %get-tuple-element.43.refs_2_, ...), custom_call_target="tpu_custom_call" | custom-call | flops 6442450944 | bytes 25165824 | tf_op jit(solution)/shard_map/conv_back/pallas_call | solution.py:390
  70.0 2.6 %collective-permute-start.15 = (bf16[128,1024]{1,0:T(8,128)(2,1)S(1)}, bf16[128,1024]{1,0:T(8,128)(2,1)S(1)}, u32[]{:S(2)}, u32[]{:S(2)}) collective-permute-start(bf16[128,1024]{1,0:T(8,128)(2,1)S(1)} %get-tuple-element.56), channel_id=1, source_target_pairs={{0,16},{8,24},{16,0},{24,8},{1,17},{9,25},{17,1},{25,9},{2,18},{10... | collective-permute-start | bytes 786440 | tf_op jit(solution)/shard_map/ppermute | solution.py:64
  73.3 1.6 %collective-permute-start.10 = (bf16[64,5120]{1,0:T(8,128)(2,1)S(1)}, bf16[64,5120]{1,0:T(8,128)(2,1)S(1)}, u32[]{:S(2)}, u32[]{:S(2)}) collective-permute-start(bf16[64,5120]{1,0:T(8,128)(2,1)S(1)} %get-tuple-element.60.refs_6_), channel_id=1, source_target_pairs={{0,4},{1,3},{2,6},{3,1},{4,0},{5,7},{6,2},{7,5},{8,12},{9,11},{10,... | collective-permute-start | bytes 1966088 | tf_op jit(solution)/shard_map/ppermute | solution.py:34
  74.9 8.1 %project_back.1 = (bf16[128,3072]{1,0:T(8,128)(2,1)S(1)}, bf16[128,3072]{1,0:T(8,128)(2,1)S(1)}) custom-call(bf16[256,1024]{1,0:T(8,128)(2,1)S(1)} %get-tuple-element.50.refs_0_, bf16[256,1024]{1,0:T(8,128)(2,1)S(1)} %get-tuple-element.51.refs_1_, bf16[256,1024]{1,0:T(8,128)(2,1)S(1)} %get-tuple-element.52.refs_2_, bf16[8192,1024]{1,0:T(8,128)(2,1)} %refs_3_.1, ...), custom_call_target="tpu_custom_call" | custom-call | flops 4831838208 | bytes 18874368 | tf_op jit(solution)/shard_map/project_back/pallas_call | solution.py:424
  83.0 2.2 %collective-permute-done.15 = bf16[128,1024]{1,0:T(8,128)(2,1)S(1)} collective-permute-done((bf16[128,1024]{1,0:T(8,128)(2,1)S(1)}, bf16[128,1024]{1,0:T(8,128)(2,1)S(1)}, u32[]{:S(2)}, u32[]{:S(2)}) %collective-permute-start.15) | collective-permute-done | bytes 262176 | tf_op jit(solution)/shard_map/ppermute | solution.py:64
  85.5 1.6 %collective-permute-start.11 = (bf16[32,5120]{1,0:T(8,128)(2,1)S(1)}, bf16[32,5120]{1,0:T(8,128)(2,1)S(1)}, u32[]{:S(2)}, u32[]{:S(2)}) collective-permute-start(bf16[32,5120]{1,0:T(8,128)(2,1)S(1)} %add_convert_fusion.5), channel_id=1, source_target_pairs={{0,2},{1,5},{2,0},{3,7},{4,6},{5,1},{6,4},{7,3},{8,10},{9,13},{10,... | collective-permute-start | bytes 983048 | tf_op jit(solution)/shard_map/ppermute | solution.py:34
  87.9 1.6 %collective-permute-start.13 = (bf16[64,3072]{1,0:T(8,128)(2,1)S(1)}, bf16[64,3072]{1,0:T(8,128)(2,1)S(1)}, u32[]{:S(2)}, u32[]{:S(2)}) collective-permute-start(bf16[64,3072]{1,0:T(8,128)(2,1)S(1)} %get-tuple-element.62), channel_id=1, source_target_pairs={{0,4},{1,3},{2,6},{3,1},{4,0},{5,7},{6,2},{7,5},{8,12},{9,11},{10,... | collective-permute-start | bytes 1179656 | tf_op jit(solution)/shard_map/ppermute | solution.py:34
  89.5 5.1 %collective-permute-done.11 = bf16[32,5120]{1,0:T(8,128)(2,1)S(1)} collective-permute-done((bf16[32,5120]{1,0:T(8,128)(2,1)S(1)}, bf16[32,5120]{1,0:T(8,128)(2,1)S(1)}, u32[]{:S(2)}, u32[]{:S(2)}) %collective-permute-start.11) | collective-permute-done | bytes 327712 | tf_op jit(solution)/shard_map/ppermute | solution.py:34
  94.7 1.7 %collective-permute-done.13 = bf16[64,3072]{1,0:T(8,128)(2,1)S(1)} collective-permute-done((bf16[64,3072]{1,0:T(8,128)(2,1)S(1)}, bf16[64,3072]{1,0:T(8,128)(2,1)S(1)}, u32[]{:S(2)}, u32[]{:S(2)}) %collective-permute-start.13) | collective-permute-done | bytes 393248 | tf_op jit(solution)/shard_map/ppermute | solution.py:34
  96.5 1.6 %collective-permute-start.14 = (bf16[32,3072]{1,0:T(8,128)(2,1)S(1)}, bf16[32,3072]{1,0:T(8,128)(2,1)S(1)}, u32[]{:S(2)}, u32[]{:S(2)}) collective-permute-start(bf16[32,3072]{1,0:T(8,128)(2,1)S(1)} %add_convert_fusion.8), channel_id=1, source_target_pairs={{0,2},{1,5},{2,0},{3,7},{4,6},{5,1},{6,4},{7,3},{8,10},{9,13},{10,... | collective-permute-start | bytes 589832 | tf_op jit(solution)/shard_map/ppermute | solution.py:34
  98.9 3.3 %collective-permute-done.14 = bf16[32,3072]{1,0:T(8,128)(2,1)S(1)} collective-permute-done((bf16[32,3072]{1,0:T(8,128)(2,1)S(1)}, bf16[32,3072]{1,0:T(8,128)(2,1)S(1)}, u32[]{:S(2)}, u32[]{:S(2)}) %collective-permute-start.14) | collective-permute-done | bytes 196640 | tf_op jit(solution)/shard_map/ppermute | solution.py:34
  (44 shorter events, 10.1 us)
Async XLA Ops:
  0.6 5.0 %copy-start.4 = (f32[128,1024]{1,0:T(8,128)S(1)}, f32[128,1024]{1,0:T(8,128)}, u32[]{:S(2)}) copy-start(f32[128,1024]{1,0:T(8,128)} %taps_ref.1) | copy-start | bytes 1572868
  0.6 10.4 %collective-permute-start = (bf16[32,8192]{1,0:T(8,128)(2,1)}, bf16[32,8192]{1,0:T(8,128)(2,1)S(1)}, u32[]{:S(2)}, u32[]{:S(2)}) collective-permute-start(bf16[32,8192]{1,0:T(8,128)(2,1)} %param.9), channel_id=1, source_target_pairs={{0,2},{1,5},{2,0},{3,7},{4,6},{5,1},{6,4},{7,3},{8,10},{9,13},{10,... | collective-permute-start | bytes 1572872 | tf_op jit(solution)/shard_map/ppermute | solution.py:34
  5.6 1.0 copy-start
  6.6 1.0 copy-start.5
  11.1 6.5 %collective-permute-start.3 = (bf16[64,2048]{1,0:T(8,128)(2,1)S(1)}, bf16[64,2048]{1,0:T(8,128)(2,1)S(1)}, u32[]{:S(2)}, u32[]{:S(2)}) collective-permute-start(bf16[64,2048]{1,0:T(8,128)(2,1)S(1)} %pad_maximum_fusion.2.refs_0_), channel_id=1, source_target_pairs={{0,4},{1,3},{2,6},{3,1},{4,0},{5,7},{6,2},{7,5},{8,12},{9,11},{10,... | collective-permute-start | bytes 786440 | tf_op jit(solution)/shard_map/ppermute | solution.py:34
  13.3 12.7 %collective-permute-start.1 = (bf16[64,6144]{1,0:T(8,128)(2,1)S(1)}, bf16[64,6144]{1,0:T(8,128)(2,1)S(1)}, u32[]{:S(2)}, u32[]{:S(2)}) collective-permute-start(bf16[64,6144]{1,0:T(8,128)(2,1)S(1)} %pad_maximum_fusion.refs_0_), channel_id=1, source_target_pairs={{0,4},{1,3},{2,6},{3,1},{4,0},{5,7},{6,2},{7,5},{8,12},{9,11},{10,... | collective-permute-start | bytes 2359304 | tf_op jit(solution)/shard_map/ppermute | solution.py:34
  13.3 4.7 %collective-permute-start.4 = (bf16[64,2048]{1,0:T(8,128)(2,1)S(1)}, bf16[64,2048]{1,0:T(8,128)(2,1)S(1)}, u32[]{:S(2)}, u32[]{:S(2)}) collective-permute-start(bf16[64,2048]{1,0:T(8,128)(2,1)S(1)} %pad_maximum_fusion.2.refs_0_), channel_id=1, source_target_pairs={{0,1},{1,0},{2,3},{3,2},{4,5},{5,4},{6,7},{7,6},{8,9},{9,8},{10,11... | collective-permute-start | bytes 786440 | tf_op jit(solution)/shard_map/ppermute | solution.py:34
  17.6 1.5 %collective-permute-start.5 = (bf16[64,2048]{1,0:T(8,128)(2,1)S(1)}, bf16[64,2048]{1,0:T(8,128)(2,1)S(1)}, u32[]{:S(2)}, u32[]{:S(2)}) collective-permute-start(bf16[64,2048]{1,0:T(8,128)(2,1)S(1)} %collective-permute-done.3.refs_1_), channel_id=1, source_target_pairs={{0,1},{1,0},{2,3},{3,2},{4,5},{5,4},{6,7},{7,6},{8,9},{9,8},{10,11... | collective-permute-start | bytes 786440 | tf_op jit(solution)/shard_map/ppermute | solution.py:34
  17.6 8.4 %collective-permute-start.2 = (bf16[64,6144]{1,0:T(8,128)(2,1)S(1)}, bf16[64,6144]{1,0:T(8,128)(2,1)S(1)}, u32[]{:S(2)}, u32[]{:S(2)}) collective-permute-start(bf16[64,6144]{1,0:T(8,128)(2,1)S(1)} %pad_maximum_fusion.refs_0_), channel_id=1, source_target_pairs={{0,1},{1,0},{2,3},{3,2},{4,5},{5,4},{6,7},{7,6},{8,9},{9,8},{10,11... | collective-permute-start | bytes 2359304 | tf_op jit(solution)/shard_map/ppermute | solution.py:34
  26.0 2.3 %collective-permute-start.6 = (bf16[64,6144]{1,0:T(8,128)(2,1)S(1)}, bf16[64,6144]{1,0:T(8,128)(2,1)S(1)}, u32[]{:S(2)}, u32[]{:S(2)}) collective-permute-start(bf16[64,6144]{1,0:T(8,128)(2,1)S(1)} %collective-permute-done.1.refs_1_), channel_id=1, source_target_pairs={{0,1},{1,0},{2,3},{3,2},{4,5},{5,4},{6,7},{7,6},{8,9},{9,8},{10,11... | collective-permute-start | bytes 2359304 | tf_op jit(solution)/shard_map/ppermute | solution.py:34
  28.3 15.6 %copy-start.1 = (bf16[1152,128]{1,0:T(8,128)(2,1)S(1)}, bf16[1152,128]{1,0:T(8,128)(2,1)}, u32[]{:S(2)}) copy-start(bf16[1152,128]{1,0:T(8,128)(2,1)} %constant.6.clone.high_ref.refs_8_.there.refs_0_) | copy-start | bytes 884740
  28.3 15.6 %copy-start.2 = (bf16[1920,128]{1,0:T(8,128)(2,1)S(1)}, bf16[1920,128]{1,0:T(8,128)(2,1)}, u32[]{:S(2)}) copy-start(bf16[1920,128]{1,0:T(8,128)(2,1)} %constant.8.clone.refs_9_.back.refs_1_) | copy-start | bytes 1474564
  28.3 15.6 %copy-start.3 = (bf16[256,1024]{1,0:T(8,128)(2,1)S(1)}, bf16[256,1024]{1,0:T(8,128)(2,1)}, u32[]{:S(2)}) copy-start(bf16[256,1024]{1,0:T(8,128)(2,1)} %grad_ref.1) | copy-start | bytes 1572868
  39.8 11.9 %collective-permute-start.7 = (bf16[128,1024]{1,0:T(8,128)(2,1)S(1)}, bf16[128,1024]{1,0:T(8,128)(2,1)S(1)}, u32[]{:S(2)}, u32[]{:S(2)}) collective-permute-start(bf16[128,1024]{1,0:T(8,128)(2,1)S(1)} %get-tuple-element.39), channel_id=1, source_target_pairs={{0,8},{8,16},{16,24},{1,9},{9,17},{17,25},{2,10},{10,18},{18,26},{... | collective-permute-start | bytes 786440 | tf_op jit(solution)/shard_map/ppermute | solution.py:29
  50.4 9.9 %collective-permute-start.8 = (bf16[128,1024]{1,0:T(8,128)(2,1)S(1)}, bf16[128,1024]{1,0:T(8,128)(2,1)S(1)}, u32[]{:S(2)}, u32[]{:S(2)}) collective-permute-start(bf16[128,1024]{1,0:T(8,128)(2,1)S(1)} %get-tuple-element.44), channel_id=1, source_target_pairs={{8,0},{16,8},{24,16},{9,1},{17,9},{25,17},{10,2},{18,10},{26,18},{... | collective-permute-start | bytes 786440 | tf_op jit(solution)/shard_map/ppermute | solution.py:29
  69.9 3.1 %collective-permute-start.9 = (bf16[128,5120]{1,0:T(8,128)(2,1)S(1)}, bf16[128,5120]{1,0:T(8,128)(2,1)S(1)}, u32[]{:S(2)}, u32[]{:S(2)}) collective-permute-start(bf16[128,5120]{1,0:T(8,128)(2,1)S(1)} %get-tuple-element.49), channel_id=1, source_target_pairs={{0,1},{1,0},{2,3},{3,2},{4,5},{5,4},{6,7},{7,6},{8,9},{9,8},{10,11... | collective-permute-start | bytes 3932168 | tf_op jit(solution)/shard_map/ppermute | solution.py:34
  70.0 15.2 %collective-permute-start.15 = (bf16[128,1024]{1,0:T(8,128)(2,1)S(1)}, bf16[128,1024]{1,0:T(8,128)(2,1)S(1)}, u32[]{:S(2)}, u32[]{:S(2)}) collective-permute-start(bf16[128,1024]{1,0:T(8,128)(2,1)S(1)} %get-tuple-element.56), channel_id=1, source_target_pairs={{0,16},{8,24},{16,0},{24,8},{1,17},{9,25},{17,1},{25,9},{2,18},{10... | collective-permute-start | bytes 786440 | tf_op jit(solution)/shard_map/ppermute | solution.py:64
  73.3 12.1 %collective-permute-start.10 = (bf16[64,5120]{1,0:T(8,128)(2,1)S(1)}, bf16[64,5120]{1,0:T(8,128)(2,1)S(1)}, u32[]{:S(2)}, u32[]{:S(2)}) collective-permute-start(bf16[64,5120]{1,0:T(8,128)(2,1)S(1)} %get-tuple-element.60.refs_6_), channel_id=1, source_target_pairs={{0,4},{1,3},{2,6},{3,1},{4,0},{5,7},{6,2},{7,5},{8,12},{9,11},{10,... | collective-permute-start | bytes 1966088 | tf_op jit(solution)/shard_map/ppermute | solution.py:34
  85.3 12.7 %collective-permute-start.16 = (bf16[128,1024]{1,0:T(8,128)(2,1)S(1)}, bf16[128,1024]{1,0:T(8,128)(2,1)S(1)}, u32[]{:S(2)}, u32[]{:S(2)}) collective-permute-start(bf16[128,1024]{1,0:T(8,128)(2,1)S(1)} %add_convert_fusion.6), channel_id=1, source_target_pairs={{0,8},{8,0},{16,24},{24,16},{1,9},{9,1},{17,25},{25,17},{2,10},{10... | collective-permute-start | bytes 786440 | tf_op jit(solution)/shard_map/ppermute | solution.py:64
  85.4 2.4 %collective-permute-start.12 = (bf16[128,3072]{1,0:T(8,128)(2,1)S(1)}, bf16[128,3072]{1,0:T(8,128)(2,1)S(1)}, u32[]{:S(2)}, u32[]{:S(2)}) collective-permute-start(bf16[128,3072]{1,0:T(8,128)(2,1)S(1)} %get-tuple-element.54), channel_id=1, source_target_pairs={{0,1},{1,0},{2,3},{3,2},{4,5},{5,4},{6,7},{7,6},{8,9},{9,8},{10,11... | collective-permute-start | bytes 2359304 | tf_op jit(solution)/shard_map/ppermute | solution.py:34
  85.5 9.0 %collective-permute-start.11 = (bf16[32,5120]{1,0:T(8,128)(2,1)S(1)}, bf16[32,5120]{1,0:T(8,128)(2,1)S(1)}, u32[]{:S(2)}, u32[]{:S(2)}) collective-permute-start(bf16[32,5120]{1,0:T(8,128)(2,1)S(1)} %add_convert_fusion.5), channel_id=1, source_target_pairs={{0,2},{1,5},{2,0},{3,7},{4,6},{5,1},{6,4},{7,3},{8,10},{9,13},{10,... | collective-permute-start | bytes 983048 | tf_op jit(solution)/shard_map/ppermute | solution.py:34
  87.9 8.5 %collective-permute-start.13 = (bf16[64,3072]{1,0:T(8,128)(2,1)S(1)}, bf16[64,3072]{1,0:T(8,128)(2,1)S(1)}, u32[]{:S(2)}, u32[]{:S(2)}) collective-permute-start(bf16[64,3072]{1,0:T(8,128)(2,1)S(1)} %get-tuple-element.62), channel_id=1, source_target_pairs={{0,4},{1,3},{2,6},{3,1},{4,0},{5,7},{6,2},{7,5},{8,12},{9,11},{10,... | collective-permute-start | bytes 1179656 | tf_op jit(solution)/shard_map/ppermute | solution.py:34
  96.5 5.7 %collective-permute-start.14 = (bf16[32,3072]{1,0:T(8,128)(2,1)S(1)}, bf16[32,3072]{1,0:T(8,128)(2,1)S(1)}, u32[]{:S(2)}, u32[]{:S(2)}) collective-permute-start(bf16[32,3072]{1,0:T(8,128)(2,1)S(1)} %add_convert_fusion.8), channel_id=1, source_target_pairs={{0,2},{1,5},{2,0},{3,7},{4,6},{5,1},{6,4},{7,3},{8,10},{9,13},{10,... | collective-permute-start | bytes 589832 | tf_op jit(solution)/shard_map/ppermute | solution.py:34

commit v6 on v5

--- a/solution.py
+++ b/solution.py
@@ -369,7 +369,8 @@
 
         def compute(k, slot):
             at = pl.ds(pl.multiple_of(k * step, step), step)
-            total = partial_ref[:, at] + contract(kg_ref[...], w_buf[slot, 0]) + contract(vg_ref[...], w_buf[slot, 1])
+            seen = pl.ds(pl.multiple_of(start + k * step, step), step)
+            total = partial_ref[:, seen] + contract(kg_ref[...], w_buf[slot, 0]) + contract(vg_ref[...], w_buf[slot, 1])
             for i in range(parts):
                 out_refs[i][:, at] = total[i * share : (i + 1) * share].astype(BF16)
 
@@ -399,22 +400,22 @@
     )(*mats, *spectra, after, keys, values, partial, *weights)
 
 
-def project_back(grads, weights, chunk, parts, ready):
+def project_back(grads, weights, chunk, partial, parts, ready):
     rows, group = grads[0].shape
     count = len(grads)
     start, depth = chunk[0], chunk[1] - chunk[0]
     step = step_rows(depth, count)
     share = rows // parts
-    n_in = 2 * count + len(ready)
+    n_in = 2 * count + 1 + len(ready)
 
     def kernel(*refs):
-        g_refs, w_refs = refs[:count], refs[count : 2 * count]
+        g_refs, w_refs, partial_ref = refs[:count], refs[count : 2 * count], refs[2 * count]
         out_refs, (w_buf, w_sem) = refs[n_in : n_in + parts], refs[n_in + parts :]
 
         def compute(k, slot):
             at = pl.ds(pl.multiple_of(k * step, step), step)
-            total = contract(g_refs[0][...], w_buf[slot, 0])
-            for m in range(1, count):
+            total = partial_ref[:, pl.ds(pl.multiple_of(start + k * step, step), step)]
+            for m in range(count):
                 total = total + contract(g_refs[m][...], w_buf[slot, m])
             for i in range(parts):
                 out_refs[i][:, at] = total[i * share : (i + 1) * share].astype(BF16)
@@ -423,14 +424,14 @@
 
     return pl.pallas_call(
         kernel,
-        in_specs=[VMEM] * count + [ANYWHERE] * count + [VMEM] * len(ready),
+        in_specs=[VMEM] * count + [ANYWHERE] * count + [VMEM] * (1 + len(ready)),
         out_specs=[VMEM] * parts,
         out_shape=[jax.ShapeDtypeStruct((share, depth), BF16)] * parts,
         scratch_shapes=weight_scratch(count, step, group),
         compiler_params=pltpu.CompilerParams(vmem_limit_bytes=BWD_VMEM),
         cost_estimate=matmul_cost(rows, depth, group, count),
         name="project_back",
-    )(*grads, *weights, *ready)
+    )(*grads, *weights, partial, *ready)
 
 
 def on_device(inputs, query_weight, key_weight, value_weight, filter_taps, out_grad):
@@ -460,7 +461,7 @@
     after = from_behind(head, "ctx", -1)
     chunks = bounds(width, BWD_PARTS)
     mixed, query_grad, local_taps, c, partial = filter_forward(
-        (p, h), before, query, conv_in_grad, out_grad, mats, query_weight, chunks[0], tp, paired
+        (p, h), before, query, conv_in_grad, out_grad, mats, query_weight, (0, width), tp, paired
     )
     *piece, keys_grad, values_grad = filter_backward(
         (c, h), after, keys, values, mats, pair, chunks[0], partial, tp, paired
@@ -468,17 +469,17 @@
     size = lax.axis_size("ctx")
     distances = [2**i for i in reversed(range(size.bit_length() - 1))] if size & (size - 1) == 0 else []
     pieces, totals = [piece], []
-    grads, weights = (query_grad, keys_grad, values_grad), (query_weight, *pair)
+    grads = (keys_grad, values_grad)
     for i, chunk in enumerate(chunks[1:]):
         ready = []
         if paired:
             totals.append(chip_sums(pieces[i], own_rows))
             ready.append(totals[-1][1])
-        pieces.append(project_back(grads, weights, chunk, 2 if paired else 1, ready))
-    if distances:
-        local_taps = add_pair(local_taps, "ctx", distances.pop(0), pieces[-1][0])
+        pieces.append(project_back(grads, pair, chunk, partial, 2 if paired else 1, ready))
     if paired:
         summed, last = scatter_rows(pieces, totals, own_rows)
+        if len(distances) > 1:
+            local_taps = add_pair(local_taps, "ctx", distances.pop(0), totals[-1][1])
     else:
         summed = [lax.psum_scatter(p, "tp", scatter_dimension=0, tiled=True) for (p,) in pieces]
         last = summed

time: 103 us -> 103 us (level)
  waiting for transfers between devices: 26.2 us -> 24.8 us
    pallas_call x1, Pallas kernels: 6.76 us -> 8.66 us  [filter_forward(): pl.pallas_call(kernel, in_specs=[VMEM] * 8 + [ANYWHERE], out_specs=[VMEM]...]
    ppermute x2, waiting for transfers between devices: 1.87 us -> 0.01 us  [from_behind(): return lax.ppermute(block, axis, route)]
    pallas_call x1, Pallas kernels: 8.06 us -> 6.31 us  [project_back(): pl.pallas_call(kernel, in_specs=[VMEM] * count + [ANYWHERE] * count + [VM...]
    ppermute x2, starting transfers between devices: 2.72 us -> 4.45 us  [add_pair(): theirs = lax.ppermute(mine, axis, route)]
  transfers between devices with their start and end apart: 17 -> 17, of which waited for: 12 -> 12; matrix products, arithmetic and copies ran while one was open for 4% -> 3% of each run, Pallas kernels for 27% -> 27%
where the time goes in v6:
time: 103 us
  Pallas kernels  49.3 us (48%)
  waiting for transfers between devices  24.8 us (24%)
  starting transfers between devices  21.1 us (20%)
  local copies, waits for them, and re-layouts  3.94 us (4%)
  other arithmetic  2.64 us (3%)
    pallas_call x3, Pallas kernels, project(): pl.pallas_call(kernel, in_specs=in_specs, out_specs=[VMEM] * len(out_shap...  24 us
    ppermute x13, waiting for transfers between devices, swap(): lax.ppermute(block, 'tp', [(i, i ^ offsets[i % 2]) for i in range(8)])  22 us
    ppermute x13, starting transfers between devices, swap(): lax.ppermute(block, 'tp', [(i, i ^ offsets[i % 2]) for i in range(8)])  11.3 us
    pallas_call x1, Pallas kernels, filter_backward(): pl.pallas_call(kernel, in_specs=[VMEM] * 8 + [ANYWHERE] * 2, out_specs=[V...  9.59 us
    pallas_call x1, Pallas kernels, filter_forward(): pl.pallas_call(kernel, in_specs=[VMEM] * 8 + [ANYWHERE], out_specs=[VMEM]...  8.66 us
    pallas_call x1, Pallas kernels, project_back(): pl.pallas_call(kernel, in_specs=[VMEM] * count + [ANYWHERE] * count + [VM...  6.31 us
    ppermute x2, starting transfers between devices, from_behind(): return lax.ppermute(block, axis, route)  5.3 us
    ppermute x2, starting transfers between devices, add_pair(): theirs = lax.ppermute(mine, axis, route)  4.45 us
  transfers between devices with their start and end apart: 17, of which 12 were waited for; matrix products, arithmetic and copies ran while one was open for 3% of the time, Pallas kernels for 27%

profile of v6, /device:TPU:0, one launch (start us, length us, event | category | flops | bytes accessed | tf_op | source)
XLA Modules:
  0.0 102.7 jit_solution(7014531486928650723)
XLA Ops:
  0.6 3.0 %collective-permute-start = (bf16[32,8192]{1,0:T(8,128)(2,1)}, bf16[32,8192]{1,0:T(8,128)(2,1)S(1)}, u32[]{:S(2)}, u32[]{:S(2)}) collective-permute-start(bf16[32,8192]{1,0:T(8,128)(2,1)} %param.9), channel_id=1, source_target_pairs={{0,2},{1,5},{2,0},{3,7},{4,6},{5,1},{6,4},{7,3},{8,10},{9,13},{10,... | collective-permute-start | bytes 1572872 | tf_op jit(solution)/shard_map/ppermute | solution.py:34
  3.6 1.1 %slice.60 = bf16[32,6144]{1,0:T(8,128)(2,1)S(1)} slice(bf16[32,8192]{1,0:T(8,128)(2,1)} %param.9), slice={[0:32], [2048:8192]} | slice | bytes 786432 | tf_op jit(solution)/shard_map/slice | solution.py:73
  8.3 2.7 %collective-permute-done = bf16[32,8192]{1,0:T(8,128)(2,1)S(1)} collective-permute-done((bf16[32,8192]{1,0:T(8,128)(2,1)}, bf16[32,8192]{1,0:T(8,128)(2,1)S(1)}, u32[]{:S(2)}, u32[]{:S(2)}) %collective-permute-start) | collective-permute-done | bytes 524320 | tf_op jit(solution)/shard_map/ppermute | solution.py:34
  11.1 2.1 %collective-permute-start.3 = (bf16[64,2048]{1,0:T(8,128)(2,1)S(1)}, bf16[64,2048]{1,0:T(8,128)(2,1)S(1)}, u32[]{:S(2)}, u32[]{:S(2)}) collective-permute-start(bf16[64,2048]{1,0:T(8,128)(2,1)S(1)} %pad_maximum_fusion.2.refs_0_), channel_id=1, source_target_pairs={{0,4},{1,3},{2,6},{3,1},{4,0},{5,7},{6,2},{7,5},{8,12},{9,11},{10,... | collective-permute-start | bytes 786440 | tf_op jit(solution)/shard_map/ppermute | solution.py:34
  13.4 4.1 %collective-permute-done.3.refs_1_ = bf16[64,2048]{1,0:T(8,128)(2,1)S(1)} collective-permute-done((bf16[64,2048]{1,0:T(8,128)(2,1)S(1)}, bf16[64,2048]{1,0:T(8,128)(2,1)S(1)}, u32[]{:S(2)}, u32[]{:S(2)}) %collective-permute-start.3) | collective-permute-done | bytes 262176 | tf_op jit(solution)/shard_map/ppermute | solution.py:34
  18.1 1.0 collective-permute-done.5.refs_3_
  19.1 6.0 %project.3 = (f32[256,1024]{1,0:T(8,128)S(1)}, f32[256,1024]{1,0:T(8,128)S(1)}, f32[256,1024]{1,0:T(8,128)S(1)}) custom-call(bf16[64,2048]{1,0:T(8,128)(2,1)S(1)} %pad_maximum_fusion.2.refs_0_, bf16[64,2048]{1,0:T(8,128)(2,1)S(1)} %collective-permute-done.3.refs_1_, bf16[64,2048]{1,0:T(8,128)(2,1)S(1)} %collective-permute-done.4.refs_2_, ...), custom_call_target="tpu_custom_call" | custom-call | flops 3221225472 | bytes 12582912 | tf_op jit(solution)/shard_map/project/pallas_call | solution.py:221
  26.0 2.3 %collective-permute-done.6.refs_3_ = bf16[64,6144]{1,0:T(8,128)(2,1)S(1)} collective-permute-done((bf16[64,6144]{1,0:T(8,128)(2,1)S(1)}, bf16[64,6144]{1,0:T(8,128)(2,1)S(1)}, u32[]{:S(2)}, u32[]{:S(2)}) %collective-permute-start.6) | collective-permute-done | bytes 786464 | tf_op jit(solution)/shard_map/ppermute | solution.py:34
  28.3 11.5 %project.4 = (bf16[256,1024]{1,0:T(8,128)(2,1)S(1)}, bf16[256,1024]{1,0:T(8,128)(2,1)S(1)}, bf16[256,1024]{1,0:T(8,128)(2,1)S(1)}, bf16[128,1024]{1,0:T(8,128)(2,1)S(1)}) custom-call(bf16[64,6144]{1,0:T(8,128)(2,1)S(1)} %pad_maximum_fusion.refs_0_, bf16[64,6144]{1,0:T(8,128)(2,1)S(1)} %collective-permute-done.1.refs_1_, ...), custom_call_target="tpu_custom_call" | custom-call | flops 6442450944 | bytes 25165824 | tf_op jit(solution)/shard_map/project/pallas_call | solution.py:221
  39.8 4.0 %collective-permute-start.7 = (bf16[128,1024]{1,0:T(8,128)(2,1)S(1)}, bf16[128,1024]{1,0:T(8,128)(2,1)S(1)}, u32[]{:S(2)}, u32[]{:S(2)}) collective-permute-start(bf16[128,1024]{1,0:T(8,128)(2,1)S(1)} %get-tuple-element.38), channel_id=1, source_target_pairs={{0,8},{8,16},{16,24},{1,9},{9,17},{17,25},{2,10},{10,18},{18,26},{... | collective-permute-start | bytes 786440 | tf_op jit(solution)/shard_map/ppermute | solution.py:29
  43.9 6.5 %project.5 = (bf16[256,1024]{1,0:T(8,128)(2,1)S(1)}, bf16[256,1024]{1,0:T(8,128)(2,1)S(1)}, bf16[128,1024]{1,0:T(8,128)(2,1)S(1)}, f32[384,1024]{1,0:T(8,128)S(1)}) custom-call(bf16[64,6144]{1,0:T(8,128)(2,1)S(1)} %pad_maximum_fusion.refs_0_, bf16[64,6144]{1,0:T(8,128)(2,1)S(1)} %collective-permute-done.1.refs_1_, ...), custom_call_target="tpu_custom_call" | custom-call | flops 3221225472 | bytes 12582912 | tf_op jit(solution)/shard_map/project/pallas_call | solution.py:221
  50.4 1.3 %collective-permute-start.8 = (bf16[128,1024]{1,0:T(8,128)(2,1)S(1)}, bf16[128,1024]{1,0:T(8,128)(2,1)S(1)}, u32[]{:S(2)}, u32[]{:S(2)}) collective-permute-start(bf16[128,1024]{1,0:T(8,128)(2,1)S(1)} %get-tuple-element.43), channel_id=1, source_target_pairs={{8,0},{16,8},{24,16},{9,1},{17,9},{25,17},{10,2},{18,10},{26,18},{... | collective-permute-start | bytes 786440 | tf_op jit(solution)/shard_map/ppermute | solution.py:29
  51.7 8.7 %conv.1 = (bf16[256,1024]{1,0:T(8,128)(2,1)}, bf16[256,1024]{1,0:T(8,128)(2,1)}, bf16[128,1024]{1,0:T(8,128)(2,1)S(1)}, f32[384,1024]{1,0:T(8,128)S(1)}, f32[256,8192]{1,0:T(8,128)S(1)}) custom-call(bf16[1152,128]{1,0:T(8,128)(2,1)S(1)} %copy-done.1, bf16[1920,128]{1,0:T(8,128)(2,1)S(1)} %copy-done.2, f32[384,1024]{1,0:T(8,128)S(1)} %get-tuple-element.37.p_ref, ...), custom_call_target="tpu_custom_call" | custom-call | flops 5368709120 | bytes 20971520 | tf_op jit(solution)/shard_map/conv/pallas_call | solution.py:345
  60.3 9.6 %conv_back.1 = (bf16[128,5120]{1,0:T(8,128)(2,1)S(1)}, bf16[128,5120]{1,0:T(8,128)(2,1)S(1)}, bf16[256,1024]{1,0:T(8,128)(2,1)S(1)}, bf16[256,1024]{1,0:T(8,128)(2,1)S(1)}) custom-call(bf16[1152,128]{1,0:T(8,128)(2,1)S(1)} %copy-done.1, bf16[1920,128]{1,0:T(8,128)(2,1)S(1)} %copy-done.2, f32[384,1024]{1,0:T(8,128)S(1)} %get-tuple-element.42.refs_2_, ...), custom_call_target="tpu_custom_call" | custom-call | flops 6442450944 | bytes 25165824 | tf_op jit(solution)/shard_map/conv_back/pallas_call | solution.py:391
  70.0 3.0 %collective-permute-done.9 = bf16[128,5120]{1,0:T(8,128)(2,1)S(1)} collective-permute-done((bf16[128,5120]{1,0:T(8,128)(2,1)S(1)}, bf16[128,5120]{1,0:T(8,128)(2,1)S(1)}, u32[]{:S(2)}, u32[]{:S(2)}) %collective-permute-start.9) | collective-permute-done | bytes 1310752 | tf_op jit(solution)/shard_map/ppermute | solution.py:34
  73.4 1.6 %collective-permute-start.10 = (bf16[64,5120]{1,0:T(8,128)(2,1)S(1)}, bf16[64,5120]{1,0:T(8,128)(2,1)S(1)}, u32[]{:S(2)}, u32[]{:S(2)}) collective-permute-start(bf16[64,5120]{1,0:T(8,128)(2,1)S(1)} %get-tuple-element.58.refs_5_), channel_id=1, source_target_pairs={{0,4},{1,3},{2,6},{3,1},{4,0},{5,7},{6,2},{7,5},{8,12},{9,11},{10,... | collective-permute-start | bytes 1966088 | tf_op jit(solution)/shard_map/ppermute | solution.py:34
  74.9 3.7 %collective-permute-start.15 = (bf16[128,1024]{1,0:T(8,128)(2,1)S(1)}, bf16[128,1024]{1,0:T(8,128)(2,1)S(1)}, u32[]{:S(2)}, u32[]{:S(2)}) collective-permute-start(bf16[128,1024]{1,0:T(8,128)(2,1)S(1)} %get-tuple-element.54), channel_id=1, source_target_pairs={{0,16},{8,24},{16,0},{24,8},{1,17},{9,25},{17,1},{25,9},{2,18},{10... | collective-permute-start | bytes 786440 | tf_op jit(solution)/shard_map/ppermute | solution.py:64
  78.6 6.3 %project_back.1 = (bf16[128,3072]{1,0:T(8,128)(2,1)S(1)}, bf16[128,3072]{1,0:T(8,128)(2,1)S(1)}) custom-call(bf16[256,1024]{1,0:T(8,128)(2,1)S(1)} %get-tuple-element.49.refs_0_, bf16[256,1024]{1,0:T(8,128)(2,1)S(1)} %get-tuple-element.50.refs_1_, bf16[8192,1024]{1,0:T(8,128)(2,1)} %refs_2_.1, bf16[8192,1024]{1,0:T(8,128)(2,1)} %refs_3_.1, ...), custom_call_target="tpu_custom_call" | custom-call | flops 3221225472 | bytes 12582912 | tf_op jit(solution)/shard_map/project_back/pallas_call | solution.py:425
  85.1 1.5 %collective-permute-start.11 = (bf16[32,5120]{1,0:T(8,128)(2,1)S(1)}, bf16[32,5120]{1,0:T(8,128)(2,1)S(1)}, u32[]{:S(2)}, u32[]{:S(2)}) collective-permute-start(bf16[32,5120]{1,0:T(8,128)(2,1)S(1)} %add_convert_fusion.5), channel_id=1, source_target_pairs={{0,2},{1,5},{2,0},{3,7},{4,6},{5,1},{6,4},{7,3},{8,10},{9,13},{10,... | collective-permute-start | bytes 983048 | tf_op jit(solution)/shard_map/ppermute | solution.py:34
  88.2 2.3 %collective-permute-done.15 = bf16[128,1024]{1,0:T(8,128)(2,1)S(1)} collective-permute-done((bf16[128,1024]{1,0:T(8,128)(2,1)S(1)}, bf16[128,1024]{1,0:T(8,128)(2,1)S(1)}, u32[]{:S(2)}, u32[]{:S(2)}) %collective-permute-start.15) | collective-permute-done | bytes 262176 | tf_op jit(solution)/shard_map/ppermute | solution.py:64
  91.3 2.8 %collective-permute-done.11 = bf16[32,5120]{1,0:T(8,128)(2,1)S(1)} collective-permute-done((bf16[32,5120]{1,0:T(8,128)(2,1)S(1)}, bf16[32,5120]{1,0:T(8,128)(2,1)S(1)}, u32[]{:S(2)}, u32[]{:S(2)}) %collective-permute-start.11) | collective-permute-done | bytes 327712 | tf_op jit(solution)/shard_map/ppermute | solution.py:34
  94.3 1.7 %collective-permute-done.13 = bf16[64,3072]{1,0:T(8,128)(2,1)S(1)} collective-permute-done((bf16[64,3072]{1,0:T(8,128)(2,1)S(1)}, bf16[64,3072]{1,0:T(8,128)(2,1)S(1)}, u32[]{:S(2)}, u32[]{:S(2)}) %collective-permute-start.13) | collective-permute-done | bytes 393248 | tf_op jit(solution)/shard_map/ppermute | solution.py:34
  96.0 1.5 %collective-permute-start.14 = (bf16[32,3072]{1,0:T(8,128)(2,1)S(1)}, bf16[32,3072]{1,0:T(8,128)(2,1)S(1)}, u32[]{:S(2)}, u32[]{:S(2)}) collective-permute-start(bf16[32,3072]{1,0:T(8,128)(2,1)S(1)} %add_convert_fusion.8), channel_id=1, source_target_pairs={{0,2},{1,5},{2,0},{3,7},{4,6},{5,1},{6,4},{7,3},{8,10},{9,13},{10,... | collective-permute-start | bytes 589832 | tf_op jit(solution)/shard_map/ppermute | solution.py:34
  98.9 2.8 %collective-permute-done.14 = bf16[32,3072]{1,0:T(8,128)(2,1)S(1)} collective-permute-done((bf16[32,3072]{1,0:T(8,128)(2,1)S(1)}, bf16[32,3072]{1,0:T(8,128)(2,1)S(1)}, u32[]{:S(2)}, u32[]{:S(2)}) %collective-permute-start.14) | collective-permute-done | bytes 196640 | tf_op jit(solution)/shard_map/ppermute | solution.py:34
  (44 shorter events, 10.7 us)
Async XLA Ops:
  0.6 5.0 %copy-start.4 = (f32[128,1024]{1,0:T(8,128)S(1)}, f32[128,1024]{1,0:T(8,128)}, u32[]{:S(2)}) copy-start(f32[128,1024]{1,0:T(8,128)} %taps_ref.1) | copy-start | bytes 1572868
  0.6 10.4 %collective-permute-start = (bf16[32,8192]{1,0:T(8,128)(2,1)}, bf16[32,8192]{1,0:T(8,128)(2,1)S(1)}, u32[]{:S(2)}, u32[]{:S(2)}) collective-permute-start(bf16[32,8192]{1,0:T(8,128)(2,1)} %param.9), channel_id=1, source_target_pairs={{0,2},{1,5},{2,0},{3,7},{4,6},{5,1},{6,4},{7,3},{8,10},{9,13},{10,... | collective-permute-start | bytes 1572872 | tf_op jit(solution)/shard_map/ppermute | solution.py:34
  5.6 1.0 copy-start
  6.6 1.0 copy-start.5
  11.1 6.5 %collective-permute-start.3 = (bf16[64,2048]{1,0:T(8,128)(2,1)S(1)}, bf16[64,2048]{1,0:T(8,128)(2,1)S(1)}, u32[]{:S(2)}, u32[]{:S(2)}) collective-permute-start(bf16[64,2048]{1,0:T(8,128)(2,1)S(1)} %pad_maximum_fusion.2.refs_0_), channel_id=1, source_target_pairs={{0,4},{1,3},{2,6},{3,1},{4,0},{5,7},{6,2},{7,5},{8,12},{9,11},{10,... | collective-permute-start | bytes 786440 | tf_op jit(solution)/shard_map/ppermute | solution.py:34
  13.3 12.7 %collective-permute-start.1 = (bf16[64,6144]{1,0:T(8,128)(2,1)S(1)}, bf16[64,6144]{1,0:T(8,128)(2,1)S(1)}, u32[]{:S(2)}, u32[]{:S(2)}) collective-permute-start(bf16[64,6144]{1,0:T(8,128)(2,1)S(1)} %pad_maximum_fusion.refs_0_), channel_id=1, source_target_pairs={{0,4},{1,3},{2,6},{3,1},{4,0},{5,7},{6,2},{7,5},{8,12},{9,11},{10,... | collective-permute-start | bytes 2359304 | tf_op jit(solution)/shard_map/ppermute | solution.py:34
  13.3 4.7 %collective-permute-start.4 = (bf16[64,2048]{1,0:T(8,128)(2,1)S(1)}, bf16[64,2048]{1,0:T(8,128)(2,1)S(1)}, u32[]{:S(2)}, u32[]{:S(2)}) collective-permute-start(bf16[64,2048]{1,0:T(8,128)(2,1)S(1)} %pad_maximum_fusion.2.refs_0_), channel_id=1, source_target_pairs={{0,1},{1,0},{2,3},{3,2},{4,5},{5,4},{6,7},{7,6},{8,9},{9,8},{10,11... | collective-permute-start | bytes 786440 | tf_op jit(solution)/shard_map/ppermute | solution.py:34
  17.6 1.5 %collective-permute-start.5 = (bf16[64,2048]{1,0:T(8,128)(2,1)S(1)}, bf16[64,2048]{1,0:T(8,128)(2,1)S(1)}, u32[]{:S(2)}, u32[]{:S(2)}) collective-permute-start(bf16[64,2048]{1,0:T(8,128)(2,1)S(1)} %collective-permute-done.3.refs_1_), channel_id=1, source_target_pairs={{0,1},{1,0},{2,3},{3,2},{4,5},{5,4},{6,7},{7,6},{8,9},{9,8},{10,11... | collective-permute-start | bytes 786440 | tf_op jit(solution)/shard_map/ppermute | solution.py:34
  17.6 8.4 %collective-permute-start.2 = (bf16[64,6144]{1,0:T(8,128)(2,1)S(1)}, bf16[64,6144]{1,0:T(8,128)(2,1)S(1)}, u32[]{:S(2)}, u32[]{:S(2)}) collective-permute-start(bf16[64,6144]{1,0:T(8,128)(2,1)S(1)} %pad_maximum_fusion.refs_0_), channel_id=1, source_target_pairs={{0,1},{1,0},{2,3},{3,2},{4,5},{5,4},{6,7},{7,6},{8,9},{9,8},{10,11... | collective-permute-start | bytes 2359304 | tf_op jit(solution)/shard_map/ppermute | solution.py:34
  26.0 2.3 %collective-permute-start.6 = (bf16[64,6144]{1,0:T(8,128)(2,1)S(1)}, bf16[64,6144]{1,0:T(8,128)(2,1)S(1)}, u32[]{:S(2)}, u32[]{:S(2)}) collective-permute-start(bf16[64,6144]{1,0:T(8,128)(2,1)S(1)} %collective-permute-done.1.refs_1_), channel_id=1, source_target_pairs={{0,1},{1,0},{2,3},{3,2},{4,5},{5,4},{6,7},{7,6},{8,9},{9,8},{10,11... | collective-permute-start | bytes 2359304 | tf_op jit(solution)/shard_map/ppermute | solution.py:34
  28.3 15.6 %copy-start.1 = (bf16[1152,128]{1,0:T(8,128)(2,1)S(1)}, bf16[1152,128]{1,0:T(8,128)(2,1)}, u32[]{:S(2)}) copy-start(bf16[1152,128]{1,0:T(8,128)(2,1)} %constant.6.clone.high_ref.refs_8_.there.refs_0_) | copy-start | bytes 884740
  28.3 15.6 %copy-start.2 = (bf16[1920,128]{1,0:T(8,128)(2,1)S(1)}, bf16[1920,128]{1,0:T(8,128)(2,1)}, u32[]{:S(2)}) copy-start(bf16[1920,128]{1,0:T(8,128)(2,1)} %constant.8.clone.refs_9_.back.refs_1_) | copy-start | bytes 1474564
  28.3 15.6 %copy-start.3 = (bf16[256,1024]{1,0:T(8,128)(2,1)S(1)}, bf16[256,1024]{1,0:T(8,128)(2,1)}, u32[]{:S(2)}) copy-start(bf16[256,1024]{1,0:T(8,128)(2,1)} %grad_ref.1) | copy-start | bytes 1572868
  39.8 11.9 %collective-permute-start.7 = (bf16[128,1024]{1,0:T(8,128)(2,1)S(1)}, bf16[128,1024]{1,0:T(8,128)(2,1)S(1)}, u32[]{:S(2)}, u32[]{:S(2)}) collective-permute-start(bf16[128,1024]{1,0:T(8,128)(2,1)S(1)} %get-tuple-element.38), channel_id=1, source_target_pairs={{0,8},{8,16},{16,24},{1,9},{9,17},{17,25},{2,10},{10,18},{18,26},{... | collective-permute-start | bytes 786440 | tf_op jit(solution)/shard_map/ppermute | solution.py:29
  50.4 10.0 %collective-permute-start.8 = (bf16[128,1024]{1,0:T(8,128)(2,1)S(1)}, bf16[128,1024]{1,0:T(8,128)(2,1)S(1)}, u32[]{:S(2)}, u32[]{:S(2)}) collective-permute-start(bf16[128,1024]{1,0:T(8,128)(2,1)S(1)} %get-tuple-element.43), channel_id=1, source_target_pairs={{8,0},{16,8},{24,16},{9,1},{17,9},{25,17},{10,2},{18,10},{26,18},{... | collective-permute-start | bytes 786440 | tf_op jit(solution)/shard_map/ppermute | solution.py:29
  69.9 3.1 %collective-permute-start.9 = (bf16[128,5120]{1,0:T(8,128)(2,1)S(1)}, bf16[128,5120]{1,0:T(8,128)(2,1)S(1)}, u32[]{:S(2)}, u32[]{:S(2)}) collective-permute-start(bf16[128,5120]{1,0:T(8,128)(2,1)S(1)} %get-tuple-element.48), channel_id=1, source_target_pairs={{0,1},{1,0},{2,3},{3,2},{4,5},{5,4},{6,7},{7,6},{8,9},{9,8},{10,11... | collective-permute-start | bytes 3932168 | tf_op jit(solution)/shard_map/ppermute | solution.py:34
  73.4 11.6 %collective-permute-start.10 = (bf16[64,5120]{1,0:T(8,128)(2,1)S(1)}, bf16[64,5120]{1,0:T(8,128)(2,1)S(1)}, u32[]{:S(2)}, u32[]{:S(2)}) collective-permute-start(bf16[64,5120]{1,0:T(8,128)(2,1)S(1)} %get-tuple-element.58.refs_5_), channel_id=1, source_target_pairs={{0,4},{1,3},{2,6},{3,1},{4,0},{5,7},{6,2},{7,5},{8,12},{9,11},{10,... | collective-permute-start | bytes 1966088 | tf_op jit(solution)/shard_map/ppermute | solution.py:34
  74.9 15.6 %collective-permute-start.15 = (bf16[128,1024]{1,0:T(8,128)(2,1)S(1)}, bf16[128,1024]{1,0:T(8,128)(2,1)S(1)}, u32[]{:S(2)}, u32[]{:S(2)}) collective-permute-start(bf16[128,1024]{1,0:T(8,128)(2,1)S(1)} %get-tuple-element.54), channel_id=1, source_target_pairs={{0,16},{8,24},{16,0},{24,8},{1,17},{9,25},{17,1},{25,9},{2,18},{10... | collective-permute-start | bytes 786440 | tf_op jit(solution)/shard_map/ppermute | solution.py:64
  84.9 2.4 %collective-permute-start.12 = (bf16[128,3072]{1,0:T(8,128)(2,1)S(1)}, bf16[128,3072]{1,0:T(8,128)(2,1)S(1)}, u32[]{:S(2)}, u32[]{:S(2)}) collective-permute-start(bf16[128,3072]{1,0:T(8,128)(2,1)S(1)} %get-tuple-element.52), channel_id=1, source_target_pairs={{0,1},{1,0},{2,3},{3,2},{4,5},{5,4},{6,7},{7,6},{8,9},{9,8},{10,11... | collective-permute-start | bytes 2359304 | tf_op jit(solution)/shard_map/ppermute | solution.py:34
  85.1 9.0 %collective-permute-start.11 = (bf16[32,5120]{1,0:T(8,128)(2,1)S(1)}, bf16[32,5120]{1,0:T(8,128)(2,1)S(1)}, u32[]{:S(2)}, u32[]{:S(2)}) collective-permute-start(bf16[32,5120]{1,0:T(8,128)(2,1)S(1)} %add_convert_fusion.5), channel_id=1, source_target_pairs={{0,2},{1,5},{2,0},{3,7},{4,6},{5,1},{6,4},{7,3},{8,10},{9,13},{10,... | collective-permute-start | bytes 983048 | tf_op jit(solution)/shard_map/ppermute | solution.py:34
  87.5 8.5 %collective-permute-start.13 = (bf16[64,3072]{1,0:T(8,128)(2,1)S(1)}, bf16[64,3072]{1,0:T(8,128)(2,1)S(1)}, u32[]{:S(2)}, u32[]{:S(2)}) collective-permute-start(bf16[64,3072]{1,0:T(8,128)(2,1)S(1)} %get-tuple-element.60), channel_id=1, source_target_pairs={{0,4},{1,3},{2,6},{3,1},{4,0},{5,7},{6,2},{7,5},{8,12},{9,11},{10,... | collective-permute-start | bytes 1179656 | tf_op jit(solution)/shard_map/ppermute | solution.py:34
  90.6 7.5 %collective-permute-start.16 = (bf16[128,1024]{1,0:T(8,128)(2,1)S(1)}, bf16[128,1024]{1,0:T(8,128)(2,1)S(1)}, u32[]{:S(2)}, u32[]{:S(2)}) collective-permute-start(bf16[128,1024]{1,0:T(8,128)(2,1)S(1)} %add_convert_fusion.6), channel_id=1, source_target_pairs={{0,8},{8,0},{16,24},{24,16},{1,9},{9,1},{17,25},{25,17},{2,10},{10... | collective-permute-start | bytes 786440 | tf_op jit(solution)/shard_map/ppermute | solution.py:64
  96.0 5.7 %collective-permute-start.14 = (bf16[32,3072]{1,0:T(8,128)(2,1)S(1)}, bf16[32,3072]{1,0:T(8,128)(2,1)S(1)}, u32[]{:S(2)}, u32[]{:S(2)}) collective-permute-start(bf16[32,3072]{1,0:T(8,128)(2,1)S(1)} %add_convert_fusion.8), channel_id=1, source_target_pairs={{0,2},{1,5},{2,0},{3,7},{4,6},{5,1},{6,4},{7,3},{8,10},{9,13},{10,... | collective-permute-start | bytes 589832 | tf_op jit(solution)/shard_map/ppermute | solution.py:34

commit v7 on v6

--- a/solution.py
+++ b/solution.py
@@ -77,11 +77,12 @@
 
 def scatter_rows(pieces, totals, own):
     far, first = [swap(t[1], 2) for t in totals], []
-    first.append(add_up(totals[0][0][own:], far[0][own:]))
-    for piece in pieces[1:]:
-        totals.append(chip_sums(piece, own, first[-1:]))
+    for piece in pieces[len(totals) :]:
+        totals.append(chip_sums(piece, own))
         far.append(swap(totals[-1][1], 2))
-        first.append(add_up(totals[-1][0][own:], far[-1][own:]))
+    for i, (total, there) in enumerate(zip(totals, far)):
+        there = once(there, totals[-1][1]) if i + 1 < len(totals) else there
+        first.append(add_up(total[0][own:], there[own:]))
     near = [swap(f, 1) for f in first]
     return [add_up(t[:own], f[:own], n) for (t, _), f, n in zip(totals, far, near)], first
 

time: 103 us -> 112 us (1.087)
  waiting for transfers between devices: 24.8 us -> 32.1 us
  starting transfers between devices: 21.1 us -> 22.8 us
    ppermute x13, waiting for transfers between devices: 22 us -> 32 us  [swap(): lax.ppermute(block, 'tp', [(i, i ^ offsets[i % 2]) for i in range(8)])]
    ppermute x2, waiting for transfers between devices: 2.82 us -> 0.01 us  [add_pair(): theirs = lax.ppermute(mine, axis, route)]
  transfers between devices with their start and end apart: 17 -> 17, of which waited for: 12 -> 9; matrix products, arithmetic and copies ran while one was open for 3% -> 3% of each run, Pallas kernels for 27% -> 20%
where the time goes in v7:
time: 112 us
  Pallas kernels  49.3 us (44%)
  waiting for transfers between devices  32.1 us (29%)
  starting transfers between devices  22.8 us (20%)
  local copies, waits for them, and re-layouts  3.94 us (4%)
  other arithmetic  2.63 us (2%)
    ppermute x13, waiting for transfers between devices, swap(): lax.ppermute(block, 'tp', [(i, i ^ offsets[i % 2]) for i in range(8)])  32 us
    pallas_call x3, Pallas kernels, project(): pl.pallas_call(kernel, in_specs=in_specs, out_specs=[VMEM] * len(out_shap...  24 us
    ppermute x13, starting transfers between devices, swap(): lax.ppermute(block, 'tp', [(i, i ^ offsets[i % 2]) for i in range(8)])  12.2 us
    pallas_call x1, Pallas kernels, filter_backward(): pl.pallas_call(kernel, in_specs=[VMEM] * 8 + [ANYWHERE] * 2, out_specs=[V...  9.59 us
    pallas_call x1, Pallas kernels, filter_forward(): pl.pallas_call(kernel, in_specs=[VMEM] * 8 + [ANYWHERE], out_specs=[VMEM]...  8.66 us
    pallas_call x1, Pallas kernels, project_back(): pl.pallas_call(kernel, in_specs=[VMEM] * count + [ANYWHERE] * count + [VM...  6.32 us
    ppermute x2, starting transfers between devices, add_pair(): theirs = lax.ppermute(mine, axis, route)  5.32 us
    ppermute x2, starting transfers between devices, from_behind(): return lax.ppermute(block, axis, route)  5.3 us
  transfers between devices with their start and end apart: 17, of which 9 were waited for; matrix products, arithmetic and copies ran while one was open for 3% of the time, Pallas kernels for 20%

profile of v7, /device:TPU:0, one launch (start us, length us, event | category | flops | bytes accessed | tf_op | source)
XLA Modules:
  0.0 111.6 jit_solution(11024267627606650006)
XLA Ops:
  0.6 3.0 %collective-permute-start = (bf16[32,8192]{1,0:T(8,128)(2,1)}, bf16[32,8192]{1,0:T(8,128)(2,1)S(1)}, u32[]{:S(2)}, u32[]{:S(2)}) collective-permute-start(bf16[32,8192]{1,0:T(8,128)(2,1)} %param.9), channel_id=1, source_target_pairs={{0,2},{1,5},{2,0},{3,7},{4,6},{5,1},{6,4},{7,3},{8,10},{9,13},{10,... | collective-permute-start | bytes 1572872 | tf_op jit(solution)/shard_map/ppermute | solution.py:34
  3.6 1.1 slice.60
  8.3 2.7 %collective-permute-done = bf16[32,8192]{1,0:T(8,128)(2,1)S(1)} collective-permute-done((bf16[32,8192]{1,0:T(8,128)(2,1)}, bf16[32,8192]{1,0:T(8,128)(2,1)S(1)}, u32[]{:S(2)}, u32[]{:S(2)}) %collective-permute-start) | collective-permute-done | bytes 524320 | tf_op jit(solution)/shard_map/ppermute | solution.py:34
  11.1 2.1 %collective-permute-start.3 = (bf16[64,2048]{1,0:T(8,128)(2,1)S(1)}, bf16[64,2048]{1,0:T(8,128)(2,1)S(1)}, u32[]{:S(2)}, u32[]{:S(2)}) collective-permute-start(bf16[64,2048]{1,0:T(8,128)(2,1)S(1)} %pad_maximum_fusion.2.refs_0_), channel_id=1, source_target_pairs={{0,4},{1,3},{2,6},{3,1},{4,0},{5,7},{6,2},{7,5},{8,12},{9,11},{10,... | collective-permute-start | bytes 786440 | tf_op jit(solution)/shard_map/ppermute | solution.py:34
  13.4 4.1 %collective-permute-done.3.refs_1_ = bf16[64,2048]{1,0:T(8,128)(2,1)S(1)} collective-permute-done((bf16[64,2048]{1,0:T(8,128)(2,1)S(1)}, bf16[64,2048]{1,0:T(8,128)(2,1)S(1)}, u32[]{:S(2)}, u32[]{:S(2)}) %collective-permute-start.3) | collective-permute-done | bytes 262176 | tf_op jit(solution)/shard_map/ppermute | solution.py:34
  19.1 6.0 %project.3 = (f32[256,1024]{1,0:T(8,128)S(1)}, f32[256,1024]{1,0:T(8,128)S(1)}, f32[256,1024]{1,0:T(8,128)S(1)}) custom-call(bf16[64,2048]{1,0:T(8,128)(2,1)S(1)} %pad_maximum_fusion.2.refs_0_, bf16[64,2048]{1,0:T(8,128)(2,1)S(1)} %collective-permute-done.3.refs_1_, bf16[64,2048]{1,0:T(8,128)(2,1)S(1)} %collective-permute-done.4.refs_2_, ...), custom_call_target="tpu_custom_call" | custom-call | flops 3221225472 | bytes 12582912 | tf_op jit(solution)/shard_map/project/pallas_call | solution.py:222
  26.0 2.3 %collective-permute-done.6.refs_3_ = bf16[64,6144]{1,0:T(8,128)(2,1)S(1)} collective-permute-done((bf16[64,6144]{1,0:T(8,128)(2,1)S(1)}, bf16[64,6144]{1,0:T(8,128)(2,1)S(1)}, u32[]{:S(2)}, u32[]{:S(2)}) %collective-permute-start.6) | collective-permute-done | bytes 786464 | tf_op jit(solution)/shard_map/ppermute | solution.py:34
  28.3 11.5 %project.4 = (bf16[256,1024]{1,0:T(8,128)(2,1)S(1)}, bf16[256,1024]{1,0:T(8,128)(2,1)S(1)}, bf16[256,1024]{1,0:T(8,128)(2,1)S(1)}, bf16[128,1024]{1,0:T(8,128)(2,1)S(1)}) custom-call(bf16[64,6144]{1,0:T(8,128)(2,1)S(1)} %pad_maximum_fusion.refs_0_, bf16[64,6144]{1,0:T(8,128)(2,1)S(1)} %collective-permute-done.1.refs_1_, ...), custom_call_target="tpu_custom_call" | custom-call | flops 6442450944 | bytes 25165824 | tf_op jit(solution)/shard_map/project/pallas_call | solution.py:222
  39.8 4.0 %collective-permute-start.7 = (bf16[128,1024]{1,0:T(8,128)(2,1)S(1)}, bf16[128,1024]{1,0:T(8,128)(2,1)S(1)}, u32[]{:S(2)}, u32[]{:S(2)}) collective-permute-start(bf16[128,1024]{1,0:T(8,128)(2,1)S(1)} %get-tuple-element.38), channel_id=1, source_target_pairs={{0,8},{8,16},{16,24},{1,9},{9,17},{17,25},{2,10},{10,18},{18,26},{... | collective-permute-start | bytes 786440 | tf_op jit(solution)/shard_map/ppermute | solution.py:29
  43.9 6.5 %project.5 = (bf16[256,1024]{1,0:T(8,128)(2,1)S(1)}, bf16[256,1024]{1,0:T(8,128)(2,1)S(1)}, bf16[128,1024]{1,0:T(8,128)(2,1)S(1)}, f32[384,1024]{1,0:T(8,128)S(1)}) custom-call(bf16[64,6144]{1,0:T(8,128)(2,1)S(1)} %pad_maximum_fusion.refs_0_, bf16[64,6144]{1,0:T(8,128)(2,1)S(1)} %collective-permute-done.1.refs_1_, ...), custom_call_target="tpu_custom_call" | custom-call | flops 3221225472 | bytes 12582912 | tf_op jit(solution)/shard_map/project/pallas_call | solution.py:222
  50.4 1.3 %collective-permute-start.8 = (bf16[128,1024]{1,0:T(8,128)(2,1)S(1)}, bf16[128,1024]{1,0:T(8,128)(2,1)S(1)}, u32[]{:S(2)}, u32[]{:S(2)}) collective-permute-start(bf16[128,1024]{1,0:T(8,128)(2,1)S(1)} %get-tuple-element.43), channel_id=1, source_target_pairs={{8,0},{16,8},{24,16},{9,1},{17,9},{25,17},{10,2},{18,10},{26,18},{... | collective-permute-start | bytes 786440 | tf_op jit(solution)/shard_map/ppermute | solution.py:29
  51.7 8.7 %conv.1 = (bf16[256,1024]{1,0:T(8,128)(2,1)}, bf16[256,1024]{1,0:T(8,128)(2,1)}, bf16[128,1024]{1,0:T(8,128)(2,1)S(1)}, f32[384,1024]{1,0:T(8,128)S(1)}, f32[256,8192]{1,0:T(8,128)S(1)}) custom-call(bf16[1152,128]{1,0:T(8,128)(2,1)S(1)} %copy-done.1, bf16[1920,128]{1,0:T(8,128)(2,1)S(1)} %copy-done.2, f32[384,1024]{1,0:T(8,128)S(1)} %get-tuple-element.37.p_ref, ...), custom_call_target="tpu_custom_call" | custom-call | flops 5368709120 | bytes 20971520 | tf_op jit(solution)/shard_map/conv/pallas_call | solution.py:346
  60.3 9.6 %conv_back.1 = (bf16[128,5120]{1,0:T(8,128)(2,1)S(1)}, bf16[128,5120]{1,0:T(8,128)(2,1)S(1)}, bf16[256,1024]{1,0:T(8,128)(2,1)S(1)}, bf16[256,1024]{1,0:T(8,128)(2,1)S(1)}) custom-call(bf16[1152,128]{1,0:T(8,128)(2,1)S(1)} %copy-done.1, bf16[1920,128]{1,0:T(8,128)(2,1)S(1)} %copy-done.2, f32[384,1024]{1,0:T(8,128)S(1)} %get-tuple-element.42.refs_2_, ...), custom_call_target="tpu_custom_call" | custom-call | flops 6442450944 | bytes 25165824 | tf_op jit(solution)/shard_map/conv_back/pallas_call | solution.py:392
  70.0 3.0 %collective-permute-done.9 = bf16[128,5120]{1,0:T(8,128)(2,1)S(1)} collective-permute-done((bf16[128,5120]{1,0:T(8,128)(2,1)S(1)}, bf16[128,5120]{1,0:T(8,128)(2,1)S(1)}, u32[]{:S(2)}, u32[]{:S(2)}) %collective-permute-start.9) | collective-permute-done | bytes 1310752 | tf_op jit(solution)/shard_map/ppermute | solution.py:34
  73.4 6.3 %project_back.1 = (bf16[128,3072]{1,0:T(8,128)(2,1)S(1)}, bf16[128,3072]{1,0:T(8,128)(2,1)S(1)}) custom-call(bf16[256,1024]{1,0:T(8,128)(2,1)S(1)} %get-tuple-element.49.refs_0_, bf16[256,1024]{1,0:T(8,128)(2,1)S(1)} %get-tuple-element.50.refs_1_, bf16[8192,1024]{1,0:T(8,128)(2,1)} %refs_2_.1, bf16[8192,1024]{1,0:T(8,128)(2,1)} %refs_3_.1, ...), custom_call_target="tpu_custom_call" | custom-call | flops 3221225472 | bytes 12582912 | tf_op jit(solution)/shard_map/project_back/pallas_call | solution.py:426
  79.9 3.7 %collective-permute-start.15 = (bf16[128,1024]{1,0:T(8,128)(2,1)S(1)}, bf16[128,1024]{1,0:T(8,128)(2,1)S(1)}, u32[]{:S(2)}, u32[]{:S(2)}) collective-permute-start(bf16[128,1024]{1,0:T(8,128)(2,1)S(1)} %get-tuple-element.54), channel_id=1, source_target_pairs={{0,16},{8,24},{16,0},{24,8},{1,17},{9,25},{17,1},{25,9},{2,18},{10... | collective-permute-start | bytes 786440 | tf_op jit(solution)/shard_map/ppermute | solution.py:64
  83.5 1.5 %collective-permute-start.10 = (bf16[64,5120]{1,0:T(8,128)(2,1)S(1)}, bf16[64,5120]{1,0:T(8,128)(2,1)S(1)}, u32[]{:S(2)}, u32[]{:S(2)}) collective-permute-start(bf16[64,5120]{1,0:T(8,128)(2,1)S(1)} %get-tuple-element.58.refs_5_), channel_id=1, source_target_pairs={{0,4},{1,3},{2,6},{3,1},{4,0},{5,7},{6,2},{7,5},{8,12},{9,11},{10,... | collective-permute-start | bytes 1966088 | tf_op jit(solution)/shard_map/ppermute | solution.py:34
  85.3 8.9 %collective-permute-done.10 = bf16[64,5120]{1,0:T(8,128)(2,1)S(1)} collective-permute-done((bf16[64,5120]{1,0:T(8,128)(2,1)S(1)}, bf16[64,5120]{1,0:T(8,128)(2,1)S(1)}, u32[]{:S(2)}, u32[]{:S(2)}) %collective-permute-start.10) | collective-permute-done | bytes 655392 | tf_op jit(solution)/shard_map/ppermute | solution.py:34
  94.2 1.5 %collective-permute-start.12 = (bf16[32,5120]{1,0:T(8,128)(2,1)S(1)}, bf16[32,5120]{1,0:T(8,128)(2,1)S(1)}, u32[]{:S(2)}, u32[]{:S(2)}) collective-permute-start(bf16[32,5120]{1,0:T(8,128)(2,1)S(1)} %add_convert_fusion.5), channel_id=1, source_target_pairs={{0,2},{1,5},{2,0},{3,7},{4,6},{5,1},{6,4},{7,3},{8,10},{9,13},{10,... | collective-permute-start | bytes 983048 | tf_op jit(solution)/shard_map/ppermute | solution.py:34
  95.8 1.5 %collective-permute-start.13 = (bf16[64,3072]{1,0:T(8,128)(2,1)S(1)}, bf16[64,3072]{1,0:T(8,128)(2,1)S(1)}, u32[]{:S(2)}, u32[]{:S(2)}) collective-permute-start(bf16[64,3072]{1,0:T(8,128)(2,1)S(1)} %get-tuple-element.60), channel_id=1, source_target_pairs={{0,4},{1,3},{2,6},{3,1},{4,0},{5,7},{6,2},{7,5},{8,12},{9,11},{10,... | collective-permute-start | bytes 1179656 | tf_op jit(solution)/shard_map/ppermute | solution.py:34
  97.4 1.7 %collective-permute-start.16 = (bf16[128,1024]{1,0:T(8,128)(2,1)S(1)}, bf16[128,1024]{1,0:T(8,128)(2,1)S(1)}, u32[]{:S(2)}, u32[]{:S(2)}) collective-permute-start(bf16[128,1024]{1,0:T(8,128)(2,1)S(1)} %add_convert_fusion.6), channel_id=1, source_target_pairs={{0,8},{8,0},{16,24},{24,16},{1,9},{9,1},{17,25},{25,17},{2,10},{10... | collective-permute-start | bytes 786440 | tf_op jit(solution)/shard_map/ppermute | solution.py:64
  99.0 5.8 %collective-permute-done.12 = bf16[32,5120]{1,0:T(8,128)(2,1)S(1)} collective-permute-done((bf16[32,5120]{1,0:T(8,128)(2,1)S(1)}, bf16[32,5120]{1,0:T(8,128)(2,1)S(1)}, u32[]{:S(2)}, u32[]{:S(2)}) %collective-permute-start.12) | collective-permute-done | bytes 327712 | tf_op jit(solution)/shard_map/ppermute | solution.py:34
  105.0 1.5 %collective-permute-start.14 = (bf16[32,3072]{1,0:T(8,128)(2,1)S(1)}, bf16[32,3072]{1,0:T(8,128)(2,1)S(1)}, u32[]{:S(2)}, u32[]{:S(2)}) collective-permute-start(bf16[32,3072]{1,0:T(8,128)(2,1)S(1)} %add_convert_fusion.8), channel_id=1, source_target_pairs={{0,2},{1,5},{2,0},{3,7},{4,6},{5,1},{6,4},{7,3},{8,10},{9,13},{10,... | collective-permute-start | bytes 589832 | tf_op jit(solution)/shard_map/ppermute | solution.py:34
  107.4 3.3 %collective-permute-done.14 = bf16[32,3072]{1,0:T(8,128)(2,1)S(1)} collective-permute-done((bf16[32,3072]{1,0:T(8,128)(2,1)S(1)}, bf16[32,3072]{1,0:T(8,128)(2,1)S(1)}, u32[]{:S(2)}, u32[]{:S(2)}) %collective-permute-start.14) | collective-permute-done | bytes 196640 | tf_op jit(solution)/shard_map/ppermute | solution.py:34
  (44 shorter events, 9.1 us)
Async XLA Ops:
  0.6 5.0 %copy-start.4 = (f32[128,1024]{1,0:T(8,128)S(1)}, f32[128,1024]{1,0:T(8,128)}, u32[]{:S(2)}) copy-start(f32[128,1024]{1,0:T(8,128)} %taps_ref.1) | copy-start | bytes 1572868
  0.6 10.4 %collective-permute-start = (bf16[32,8192]{1,0:T(8,128)(2,1)}, bf16[32,8192]{1,0:T(8,128)(2,1)S(1)}, u32[]{:S(2)}, u32[]{:S(2)}) collective-permute-start(bf16[32,8192]{1,0:T(8,128)(2,1)} %param.9), channel_id=1, source_target_pairs={{0,2},{1,5},{2,0},{3,7},{4,6},{5,1},{6,4},{7,3},{8,10},{9,13},{10,... | collective-permute-start | bytes 1572872 | tf_op jit(solution)/shard_map/ppermute | solution.py:34
  5.6 1.0 copy-start
  6.6 1.0 copy-start.5
  11.1 6.5 %collective-permute-start.3 = (bf16[64,2048]{1,0:T(8,128)(2,1)S(1)}, bf16[64,2048]{1,0:T(8,128)(2,1)S(1)}, u32[]{:S(2)}, u32[]{:S(2)}) collective-permute-start(bf16[64,2048]{1,0:T(8,128)(2,1)S(1)} %pad_maximum_fusion.2.refs_0_), channel_id=1, source_target_pairs={{0,4},{1,3},{2,6},{3,1},{4,0},{5,7},{6,2},{7,5},{8,12},{9,11},{10,... | collective-permute-start | bytes 786440 | tf_op jit(solution)/shard_map/ppermute | solution.py:34
  13.3 12.7 %collective-permute-start.1 = (bf16[64,6144]{1,0:T(8,128)(2,1)S(1)}, bf16[64,6144]{1,0:T(8,128)(2,1)S(1)}, u32[]{:S(2)}, u32[]{:S(2)}) collective-permute-start(bf16[64,6144]{1,0:T(8,128)(2,1)S(1)} %pad_maximum_fusion.refs_0_), channel_id=1, source_target_pairs={{0,4},{1,3},{2,6},{3,1},{4,0},{5,7},{6,2},{7,5},{8,12},{9,11},{10,... | collective-permute-start | bytes 2359304 | tf_op jit(solution)/shard_map/ppermute | solution.py:34
  13.3 4.7 %collective-permute-start.4 = (bf16[64,2048]{1,0:T(8,128)(2,1)S(1)}, bf16[64,2048]{1,0:T(8,128)(2,1)S(1)}, u32[]{:S(2)}, u32[]{:S(2)}) collective-permute-start(bf16[64,2048]{1,0:T(8,128)(2,1)S(1)} %pad_maximum_fusion.2.refs_0_), channel_id=1, source_target_pairs={{0,1},{1,0},{2,3},{3,2},{4,5},{5,4},{6,7},{7,6},{8,9},{9,8},{10,11... | collective-permute-start | bytes 786440 | tf_op jit(solution)/shard_map/ppermute | solution.py:34
  17.6 1.5 %collective-permute-start.5 = (bf16[64,2048]{1,0:T(8,128)(2,1)S(1)}, bf16[64,2048]{1,0:T(8,128)(2,1)S(1)}, u32[]{:S(2)}, u32[]{:S(2)}) collective-permute-start(bf16[64,2048]{1,0:T(8,128)(2,1)S(1)} %collective-permute-done.3.refs_1_), channel_id=1, source_target_pairs={{0,1},{1,0},{2,3},{3,2},{4,5},{5,4},{6,7},{7,6},{8,9},{9,8},{10,11... | collective-permute-start | bytes 786440 | tf_op jit(solution)/shard_map/ppermute | solution.py:34
  17.6 8.4 %collective-permute-start.2 = (bf16[64,6144]{1,0:T(8,128)(2,1)S(1)}, bf16[64,6144]{1,0:T(8,128)(2,1)S(1)}, u32[]{:S(2)}, u32[]{:S(2)}) collective-permute-start(bf16[64,6144]{1,0:T(8,128)(2,1)S(1)} %pad_maximum_fusion.refs_0_), channel_id=1, source_target_pairs={{0,1},{1,0},{2,3},{3,2},{4,5},{5,4},{6,7},{7,6},{8,9},{9,8},{10,11... | collective-permute-start | bytes 2359304 | tf_op jit(solution)/shard_map/ppermute | solution.py:34
  26.0 2.3 %collective-permute-start.6 = (bf16[64,6144]{1,0:T(8,128)(2,1)S(1)}, bf16[64,6144]{1,0:T(8,128)(2,1)S(1)}, u32[]{:S(2)}, u32[]{:S(2)}) collective-permute-start(bf16[64,6144]{1,0:T(8,128)(2,1)S(1)} %collective-permute-done.1.refs_1_), channel_id=1, source_target_pairs={{0,1},{1,0},{2,3},{3,2},{4,5},{5,4},{6,7},{7,6},{8,9},{9,8},{10,11... | collective-permute-start | bytes 2359304 | tf_op jit(solution)/shard_map/ppermute | solution.py:34
  28.3 15.6 %copy-start.1 = (bf16[1152,128]{1,0:T(8,128)(2,1)S(1)}, bf16[1152,128]{1,0:T(8,128)(2,1)}, u32[]{:S(2)}) copy-start(bf16[1152,128]{1,0:T(8,128)(2,1)} %constant.6.clone.high_ref.refs_8_.there.refs_0_) | copy-start | bytes 884740
  28.3 15.6 %copy-start.2 = (bf16[1920,128]{1,0:T(8,128)(2,1)S(1)}, bf16[1920,128]{1,0:T(8,128)(2,1)}, u32[]{:S(2)}) copy-start(bf16[1920,128]{1,0:T(8,128)(2,1)} %constant.8.clone.refs_9_.back.refs_1_) | copy-start | bytes 1474564
  28.3 15.6 %copy-start.3 = (bf16[256,1024]{1,0:T(8,128)(2,1)S(1)}, bf16[256,1024]{1,0:T(8,128)(2,1)}, u32[]{:S(2)}) copy-start(bf16[256,1024]{1,0:T(8,128)(2,1)} %grad_ref.1) | copy-start | bytes 1572868
  39.8 11.9 %collective-permute-start.7 = (bf16[128,1024]{1,0:T(8,128)(2,1)S(1)}, bf16[128,1024]{1,0:T(8,128)(2,1)S(1)}, u32[]{:S(2)}, u32[]{:S(2)}) collective-permute-start(bf16[128,1024]{1,0:T(8,128)(2,1)S(1)} %get-tuple-element.38), channel_id=1, source_target_pairs={{0,8},{8,16},{16,24},{1,9},{9,17},{17,25},{2,10},{10,18},{18,26},{... | collective-permute-start | bytes 786440 | tf_op jit(solution)/shard_map/ppermute | solution.py:29
  50.4 10.0 %collective-permute-start.8 = (bf16[128,1024]{1,0:T(8,128)(2,1)S(1)}, bf16[128,1024]{1,0:T(8,128)(2,1)S(1)}, u32[]{:S(2)}, u32[]{:S(2)}) collective-permute-start(bf16[128,1024]{1,0:T(8,128)(2,1)S(1)} %get-tuple-element.43), channel_id=1, source_target_pairs={{8,0},{16,8},{24,16},{9,1},{17,9},{25,17},{10,2},{18,10},{26,18},{... | collective-permute-start | bytes 786440 | tf_op jit(solution)/shard_map/ppermute | solution.py:29
  69.9 3.1 %collective-permute-start.9 = (bf16[128,5120]{1,0:T(8,128)(2,1)S(1)}, bf16[128,5120]{1,0:T(8,128)(2,1)S(1)}, u32[]{:S(2)}, u32[]{:S(2)}) collective-permute-start(bf16[128,5120]{1,0:T(8,128)(2,1)S(1)} %get-tuple-element.48), channel_id=1, source_target_pairs={{0,1},{1,0},{2,3},{3,2},{4,5},{5,4},{6,7},{7,6},{8,9},{9,8},{10,11... | collective-permute-start | bytes 3932168 | tf_op jit(solution)/shard_map/ppermute | solution.py:34
  79.7 5.4 %collective-permute-start.11 = (bf16[128,3072]{1,0:T(8,128)(2,1)S(1)}, bf16[128,3072]{1,0:T(8,128)(2,1)S(1)}, u32[]{:S(2)}, u32[]{:S(2)}) collective-permute-start(bf16[128,3072]{1,0:T(8,128)(2,1)S(1)} %get-tuple-element.52), channel_id=1, source_target_pairs={{0,1},{1,0},{2,3},{3,2},{4,5},{5,4},{6,7},{7,6},{8,9},{9,8},{10,11... | collective-permute-start | bytes 2359304 | tf_op jit(solution)/shard_map/ppermute | solution.py:34
  79.9 17.4 %collective-permute-start.15 = (bf16[128,1024]{1,0:T(8,128)(2,1)S(1)}, bf16[128,1024]{1,0:T(8,128)(2,1)S(1)}, u32[]{:S(2)}, u32[]{:S(2)}) collective-permute-start(bf16[128,1024]{1,0:T(8,128)(2,1)S(1)} %get-tuple-element.54), channel_id=1, source_target_pairs={{0,16},{8,24},{16,0},{24,8},{1,17},{9,25},{17,1},{25,9},{2,18},{10... | collective-permute-start | bytes 786440 | tf_op jit(solution)/shard_map/ppermute | solution.py:64
  83.5 10.6 %collective-permute-start.10 = (bf16[64,5120]{1,0:T(8,128)(2,1)S(1)}, bf16[64,5120]{1,0:T(8,128)(2,1)S(1)}, u32[]{:S(2)}, u32[]{:S(2)}) collective-permute-start(bf16[64,5120]{1,0:T(8,128)(2,1)S(1)} %get-tuple-element.58.refs_5_), channel_id=1, source_target_pairs={{0,4},{1,3},{2,6},{3,1},{4,0},{5,7},{6,2},{7,5},{8,12},{9,11},{10,... | collective-permute-start | bytes 1966088 | tf_op jit(solution)/shard_map/ppermute | solution.py:34
  94.2 10.6 %collective-permute-start.12 = (bf16[32,5120]{1,0:T(8,128)(2,1)S(1)}, bf16[32,5120]{1,0:T(8,128)(2,1)S(1)}, u32[]{:S(2)}, u32[]{:S(2)}) collective-permute-start(bf16[32,5120]{1,0:T(8,128)(2,1)S(1)} %add_convert_fusion.5), channel_id=1, source_target_pairs={{0,2},{1,5},{2,0},{3,7},{4,6},{5,1},{6,4},{7,3},{8,10},{9,13},{10,... | collective-permute-start | bytes 983048 | tf_op jit(solution)/shard_map/ppermute | solution.py:34
  95.8 9.2 %collective-permute-start.13 = (bf16[64,3072]{1,0:T(8,128)(2,1)S(1)}, bf16[64,3072]{1,0:T(8,128)(2,1)S(1)}, u32[]{:S(2)}, u32[]{:S(2)}) collective-permute-start(bf16[64,3072]{1,0:T(8,128)(2,1)S(1)} %get-tuple-element.60), channel_id=1, source_target_pairs={{0,4},{1,3},{2,6},{3,1},{4,0},{5,7},{6,2},{7,5},{8,12},{9,11},{10,... | collective-permute-start | bytes 1179656 | tf_op jit(solution)/shard_map/ppermute | solution.py:34
  97.4 9.2 %collective-permute-start.16 = (bf16[128,1024]{1,0:T(8,128)(2,1)S(1)}, bf16[128,1024]{1,0:T(8,128)(2,1)S(1)}, u32[]{:S(2)}, u32[]{:S(2)}) collective-permute-start(bf16[128,1024]{1,0:T(8,128)(2,1)S(1)} %add_convert_fusion.6), channel_id=1, source_target_pairs={{0,8},{8,0},{16,24},{24,16},{1,9},{9,1},{17,25},{25,17},{2,10},{10... | collective-permute-start | bytes 786440 | tf_op jit(solution)/shard_map/ppermute | solution.py:64
  105.0 5.7 %collective-permute-start.14 = (bf16[32,3072]{1,0:T(8,128)(2,1)S(1)}, bf16[32,3072]{1,0:T(8,128)(2,1)S(1)}, u32[]{:S(2)}, u32[]{:S(2)}) collective-permute-start(bf16[32,3072]{1,0:T(8,128)(2,1)S(1)} %add_convert_fusion.8), channel_id=1, source_target_pairs={{0,2},{1,5},{2,0},{3,7},{4,6},{5,1},{6,4},{7,3},{8,10},{9,13},{10,... | collective-permute-start | bytes 589832 | tf_op jit(solution)/shard_map/ppermute | solution.py:34
